TPU v7x, 128 devices: a whole 4x4x4 slice. The times are simulated.
128 devices in a mesh: seq: 16 (over x, y), tp: 8 (over z, core).
Axes of the slice: x: 4, y: 4, z: 4, core: 2. Of those that a mesh axis runs over, the one named last changes fastest.
Arguments:
- x_in: bfloat16 [16, 4096, 8192], P('tp', 'seq'), may hold values from -6 to 6
- dt_raw: bfloat16 [16, 4096, 128], P('tp', 'seq'), may hold values from -4 to 4
- bc_in: bfloat16 [16, 4096, 32], P('tp', 'seq'), may hold values from -1.1953125 to 1.1953125
- decay_rate: float32 [128], replicated, may hold values from 2.4414063e-05 to 0.1
- skip_gain: float32 [128], replicated, may hold values from 0.5 to 1.5
- kv_pre: bfloat16 [16, 4096, 2048], P('tp', 'seq'), may hold values from -8 to 8
- lengths: int32 [16], replicated, may hold values from 256 to 4096, as said below
- group_of: int32 [16], replicated, may hold values from 0 to 15, each once
- slot_of: int32 [16, 16], replicated, may hold values from 0 to 15, each once within a row
- dec_x: bfloat16 [16, 4, 8192], P('seq', None, 'tp'), may hold values from -6 to 6
- dec_dt: bfloat16 [16, 4, 128], P('seq', None, 'tp'), may hold values from -4 to 4
- dec_bc: bfloat16 [16, 4, 32], P('seq'), may hold values from -1.1953125 to 1.1953125
- dec_z: bfloat16 [16, 4, 8192], P('seq', None, 'tp'), may hold values from -6 to 6
- norm_gain: bfloat16 [8192], P('tp'), may hold values from 0.5 to 1.5
- dec_q: bfloat16 [16, 4, 8192], P('seq', None, 'tp'), may hold values from -8 to 8
- dec_kv: bfloat16 [16, 4, 2048], P('seq', None, 'tp'), may hold values from -6 to 6
Outputs:
- y_pre: bfloat16 [16, 4096, 8192], P('tp', 'seq')
- kv_pool: bfloat16 [16, 4096, 2048], P('seq', None, 'tp')
- dec_mamba: bfloat16 [16, 4, 8192], P('seq', None, 'tp')
- dec_state: float32 [16, 16, 8192], P('seq', None, 'tp')
- dec_attn: bfloat16 [16, 4, 8192], P('seq', None, 'tp')
Inputs may be any that keep to these rules, and one draw needn't show every extreme that they name: `lengths`: every length is a multiple of 256; some prompt has length 4096. `group_of`: every decode group serves exactly one prompt. `slot_of`: each row is a permutation of the 16 slots.
All inputs are finite; a program needn't handle non-finite values.
Results may differ from a plain program's by a relative error of at most 0.005.
Values may be sent and summed in bfloat16 or wider, within the bound.
No kernel may reach another device: no remote copies, remote signals or barrier semaphores. Data moves between devices by JAX's collectives and lax.ppermute only.
A program may use at most 128 MiB of HBM per device.

v0:
```python
import jax
import jax.numpy as jnp
from jax import lax
from jax.sharding import PartitionSpec as P

HD = 128
BLK = 256
PAGE = 256


highest = lax.Precision.HIGHEST


def prefix(value, axis, join, neutral):
    count, mine = (lax.axis_size(axis), lax.axis_index(axis))
    pieces = jax.tree.map(lambda part: lax.all_gather(part, axis), value)
    total = jax.tree.map(
        lambda part, zero: jnp.full_like(part, 0) + jnp.asarray(zero, part.dtype), value, neutral
    )

    def step(position, total):
        longer = join(total, jax.tree.map(lambda part: part[position], pieces))
        return jax.tree.map(lambda new, old: jnp.where(position < mine, new, old), longer, total)

    return lax.fori_loop(0, count - 1, step, total)


def broadcast(value, axis, root):
    mine = lax.axis_index(axis) == root
    return lax.psum(jnp.where(mine, value, jnp.zeros_like(value)), axis)


def block_terms(x_block, step_block, log_block, bc_block):
    states = bc_block.shape[1] // 2
    heads = log_block.shape[1]
    cumulative = jnp.cumsum(log_block, axis=0)
    x_heads = x_block.reshape(BLK, heads, -1)
    to_end = jnp.exp(cumulative[-1][None, :] - cumulative) * step_block
    scaled = (to_end[:, :, None] * x_heads.astype(jnp.float32)).astype(jnp.bfloat16)
    local_state = jnp.einsum(
        "sn,shp->nhp", bc_block[:, :states], scaled, preferred_element_type=jnp.float32
    )
    return (local_state, cumulative[-1])


def block_output(x_block, step_block, log_block, bc_block, live_block, carry_state, skip_gain):
    states = bc_block.shape[1] // 2
    heads = log_block.shape[1]
    cumulative = jnp.cumsum(log_block, axis=0)
    b_rows = bc_block[:, :states]
    c_rows = bc_block[:, states:]
    scores = jnp.dot(c_rows, b_rows.T, preferred_element_type=jnp.float32)
    order = jnp.arange(BLK)
    causal = (order[:, None] >= order[None, :])[None]
    by_head = cumulative.T
    spread = jnp.where(causal, by_head[:, :, None] - by_head[:, None, :], 0.0)
    weights = jnp.where(
        causal, scores[None] * jnp.exp(spread) * step_block.T[:, None, :], 0.0
    ).astype(jnp.bfloat16)
    x_heads = x_block.reshape(BLK, heads, -1)
    within = jnp.einsum("hts,shp->thp", weights, x_heads, preferred_element_type=jnp.float32)
    carried = jnp.exp(cumulative)[:, :, None] * jnp.einsum(
        "tn,nhp->thp", c_rows.astype(jnp.float32), carry_state, precision=highest
    )
    output = (
        within + carried + skip_gain[None, :, None] * x_heads.astype(jnp.float32)
    ) * live_block[:, None, None]
    return output.astype(jnp.bfloat16).reshape(BLK, -1)


def join_states(earlier, later):
    return (earlier[0] + later[0], jnp.exp(later[0])[:, None, :, None] * earlier[1] + later[1])


def spread_channels(state_rows):
    flat_rows = state_rows.reshape(state_rows.shape[0], state_rows.shape[1], -1)
    return lax.all_to_all(flat_rows, "tp", split_axis=2, concat_axis=0, tiled=True)


def shards(
    x_in,
    dt_raw,
    bc_in,
    decay_rate,
    skip_gain,
    kv_pre,
    lengths,
    group_of,
    slot_of,
    dec_x,
    dec_dt,
    dec_bc,
    dec_z,
    norm_gain,
    dec_q,
    dec_kv,
):
    seq_count = lax.axis_size("seq")
    seq_index = lax.axis_index("seq")
    tp_index = lax.axis_index("tp")
    per_tp, tok_rows, width = x_in.shape
    heads = decay_rate.shape[0]
    head_size = width // heads
    states = bc_in.shape[2] // 2
    requests = lengths.shape[0]
    blocks = tok_rows // BLK
    request_ids = tp_index * per_tp + jnp.arange(per_tp, dtype=jnp.int32)
    own_lengths = jnp.take(lengths, request_ids)
    positions = seq_index * tok_rows + jnp.arange(tok_rows, dtype=jnp.int32)
    live = (positions[None, :] < own_lengths[:, None]).astype(jnp.float32)
    step_size = jax.nn.softplus(dt_raw.astype(jnp.float32)) * live[:, :, None]
    log_decay = -step_size * decay_rate[None, None, :]
    local_states, block_ends = jax.vmap(block_terms)(x_in, step_size, log_decay, bc_in)
    local_states = local_states.reshape(per_tp, blocks, states, heads, head_size)
    block_ends = block_ends.reshape(per_tp, blocks, heads)

    def accumulate(carry, item):
        return (join_states(carry, (item[1], item[0])), None)

    zero_log = jnp.zeros((per_tp, heads), jnp.float32)
    zero_state = jnp.zeros((per_tp, states, heads, head_size), jnp.float32)
    totals, unused = lax.scan(
        accumulate,
        (zero_log, zero_state),
        (jnp.swapaxes(local_states, 0, 1), jnp.swapaxes(block_ends, 0, 1)),
    )
    total_log, total_state = totals
    start_log, start_state = prefix(
        (total_log, total_state), "seq", join_states, (zero_log, zero_state)
    )

    def run_request(inputs):
        x_rows, step_rows, log_rows, bc_rows, live_rows, entering, local_rows, end_rows = inputs

        def advance(carry_state, block):
            x_block, step_block, log_block, bc_block, live_block, local_state, block_end = block
            output = block_output(
                x_block, step_block, log_block, bc_block, live_block, carry_state, skip_gain
            )
            return (jnp.exp(block_end)[None, :, None] * carry_state + local_state, output)

        unused_state, outputs = lax.scan(
            advance,
            entering,
            (
                x_rows.reshape(blocks, BLK, width),
                step_rows.reshape(blocks, BLK, heads),
                log_rows.reshape(blocks, BLK, heads),
                bc_rows.reshape(blocks, BLK, 2 * states),
                live_rows.reshape(blocks, BLK),
                local_rows,
                end_rows,
            ),
        )
        return outputs.reshape(tok_rows, width)

    y_pre = lax.map(
        run_request,
        (x_in, step_size, log_decay, bc_in, live, start_state, local_states, block_ends),
    )
    r_of_group = (
        jnp.zeros((requests,), jnp.int32).at[group_of].set(jnp.arange(requests, dtype=jnp.int32))
    )
    my_request = jnp.take(r_of_group, seq_index)
    my_length = jnp.take(lengths, my_request)
    inclusive = join_states((start_log, start_state), (total_log, total_state))
    ending = broadcast(inclusive[1], "seq", seq_count - 1)
    handed = jnp.take(spread_channels(ending), my_request, axis=0)
    head_rows = lax.all_to_all(kv_pre, "tp", split_axis=2, concat_axis=0, tiled=True)
    sorted_rows = jnp.take(head_rows, r_of_group, axis=0)
    mine = lax.all_to_all(sorted_rows, "seq", split_axis=0, concat_axis=1, tiled=True)[0]
    full_length = mine.shape[0]
    valid = jnp.arange(full_length) < my_length
    kept = jnp.where(valid[:, None], mine, jnp.zeros((), jnp.bfloat16))
    page_count = full_length // PAGE
    source = (
        jnp.zeros((page_count,), jnp.int32)
        .at[jnp.take(slot_of, my_request, axis=0)]
        .set(jnp.arange(page_count, dtype=jnp.int32))
    )
    kv_pool = kept.reshape(page_count, PAGE, -1)[source].reshape(1, full_length, -1)
    head_slice = dec_dt.shape[2]
    rate_slice = lax.dynamic_slice_in_dim(decay_rate, tp_index * head_slice, head_slice)
    skip_slice = lax.dynamic_slice_in_dim(skip_gain, tp_index * head_slice, head_slice)
    carry_state = handed.reshape(states, head_slice, head_size)
    turns = dec_x.shape[1]
    mamba_rows = []
    for turn_index in range(turns):
        x_now = dec_x[0, turn_index].astype(jnp.float32).reshape(head_slice, head_size)
        step_now = jax.nn.softplus(dec_dt[0, turn_index].astype(jnp.float32))
        b_now = dec_bc[0, turn_index, :states].astype(jnp.float32)
        c_now = dec_bc[0, turn_index, states:].astype(jnp.float32)
        carry_state = (
            jnp.exp(-step_now * rate_slice)[None, :, None] * carry_state
            + b_now[:, None, None] * (step_now[:, None] * x_now)[None]
        )
        read_out = (
            jnp.einsum("n,nhp->hp", c_now, carry_state, precision=highest)
            + skip_slice[:, None] * x_now
        )
        gated = read_out * jax.nn.silu(dec_z[0, turn_index].astype(jnp.float32)).reshape(
            head_slice, head_size
        )
        squares = lax.psum(jnp.sum(gated * gated), "tp")
        factor = lax.rsqrt(squares / width + 1e-05)
        mamba_rows.append(
            ((gated * factor).reshape(-1) * norm_gain.astype(jnp.float32)).astype(jnp.bfloat16)
        )
    dec_mamba = jnp.stack(mamba_rows)[None]
    dec_state = carry_state.reshape(1, states, -1)
    scale = HD ** (-0.5)
    kv_slice = mine.shape[1] // (2 * HD)
    cache = mine.reshape(full_length, kv_slice, 2, HD)
    fresh_rows = dec_kv[0].reshape(turns, kv_slice, 2, HD)
    grouped = dec_q[0].reshape(turns, kv_slice, -1, HD)
    scores_old = (
        jnp.einsum("skgd,lkd->skgl", grouped, cache[:, :, 0], preferred_element_type=jnp.float32)
        * scale
    )
    scores_old = jnp.where(valid[None, None, None, :], scores_old, -1e30)
    order = jnp.arange(turns)
    allowed = (order[None, :] <= order[:, None])[:, None, None, :]
    scores_new = jnp.where(
        allowed,
        jnp.einsum(
            "skgd,jkd->skgj", grouped, fresh_rows[:, :, 0], preferred_element_type=jnp.float32
        )
        * scale,
        -1e30,
    )
    peak = jnp.maximum(jnp.max(scores_old, axis=-1), jnp.max(scores_new, axis=-1))[..., None]
    probs_old = jnp.exp(scores_old - peak)
    probs_new = jnp.exp(scores_new - peak)
    total = jnp.sum(probs_old, axis=-1) + jnp.sum(probs_new, axis=-1)
    mixed = jnp.einsum(
        "skgl,lkd->skgd",
        probs_old.astype(jnp.bfloat16),
        cache[:, :, 1],
        preferred_element_type=jnp.float32,
    )
    mixed = mixed + jnp.einsum(
        "skgj,jkd->skgd",
        probs_new.astype(jnp.bfloat16),
        fresh_rows[:, :, 1],
        preferred_element_type=jnp.float32,
    )
    dec_attn = (mixed / total[..., None]).astype(jnp.bfloat16).reshape(1, turns, -1)
    return (y_pre, kv_pool, dec_mamba, dec_state, dec_attn)


def solution(mesh):
    return jax.shard_map(
        shards,
        mesh=mesh,
        in_specs=(
            P("tp", "seq", None),
            P("tp", "seq", None),
            P("tp", "seq", None),
            P(),
            P(),
            P("tp", "seq", None),
            P(),
            P(),
            P(),
            P("seq", None, "tp"),
            P("seq", None, "tp"),
            P("seq", None, None),
            P("seq", None, "tp"),
            P("tp"),
            P("seq", None, "tp"),
            P("seq", None, "tp"),
        ),
        out_specs=(
            P("tp", "seq", None),
            P("seq", None, "tp"),
            P("seq", None, "tp"),
            P("seq", None, "tp"),
            P("seq", None, "tp"),
        ),
        check_vma=False,
    )
```

profile of v0, /device:TPU:0, one launch (start us, length us, event | category | flops | bytes accessed | tf_op | source)
XLA Modules:
  0.0 496.3 jit_solution(14340519387508712559)
XLA Ops:
  11.2 12.0 %copy.94 = bf16[2,256,8192]{1,2,0:T(8,128)(2,1)} copy(bf16[2,256,8192]{2,1,0:T(8,128)(2,1)} %param.20) | data formatting | bytes 16777216 | tf_op jit(solution)/shard_map/while | solution.py:157
  23.2 5.7 %add_bitcast_fusion = f32[2,16,128,64]{3,1,2,0:T(8,128)S(1)} fusion(bf16[2,256,128,64]{1,3,2,0:T(8,128)(2,1)} %bitcast.286, f32[2,256,128]{1,2,0:T(8,128)S(1)} %copy.90, f32[2,128]{1,0:T(2,128)S(1)} %get-tuple-element.451, bf16[2,256,32]{1,2,0:T(8,128)(2,1)S(1)} %copy-done.9), kind=kOutput, calls=%fused_computation.51 | convolution fusion | flops 147062784 | bytes 9716736 | tf_op jit(solution)/shard_map/vmap(sn,shp->nhp)/dot_general | solution.py:40
  30.7 6.1 %copy.97 = bf16[2,256,2048]{1,0,2:T(2,128)(2,1)} copy(bf16[2,256,2048]{2,1,0:T(8,128)(2,1)} %param.25) | data formatting | bytes 4194304 | tf_op args[5]
  36.9 5.5 %all-to-all-start = ((bf16[2,256,2048]{1,0,2:T(2,128)(2,1)}), bf16[2,256,2048]{1,0,2:T(2,128)(2,1)S(1)}, u32[]{:S(2)}, u32[]{:S(2)}) async-start(bf16[2,256,2048]{1,0,2:T(2,128)(2,1)} %copy.97), calls=%async_computation | async-start | bytes 4194304 | tf_op jit(solution)/shard_map/all_to_all | solution.py:169
  45.0 24.6 %all-to-all-done = bf16[2,256,2048]{1,0,2:T(2,128)(2,1)S(1)} async-done(((bf16[2,256,2048]{1,0,2:T(2,128)(2,1)}), bf16[2,256,2048]{1,0,2:T(2,128)(2,1)S(1)}, u32[]{:S(2)}, u32[]{:S(2)}) %all-to-all-start) | async-done | bytes 2097184 | tf_op jit(solution)/shard_map/all_to_all | solution.py:169
  71.2 4.0 copy.99
  75.2 2.5 gather_fusion.1
  79.3 7.1 %all-to-all-start.1 = ((bf16[16,256,256]{2,1,0:T(8,128)(2,1)}), bf16[16,256,256]{2,1,0:T(8,128)(2,1)S(1)}, u32[]{:S(2)}, u32[]{:S(2)}) async-start(bf16[16,256,256]{2,1,0:T(8,128)(2,1)} %broadcast_select_fusion), calls=%async_computation.1 | async-start | bytes 4194304 | tf_op jit(solution)/shard_map/all_to_all | solution.py:171
  103.7 46.2 %all-gather = f32[32,1,128]{2,1,0:T(1,128)S(1)} all-gather(f32[2,1,128]{2,1,0:T(1,128)S(1)} %slice.168), channel_id=2, replica_groups=mesh['seq'=16,'tp'=8] {'seq'}, dimensions={0}, use_global_device_ids=true | all-gather | bytes 17408 | tf_op jit(solution)/shard_map/all_gather | solution.py:16
  150.9 2.2 reshape.1360
  153.1 6.5 %fusion.109 = (bf16[4096,1,1,128]{3,2,0,1:T(2,128)(2,1)S(1)}, bf16[4096,1,1,128]{3,2,0,1:T(2,128)(2,1)}) fusion(bf16[4096,1,2,128]{3,2,0,1:T(2,128)(2,1)} %reshape.1360), kind=kLoop, calls=%fused_computation.221 | loop fusion | bytes 4194304 | tf_op jit(solution)/shard_map/slice | solution.py:217
  160.9 6.2 %all-gather.4.cloned.1.call-done = f32[32,16,128,64]{2,3,1,0:T(8,128)} async-done(((f32[2,16,128,64]{2,3,1,0:T(8,128)}), f32[32,16,128,64]{2,3,1,0:T(8,128)}) %all-gather.4.cloned.1.call-update) | async-done | bytes 16777232 | tf_op jit(solution)/shard_map/all_gather | solution.py:16
  167.1 78.4 %while.40 = (s32[]{:T(128)}, f32[2,16,128,64]{3,2,1,0:T(8,128)}, s32[]{:T(128)}, f32[16,2,128]{2,1,0:T(2,128)S(1)}, f32[16,2,16,128,64]{3,4,2,1,0:T(8,128)}, /*index=5*/s32[]{:T(128)}, s32[]{:T(128)}) while((s32[]{:T(128)}, f32[2,16,128,64]{3,2,1,0:T(8,128)}, s32[]{:T(128)}, f32[16,2,128]{2,1,0:T(2,128)S(1)}, ...), condition=%wide.region_3.4_spmd.clone, body=%wide.region_2.3_spmd.clone.sunk | while | flops 1048580 | bytes 7343209 | solution.py:25
  172.8 3.4 fusion.139
  178.1 3.4 fusion.139
  183.4 3.4 fusion.139
  188.8 3.4 fusion.139
  194.1 3.4 fusion.139
  199.4 3.4 fusion.139
  204.8 3.4 fusion.139
  210.1 3.4 fusion.139
  215.4 3.4 fusion.139
  220.8 3.4 fusion.139
  226.1 3.4 fusion.139
  231.4 3.4 fusion.139
  236.8 3.4 fusion.139
  242.1 3.4 fusion.139
  245.5 3.7 fusion.27
  256.4 3.7 gather_fusion.2
  260.9 77.3 %all-reduce.3.cloned.1.call-done = f32[2,16,8192]{2,1,0:T(8,128)} async-done(((f32[2,16,8192]{2,1,0:T(8,128)}), f32[2,16,8192]{2,1,0:T(8,128)}) %all-reduce.3.cloned.1.call-update) | async-done | bytes 1048592 | tf_op jit(solution)/shard_map/psum | solution.py:30
  338.2 9.9 %copy.102 = f32[2,16,8192]{1,0,2:T(2,128)} copy(f32[2,16,8192]{2,1,0:T(8,128)} %all-reduce.3.cloned.1.call-done) | data formatting | bytes 2097152 | tf_op jit(solution)/shard_map/psum | solution.py:30
  348.1 13.6 %reshape.1427 = f32[8,1,32768]{2,1,0:T(1,128)} reshape(f32[8192,2,16]{2,1,0:T(2,128)} %bitcast.287) | data formatting | bytes 2097152
  361.7 4.6 all-to-all-start.2
  366.3 70.9 %while.39 = (s32[]{:T(128)}, bf16[2,256,8192]{2,1,0:T(8,128)(2,1)}, bf16[2,256,8192]{1,2,0:T(8,128)(2,1)}, bf16[2,256,32]{1,2,0:T(8,128)(2,1)S(1)}, f32[2,256,12...) while((s32[]{:T(128)}, bf16[2,256,8192]{2,1,0:T(8,128)(2,1)}, ...), condition=%wide.region_7.8_spmd, body=%wide.region_4.7_spmd.sunk | while | flops 1547764096 | bytes 77934240 | solution.py:157
  366.8 2.5 constant_dynamic-slice_fusion.9
  369.6 11.3 %fusion.137 = f32[128,64,256]{2,1,0:T(8,128)} fusion(bf16[256,128,64]{0,2,1:T(8,128)(2,1)S(1)} %bitcast.283, f32[128,256]{1,0:T(8,128)S(1)} %bitcast.296, f32[128,256]{1,0:T(8,128)S(1)} %copy.189, f32[256,256]{1,0:T(8,128)S(1)} %fusion.136, pred[256,256]{1,0:T(8,128)(4,1)S(1)} %iota_compare_fusion.4), kind=kOutput, calls=%fused_computation.6.clone.1 | convolution fusion | flops 1124073472 | bytes 13172736 | tf_op jit(solution)/shard_map/while/body/eval_jaxpr/while/body/eval_jaxpr/hts,shp->thp/dot_general | solution.py:61
  381.6 9.1 %fusion.138 = bf16[256,128,64]{0,2,1:T(8,128)(2,1)} fusion(f32[128,64,256]{2,1,0:T(8,128)} %fusion.137, bf16[256,128,64]{0,2,1:T(8,128)(2,1)} %bitcast.284, f32[256]{0:T(256)S(1)} %bitcast.302, f32[128]{0:T(128)S(1)} %get-tuple-element.612, f32[256,128]{0,1:T(8,128)S(1)} %copy.190, f32[16,128,64]{2,0,1:T(8,128)S(1)} %copy.191, ...), kind=kOutput, calls=%fused_computation.16.clone.1 | convolution fusion | flops 417333248 | bytes 17966592 | tf_op jit(solution)/shard_map/while/body/eval_jaxpr/while/body/eval_jaxpr/tn,nhp->thp/dot_general | solution.py:62
  390.8 6.4 %copy.192 = bf16[1,256,8192]{2,1,0:T(8,128)(2,1)} copy(bf16[1,256,8192]{1,2,0:T(8,128)(2,1)} %bitcast.285) | data formatting | bytes 8388608 | tf_op jit(solution)/shard_map/while/body/jit(dynamic_update_index_in_dim)/dynamic_update_slice | solution.py:157
  397.2 4.6 constant_dynamic-update-slice_fusion.2
  402.3 2.5 constant_dynamic-slice_fusion.9
  405.0 11.3 %fusion.137 = f32[128,64,256]{2,1,0:T(8,128)} fusion(bf16[256,128,64]{0,2,1:T(8,128)(2,1)S(1)} %bitcast.283, f32[128,256]{1,0:T(8,128)S(1)} %bitcast.296, f32[128,256]{1,0:T(8,128)S(1)} %copy.189, f32[256,256]{1,0:T(8,128)S(1)} %fusion.136, pred[256,256]{1,0:T(8,128)(4,1)S(1)} %iota_compare_fusion.4), kind=kOutput, calls=%fused_computation.6.clone.1 | convolution fusion | flops 1124073472 | bytes 13172736 | tf_op jit(solution)/shard_map/while/body/eval_jaxpr/while/body/eval_jaxpr/hts,shp->thp/dot_general | solution.py:61
  417.1 9.1 %fusion.138 = bf16[256,128,64]{0,2,1:T(8,128)(2,1)} fusion(f32[128,64,256]{2,1,0:T(8,128)} %fusion.137, bf16[256,128,64]{0,2,1:T(8,128)(2,1)} %bitcast.284, f32[256]{0:T(256)S(1)} %bitcast.302, f32[128]{0:T(128)S(1)} %get-tuple-element.612, f32[256,128]{0,1:T(8,128)S(1)} %copy.190, f32[16,128,64]{2,0,1:T(8,128)S(1)} %copy.191, ...), kind=kOutput, calls=%fused_computation.16.clone.1 | convolution fusion | flops 417333248 | bytes 17966592 | tf_op jit(solution)/shard_map/while/body/eval_jaxpr/while/body/eval_jaxpr/tn,nhp->thp/dot_general | solution.py:62
  426.2 6.4 %copy.192 = bf16[1,256,8192]{2,1,0:T(8,128)(2,1)} copy(bf16[1,256,8192]{1,2,0:T(8,128)(2,1)} %bitcast.285) | data formatting | bytes 8388608 | tf_op jit(solution)/shard_map/while/body/jit(dynamic_update_index_in_dim)/dynamic_update_slice | solution.py:157
  432.6 4.6 constant_dynamic-update-slice_fusion.2
  437.8 4.4 reduce.52
  442.2 14.2 %reshape.1428 = f32[8192,2,16]{2,1,0:T(2,128)} reshape(f32[8,32768]{1,0:T(8,128)S(1)} %reduce.52) | data formatting | bytes 2097152
  456.7 10.2 %copy.123 = f32[2,16,8,1024]{3,1,0,2:T(8,128)S(1)} copy(f32[2,16,8,1024]{1,0,3,2:T(2,128)} %bitcast.288) | data formatting | bytes 2097152 | tf_op jit(solution)/shard_map/all_to_all | solution.py:77
  469.8 16.0 %all-reduce = (f32[]{:T(128)}, f32[]{:T(128)}, f32[]{:T(128)}, f32[]{:T(128)}) all-reduce(f32[]{:T(128)} %get-tuple-element.460, f32[]{:T(128)} %get-tuple-element.458, f32[]{:T(128)} %get-tuple-element.456, f32[]{:T(128)} %get-tuple-element.401), channel_id=1, replica_groups=mesh['seq'=16,'tp'=8] {'tp'}, use_global_device_ids=true, to_apply=%region_18.19 | all-reduce | flops 4 | bytes 32 | tf_op jit(solution)/shard_map/psum | solution.py:204
  (323 shorter events, 75.1 us)
Async XLA Ops:
  7.2 159.9 %all-gather.4.cloned.1.call-start = ((), (), s32[]{:S(2)}) async-start(), calls=%async_computation.4 | async-start | bytes 17825792 | tf_op jit(solution)/shard_map/all_gather | solution.py:16
  8.6 14.6 %copy-start.11 = (f32[2,256]{1,0:T(2,128)}, f32[2,256]{1,0:T(2,128)S(1)}, u32[]{:S(2)}) copy-start(f32[2,256]{1,0:T(2,128)S(1)} %compare_convert_fusion) | copy-start | bytes 6148
  11.2 12.0 %copy-start.9 = (bf16[2,256,32]{1,2,0:T(8,128)(2,1)S(1)}, bf16[2,256,32]{1,2,0:T(8,128)(2,1)}, u32[]{:S(2)}) copy-start(bf16[2,256,32]{1,2,0:T(8,128)(2,1)} %param.22) | copy-start | bytes 98308
  36.9 32.7 %all-to-all-start = ((bf16[2,256,2048]{1,0,2:T(2,128)(2,1)}), bf16[2,256,2048]{1,0,2:T(2,128)(2,1)S(1)}, u32[]{:S(2)}, u32[]{:S(2)}) async-start(bf16[2,256,2048]{1,0,2:T(2,128)(2,1)} %copy.97), calls=%async_computation | async-start | bytes 4194304 | tf_op jit(solution)/shard_map/all_to_all | solution.py:169
  42.5 48.6 %copy-start.49 = (f32[16]{0:T(128)}, f32[16]{0:T(128)S(1)}, u32[]{:S(2)}) copy-start(f32[16]{0:T(128)S(1)} %get-tuple-element.409) | copy-start | bytes 196
  42.6 46.3 %copy-start.47 = (f32[16]{0:T(128)}, f32[16]{0:T(128)S(1)}, u32[]{:S(2)}) copy-start(f32[16]{0:T(128)S(1)} %get-tuple-element.448) | copy-start | bytes 196
  42.6 47.1 %copy-start.45 = (f32[16]{0:T(128)}, f32[16]{0:T(128)S(1)}, u32[]{:S(2)}) copy-start(f32[16]{0:T(128)S(1)} %get-tuple-element.446) | copy-start | bytes 196
  42.6 47.8 %copy-start.43 = (f32[16]{0:T(128)}, f32[16]{0:T(128)S(1)}, u32[]{:S(2)}) copy-start(f32[16]{0:T(128)S(1)} %get-tuple-element.412) | copy-start | bytes 196
  79.3 16.4 %copy-start.36 = (f32[128]{0:T(128)S(1)}, f32[128]{0:T(128)}, u32[]{:S(2)}) copy-start(f32[128]{0:T(128)} %param.24) | copy-start | bytes 1540
  79.3 17.1 %copy-start.27 = (bf16[1,4,1024]{2,1,0:T(4,128)(2,1)S(1)}, bf16[1,4,1024]{2,1,0:T(4,128)(2,1)}, u32[]{:S(2)}) copy-start(bf16[1,4,1024]{2,1,0:T(4,128)(2,1)} %param.32) | copy-start | bytes 24580
  79.3 70.7 %copy-start.38 = (bf16[1,4,1024]{2,1,0:T(4,128)(2,1)S(1)}, bf16[1,4,1024]{2,1,0:T(4,128)(2,1)}, u32[]{:S(2)}) copy-start(bf16[1,4,1024]{2,1,0:T(4,128)(2,1)} %param.34) | copy-start | bytes 24580
  79.3 70.7 %copy-start.55 = (bf16[1,4,256]{2,1,0:T(4,128)(2,1)S(1)}, bf16[1,4,256]{2,1,0:T(4,128)(2,1)}, u32[]{:S(2)}) copy-start(bf16[1,4,256]{2,1,0:T(4,128)(2,1)} %param.35) | copy-start | bytes 6148
  79.3 71.0 %copy-start.13 = (bf16[1,4,32]{2,1,0:T(4,128)(2,1)S(1)}, bf16[1,4,32]{2,1,0:T(4,128)(2,1)}, u32[]{:S(2)}) copy-start(bf16[1,4,32]{2,1,0:T(4,128)(2,1)} %param.31) | copy-start | bytes 772
  79.3 71.6 %all-to-all-start.1 = ((bf16[16,256,256]{2,1,0:T(8,128)(2,1)}), bf16[16,256,256]{2,1,0:T(8,128)(2,1)S(1)}, u32[]{:S(2)}, u32[]{:S(2)}) async-start(bf16[16,256,256]{2,1,0:T(8,128)(2,1)} %broadcast_select_fusion), calls=%async_computation.1 | async-start | bytes 4194304 | tf_op jit(solution)/shard_map/all_to_all | solution.py:171
  86.4 251.8 %all-reduce.3.cloned.1.call-start = ((), (), s32[]{:S(2)}) async-start(), calls=%async_computation.3 | async-start | bytes 2097152 | tf_op jit(solution)/shard_map/psum | solution.py:30
  361.7 75.6 %all-to-all-start.2 = ((f32[8,1,32768]{2,1,0:T(1,128)}), f32[8,1,32768]{2,1,0:T(1,128)}, u32[]{:S(2)}, u32[]{:S(2)}) async-start(f32[8,1,32768]{2,1,0:T(1,128)} %reshape.1427), calls=%async_computation.2 | async-start | bytes 2097152 | tf_op jit(solution)/shard_map/all_to_all | solution.py:77
  369.3 11.6 %copy-start.1 = (bf16[1,256,8192]{1,2,0:T(8,128)(2,1)}, bf16[1,256,8192]{1,2,0:T(8,128)(2,1)S(1)}, u32[]{:S(2)}) copy-start(bf16[1,256,8192]{1,2,0:T(8,128)(2,1)S(1)} %constant_dynamic-slice_fusion.9) | copy-start | bytes 12582916 | tf_op jit(solution)/shard_map/while
  404.7 11.6 %copy-start.1 = (bf16[1,256,8192]{1,2,0:T(8,128)(2,1)}, bf16[1,256,8192]{1,2,0:T(8,128)(2,1)S(1)}, u32[]{:S(2)}) copy-start(bf16[1,256,8192]{1,2,0:T(8,128)(2,1)S(1)} %constant_dynamic-slice_fusion.9) | copy-start | bytes 12582916 | tf_op jit(solution)/shard_map/while
  456.4 10.5 %copy-start.29 = (f32[1024]{0:T(1024)S(1)}, f32[1024]{0:T(1024)}, u32[]{:S(2)}) copy-start(f32[1024]{0:T(1024)} %get-tuple-element.440) | copy-start | bytes 12292
  456.4 10.5 %copy-start.30 = (f32[1024]{0:T(1024)S(1)}, f32[1024]{0:T(1024)}, u32[]{:S(2)}) copy-start(f32[1024]{0:T(1024)} %mul.842) | copy-start | bytes 12292
  456.4 10.5 %copy-start.31 = (f32[1024]{0:T(1024)S(1)}, f32[1024]{0:T(1024)}, u32[]{:S(2)}) copy-start(f32[1024]{0:T(1024)} %mul.845) | copy-start | bytes 12292
  456.4 10.5 %copy-start.32 = (f32[1024]{0:T(1024)S(1)}, f32[1024]{0:T(1024)}, u32[]{:S(2)}) copy-start(f32[1024]{0:T(1024)} %mul.851) | copy-start | bytes 12292
  456.5 10.5 %copy-start.33 = (f32[1024]{0:T(1024)S(1)}, f32[1024]{0:T(1024)}, u32[]{:S(2)}) copy-start(f32[1024]{0:T(1024)} %mul.848) | copy-start | bytes 12292
  456.5 10.5 %copy-start.34 = (f32[1024]{0:T(1024)S(1)}, f32[1024]{0:T(1024)}, u32[]{:S(2)}) copy-start(f32[1024]{0:T(1024)} %get-tuple-element.434) | copy-start | bytes 12292
  456.5 10.5 %copy-start.35 = (f32[1024]{0:T(1024)S(1)}, f32[1024]{0:T(1024)}, u32[]{:S(2)}) copy-start(f32[1024]{0:T(1024)} %get-tuple-element.436) | copy-start | bytes 12292
  456.5 10.5 %copy-start.39 = (f32[16]{0:T(128)S(1)}, f32[16]{0:T(128)}, u32[]{:S(2)}) copy-start(f32[16]{0:T(128)} %get-tuple-element.452) | copy-start | bytes 196
  456.5 10.5 %copy-start.40 = (f32[16]{0:T(128)S(1)}, f32[16]{0:T(128)}, u32[]{:S(2)}) copy-start(f32[16]{0:T(128)} %get-tuple-element.453) | copy-start | bytes 196
  456.5 10.5 %copy-start.41 = (f32[16]{0:T(128)S(1)}, f32[16]{0:T(128)}, u32[]{:S(2)}) copy-start(f32[16]{0:T(128)} %get-tuple-element.454) | copy-start | bytes 196
  456.5 10.5 %copy-start.42 = (f32[16]{0:T(128)S(1)}, f32[16]{0:T(128)}, u32[]{:S(2)}) copy-start(f32[16]{0:T(128)} %get-tuple-element.455) | copy-start | bytes 196
  456.5 11.3 %copy-start.15 = (f32[16,64]{1,0:T(8,128)S(1)}, f32[16,64]{1,0:T(8,128)}, u32[]{:S(2)}) copy-start(f32[16,64]{1,0:T(8,128)} %mul.814) | copy-start | bytes 12292
  456.5 11.3 %copy-start.16 = (f32[16,64]{1,0:T(8,128)S(1)}, f32[16,64]{1,0:T(8,128)}, u32[]{:S(2)}) copy-start(f32[16,64]{1,0:T(8,128)} %mul.831) | copy-start | bytes 12292
  456.5 11.3 %copy-start.17 = (f32[16,64]{1,0:T(8,128)S(1)}, f32[16,64]{1,0:T(8,128)}, u32[]{:S(2)}) copy-start(f32[16,64]{1,0:T(8,128)} %mul.779) | copy-start | bytes 12292
  456.6 11.3 %copy-start.18 = (f32[16,64]{1,0:T(8,128)S(1)}, f32[16,64]{1,0:T(8,128)}, u32[]{:S(2)}) copy-start(f32[16,64]{1,0:T(8,128)} %mul.797) | copy-start | bytes 12292
  456.6 11.3 %copy-start.44 = (f32[16]{0:T(128)S(1)}, f32[16]{0:T(128)}, u32[]{:S(2)}) copy-start(f32[16]{0:T(128)} %copy-done.43) | copy-start | bytes 196
  456.6 11.3 %copy-start.46 = (f32[16]{0:T(128)S(1)}, f32[16]{0:T(128)}, u32[]{:S(2)}) copy-start(f32[16]{0:T(128)} %copy-done.45) | copy-start | bytes 196
  456.6 11.3 %copy-start.48 = (f32[16]{0:T(128)S(1)}, f32[16]{0:T(128)}, u32[]{:S(2)}) copy-start(f32[16]{0:T(128)} %copy-done.47) | copy-start | bytes 196
  456.6 11.3 %copy-start.50 = (f32[16]{0:T(128)S(1)}, f32[16]{0:T(128)}, u32[]{:S(2)}) copy-start(f32[16]{0:T(128)} %copy-done.49) | copy-start | bytes 196
  456.6 11.5 %copy-start.14 = (bf16[1,4,32]{2,1,0:T(4,128)(2,1)S(1)}, bf16[1,4,32]{2,1,0:T(4,128)(2,1)}, u32[]{:S(2)}) copy-start(bf16[1,4,32]{2,1,0:T(4,128)(2,1)} %param.31) | copy-start | bytes 772
  456.6 12.4 %copy-start.19 = (f32[16,64]{1,0:T(8,128)S(1)}, f32[16,64]{1,0:T(8,128)}, u32[]{:S(2)}) copy-start(f32[16,64]{1,0:T(8,128)} %reshape.1276) | copy-start | bytes 12292
  456.6 12.4 %copy-start.20 = (f32[16,64]{1,0:T(8,128)S(1)}, f32[16,64]{1,0:T(8,128)}, u32[]{:S(2)}) copy-start(f32[16,64]{1,0:T(8,128)} %reshape.1277) | copy-start | bytes 12292
  456.6 12.4 %copy-start.21 = (f32[16,64]{1,0:T(8,128)S(1)}, f32[16,64]{1,0:T(8,128)}, u32[]{:S(2)}) copy-start(f32[16,64]{1,0:T(8,128)} %reshape.1281) | copy-start | bytes 12292
  456.7 12.4 %copy-start.22 = (f32[16,64]{1,0:T(8,128)S(1)}, f32[16,64]{1,0:T(8,128)}, u32[]{:S(2)}) copy-start(f32[16,64]{1,0:T(8,128)} %reshape.1282) | copy-start | bytes 12292
  456.7 12.4 %copy-start.23 = (f32[16,64]{1,0:T(8,128)S(1)}, f32[16,64]{1,0:T(8,128)}, u32[]{:S(2)}) copy-start(f32[16,64]{1,0:T(8,128)} %reshape.1286) | copy-start | bytes 12292
  456.7 12.4 %copy-start.24 = (f32[16,64]{1,0:T(8,128)S(1)}, f32[16,64]{1,0:T(8,128)}, u32[]{:S(2)}) copy-start(f32[16,64]{1,0:T(8,128)} %reshape.1287) | copy-start | bytes 12292
  456.7 12.4 %copy-start.25 = (f32[16,64]{1,0:T(8,128)S(1)}, f32[16,64]{1,0:T(8,128)}, u32[]{:S(2)}) copy-start(f32[16,64]{1,0:T(8,128)} %reshape.1291) | copy-start | bytes 12292
  456.7 12.4 %copy-start.26 = (f32[16,64]{1,0:T(8,128)S(1)}, f32[16,64]{1,0:T(8,128)}, u32[]{:S(2)}) copy-start(f32[16,64]{1,0:T(8,128)} %reshape.1292) | copy-start | bytes 12292
  456.7 12.4 %copy-start.54 = (f32[16]{0:T(128)S(1)}, f32[16]{0:T(128)}, u32[]{:S(2)}) copy-start(f32[16]{0:T(128)} %dynamic_slice.80) | copy-start | bytes 196
  456.7 32.1 %copy-start.53 = (bf16[1024]{0:T(1024)(128)(2,1)S(1)}, bf16[1024]{0:T(1024)(128)(2,1)}, u32[]{:S(2)}) copy-start(bf16[1024]{0:T(1024)(128)(2,1)} %param.33) | copy-start | bytes 6148
  (15 other events, 73.1 us)
Sparse Core Ops, SparseCore 0:
  30.8 136.1 all-gather.3
  251.6 86.6 all-reduce.2
where the time goes:
time: 500 us; the launch traced here: 496 us
  local copies, waits for them, and re-layouts  167 us (33%)
  waiting for transfers between devices  108 us (22%)
  other arithmetic  70.3 us (14%)
  blocking collectives  62.2 us (12%)
  matrix products  51.4 us (10%)
  between operations  19 us (4%)
  starting transfers between devices  17.4 us (3%)
    psum x1, waiting for transfers between devices, broadcast(): return lax.psum(jnp.where(mine, value, jnp.zeros_like(value)), axis)  77.3 us
    select_n x15, other arithmetic, step(): jnp.where(position < mine, new, old)  49.4 us
    all_gather x1, blocking collectives, prefix(): pieces = jax.tree.map(lambda part: lax.all_gather(part, axis), value)  46.2 us
    unnamed x115, local copies, waits for them, and re-layouts  34.2 us
    dynamic_slice x30, local copies, waits for them, and re-layouts, step(): longer = join(total, jax.tree.map(lambda part: part[position], pieces))  28.5 us
    all_to_all x1, waiting for transfers between devices, shards(): lax.all_to_all(kv_pre, 'tp', split_axis=2, concat_axis=0, tiled=True)  24.6 us
    dot_general x2, matrix products, block_output(): jnp.einsum('hts,shp->thp', weights, x_heads, preferred_element_type=jnp.f...  22.5 us
    dynamic_update_slice x4, local copies, waits for them, and re-layouts, shards(): lax.map(run_request, (x_in, step_size, log_decay, bc_in, live, start_stat...  22.1 us
  transfers between devices with their start and end apart: 5, of which 3 were waited for; matrix products, arithmetic and copies ran while one was open for 25% of the time, Pallas kernels for 0%

commit v1 on v0

v1 whole, which is shorter than its diff:
```python
import jax
import jax.numpy as jnp
from jax import lax
from jax.experimental import pallas as pl
from jax.experimental.pallas import tpu as pltpu
from jax.sharding import PartitionSpec as P

HD = 128
BLK = 256
HP = 64
NS = 16
HEADS = 128
WIDTH = 8192
SEQ = 16
TP = 8
WC = 1024
LANE = 128
CHUNKS = WC // LANE
STEPS = WIDTH // WC
ROW = 4
PARTS = WIDTH // (ROW * LANE)
STATE_ROWS = 2 * PARTS * NS
FINAL_ROWS = PARTS * NS
DEC_X, DEC_Z, DEC_T = 2 * BLK, 2 * BLK + 16, 2 * BLK + 32
PAGE_ROWS = 2 * BLK + 48
F32 = jnp.float32
BF16 = jnp.bfloat16
MIB = 1024 * 1024
highest = lax.Precision.HIGHEST
ANY = pl.BlockSpec(memory_space=pl.ANY)
VM = pl.BlockSpec(memory_space=pltpu.VMEM)
SM = pl.BlockSpec(memory_space=pltpu.SMEM)


def params(mib=48):
    return pltpu.CompilerParams(vmem_limit_bytes=mib * MIB)


def cost(us):
    return pl.CostEstimate(flops=0, bytes_accessed=int(us * 3.0e6), transcendentals=0)


def softplus(v):
    return jnp.maximum(v, 0.0) + jnp.log1p(jnp.exp(-jnp.abs(v)))


def halves(v):
    high = v.astype(BF16)
    return high, (v - high.astype(F32)).astype(BF16)


def split_kernel(kv_ref, x_ref, z_ref, dt_ref, out_ref, token_ref):
    out_ref[0, :BLK, :] = kv_ref[0]
    out_ref[0, BLK : 2 * BLK, :] = kv_ref[1]

    def fold(rows):
        rows = rows.astype(F32)
        return jnp.concatenate([rows[:, q * 256 : (q + 1) * 256] for q in range(4)], axis=0)

    out_ref[0, DEC_X : DEC_X + 16, :] = fold(x_ref[0]).astype(BF16)
    out_ref[0, DEC_Z : DEC_Z + 16, :] = fold(z_ref[0]).astype(BF16)
    steps = dt_ref[0].astype(F32)
    steps = jnp.concatenate([steps, jnp.zeros((steps.shape[0], 256 - steps.shape[1]), F32)], axis=1)
    steps = jnp.concatenate([steps, jnp.zeros((12, 256), F32)], axis=0)
    out_ref[0, DEC_T : DEC_T + 16, :] = steps.astype(BF16)
    token_ref[0] = 0


def split_heads(kv_pre, dec_x, dec_z, dec_dt):
    whole = lambda h: (0, 0, 0)
    return pl.pallas_call(
        split_kernel,
        grid=(TP,),
        out_shape=[
            jax.ShapeDtypeStruct((TP, PAGE_ROWS, 2 * HD), BF16),
            jax.ShapeDtypeStruct((1,), jnp.int32),
        ],
        in_specs=[
            pl.BlockSpec((2, BLK, 2 * HD), lambda h: (0, 0, h)),
            pl.BlockSpec((1, 4, WC), whole),
            pl.BlockSpec((1, 4, WC), whole),
            pl.BlockSpec((1, 4, WC // HP), whole),
        ],
        out_specs=[pl.BlockSpec((1, PAGE_ROWS, 2 * HD), lambda h: (h, 0, 0)), SM],
        cost_estimate=cost(2),
        compiler_params=params(),
        name="split_heads",
    )(kv_pre, dec_x, dec_z, dec_dt)


def spread_matrix(ebig):
    rows = lax.broadcasted_iota(jnp.int32, ebig.shape, 0)
    cols = lax.broadcasted_iota(jnp.int32, ebig.shape, 1)
    ebig[...] = jnp.where((rows & (HEADS - 1)) == (cols >> 6), 1.0, 0.0).astype(BF16)


def spread_rows(ebig, j):
    start = pl.multiple_of(HEADS - (WC // HP) * j, 16)
    return ebig[pl.ds(start, 2 * HEADS), :]


def decays(len_ref, dt_ref, rate_ref, p):
    prompt = lax.axis_index("tp") * 2 + p
    live = jnp.where(len_ref[prompt] > lax.axis_index("seq") * BLK, 1.0, 0.0).astype(F32)
    step = softplus(dt_ref[p].astype(F32)) * live
    rows = lax.broadcasted_iota(jnp.int32, (BLK, BLK), 0)
    cols = lax.broadcasted_iota(jnp.int32, (BLK, BLK), 1)
    tri = jnp.where(rows >= cols, 1.0, 0.0).astype(F32)
    cum = jnp.dot(tri, -step * rate_ref[...], precision=highest, preferred_element_type=F32)
    mid = 0.5 * cum[BLK - 1 :, :]
    return live, step, cum - mid, mid


def block_copies(hbm, buf, sem, out=False):
    copies = []
    for p in range(2):
        for j in range(STEPS):
            cols = pl.ds(j * WC, WC)
            ends = (hbm.at[p, :, cols], buf.at[p, :, cols])
            copies.append(pltpu.make_async_copy(*(ends[::-1] if out else ends), sem.at[p * STEPS + j]))
    return copies


def block_copy(hbm, buf, sem, p, j, out=False):
    cols = pl.ds(pl.multiple_of(j * WC, WC), WC)
    ends = (hbm.at[p, :, cols], buf.at[p, :, cols])
    return pltpu.make_async_copy(*(ends[::-1] if out else ends), sem.at[p * STEPS + j])


def local_kernel(len_ref, x_hbm, dt_ref, bc_ref, rate_ref, *refs):
    outs, (stage, ft, bt, x_buf, sem) = refs[:ROW], refs[ROW:]
    for c in block_copies(x_hbm, x_buf, sem):
        c.start()
    lane = lax.broadcasted_iota(jnp.int32, (NS, LANE), 1)
    row = lax.broadcasted_iota(jnp.int32, (NS, HEADS), 0)
    heads = WC // HP
    dec = jnp.zeros((NS, HEADS), F32)
    for p in range(2):
        live, step, rel, mid = decays(len_ref, dt_ref, rate_ref, p)
        ft[p] = jnp.transpose(jnp.exp(-rel) * step)
        bt[p] = jnp.transpose(bc_ref[p].astype(F32))[:NS]
        high, low = halves(jnp.exp(mid))
        dec = jnp.where(row == p, high.astype(F32), jnp.where(row == 2 + p, low.astype(F32), dec))
    for s in range(ROW):
        stage[s, STATE_ROWS:, :] = dec.astype(BF16)
    for p in range(2):

        def body(j, carry):
            quarter, part = lax.div(j, 2), lax.rem(j, 2)
            block_copy(x_hbm, x_buf, sem, p, j).wait()
            fj = ft[p, pl.ds(pl.multiple_of(j * heads, heads), heads), :]
            for u in range(WC // 256):
                left = jnp.concatenate([bt[p] * fj[u * 4 + h : u * 4 + h + 1, :] for h in range(4)], axis=0)
                cols = pl.ds(pl.multiple_of(j * WC + u * 256, 256), 256)
                prod = jnp.dot(left.astype(BF16), x_buf[p, :, cols], preferred_element_type=F32)
                for v in range(2):
                    cols = slice(v * LANE, (v + 1) * LANE)
                    first = prod[2 * v * NS : (2 * v + 1) * NS, cols]
                    second = prod[(2 * v + 1) * NS : (2 * v + 2) * NS, cols]
                    local = jnp.where(lane < HP, first, second).astype(BF16)
                    at = ((p * 2 + part) * CHUNKS + u * 2 + v) * NS
                    stage[quarter, pl.ds(pl.multiple_of(at, NS), NS), :] = local
            return carry

        lax.fori_loop(0, STEPS, body, 0)
    y = lax.rem(lax.axis_index("seq"), ROW)
    for o in range(ROW):
        outs[o][...] = stage[lax.rem(y + o, ROW)]


def local_states(lengths, x_in, dt_raw, bc_in, rate):
    return pl.pallas_call(
        local_kernel,
        out_shape=[jax.ShapeDtypeStruct((STATE_ROWS + NS, LANE), BF16)] * ROW,
        in_specs=[SM, ANY, VM, VM, VM],
        out_specs=[VM] * ROW,
        scratch_shapes=[
            pltpu.VMEM((ROW, STATE_ROWS + NS, LANE), BF16),
            pltpu.VMEM((2, HEADS, BLK), F32),
            pltpu.VMEM((2, NS, BLK), F32),
            pltpu.VMEM((2, BLK, WIDTH), BF16),
            pltpu.SemaphoreType.DMA((2 * STEPS,)),
        ],
        cost_estimate=cost(6),
        compiler_params=params(),
        name="local_states",
    )(lengths, x_in, dt_raw, bc_in, rate)


def place(arrays, scratch, me):
    for o in range(ROW):
        scratch[lax.rem(me + ROW - o, ROW)] = arrays[o][...]


def spread_decays(blocks, y):
    rows = lax.broadcasted_iota(jnp.int32, (HEADS, PARTS * LANE), 0)
    cols = lax.broadcasted_iota(jnp.int32, (HEADS, PARTS * LANE), 1)
    pick = jnp.where(rows == y * (PARTS * 2) + (cols >> 6), 1.0, 0.0).astype(BF16)
    return jnp.dot(jnp.concatenate(blocks, axis=0), pick, preferred_element_type=F32)


def decay_of(wide, block, p, c):
    cols = slice(c * LANE, (c + 1) * LANE)
    return wide[block * NS + p : block * NS + p + 1, cols] + wide[block * NS + 2 + p : block * NS + 3 + p, cols]


def groups():
    return [(p, c, (p * PARTS + c) * NS) for p in range(2) for c in range(PARTS)]


def row_kernel(*refs):
    ins, out, scr = refs[:ROW], refs[ROW], refs[ROW + 1]
    y = lax.rem(lax.axis_index("seq"), ROW)
    place(ins, scr, y)
    wide = spread_decays([scr[b, STATE_ROWS:, :] for b in range(ROW)], y)
    for p, c, at in groups():
        state = jnp.zeros((NS, LANE), F32)
        for b in range(ROW):
            half = decay_of(wide, b, p, c)
            state = half * (half * state + scr[b, at : at + NS, :].astype(F32))
        out[at : at + NS, :] = state.astype(BF16)
    compact = [scr[b, STATE_ROWS:, :].astype(F32) for b in range(ROW)]
    row = lax.broadcasted_iota(jnp.int32, (NS, LANE), 0)
    dec = jnp.zeros((NS, LANE), F32)
    for p in range(2):
        all_rows = jnp.ones((1, LANE), F32)
        for b in range(ROW):
            half = compact[b][p : p + 1, :] + compact[b][2 + p : 3 + p, :]
            all_rows = all_rows * (half * half)
        high, low = halves(all_rows)
        dec = jnp.where(row == p, high.astype(F32), jnp.where(row == 2 + p, low.astype(F32), dec))
    out[STATE_ROWS:, :] = dec.astype(BF16)


def row_totals(blocks):
    return pl.pallas_call(
        row_kernel,
        out_shape=jax.ShapeDtypeStruct((STATE_ROWS + NS, LANE), BF16),
        in_specs=[VM] * ROW,
        out_specs=VM,
        scratch_shapes=[pltpu.VMEM((ROW, STATE_ROWS + NS, LANE), BF16)],
        cost_estimate=cost(1),
        compiler_params=params(),
        name="row_totals",
    )(*blocks)


def enter_kernel(group_ref, *refs):
    blocks, totals, outs = refs[:ROW], refs[ROW : 2 * ROW], refs[2 * ROW : 3 * ROW]
    scr, rows, start, stage = refs[3 * ROW :]
    me = lax.axis_index("seq")
    x, y = lax.div(me, ROW), lax.rem(me, ROW)
    place(blocks, scr, y)
    place(totals, rows, x)
    wide = spread_decays(
        [scr[b, STATE_ROWS:, :] for b in range(ROW)] + [rows[b, STATE_ROWS:, :] for b in range(ROW)], y
    )
    for p, c, at in groups():
        state = jnp.zeros((NS, LANE), F32)
        for b in range(ROW):
            start[b, at : at + NS, :] = state
            state = decay_of(wide, ROW + b, p, c) * state + rows[b, at : at + NS, :].astype(F32)
        start[ROW, at : at + NS, :] = state
    for p, c, at in groups():
        state = start[x, at : at + NS, :]
        for b in range(ROW):
            half = decay_of(wide, b, p, c)
            entering = half * state
            stage[b, at : at + NS, :] = entering.astype(BF16)
            state = half * (entering + scr[b, at : at + NS, :].astype(F32))
    second = group_ref[lax.axis_index("tp") * 2 + 1]
    for b in range(ROW):
        at = jnp.where(second == x * ROW + b, FINAL_ROWS, 0)
        final = start[ROW, pl.ds(pl.multiple_of(at, FINAL_ROWS), FINAL_ROWS), :]
        stage[b, STATE_ROWS:, :] = final.astype(BF16)
    for o in range(ROW):
        outs[o][...] = stage[lax.rem(y + o, ROW)]


def enter_states(group_of, blocks, totals):
    return pl.pallas_call(
        enter_kernel,
        out_shape=[jax.ShapeDtypeStruct((STATE_ROWS + FINAL_ROWS, LANE), BF16)] * ROW,
        in_specs=[SM] + [VM] * (2 * ROW),
        out_specs=[VM] * ROW,
        scratch_shapes=[
            pltpu.VMEM((ROW, STATE_ROWS + NS, LANE), BF16),
            pltpu.VMEM((ROW, STATE_ROWS + NS, LANE), BF16),
            pltpu.VMEM((ROW + 1, STATE_ROWS, LANE), F32),
            pltpu.VMEM((ROW, STATE_ROWS + FINAL_ROWS, LANE), BF16),
        ],
        cost_estimate=cost(2),
        compiler_params=params(),
        name="enter_states",
    )(group_of, *blocks, *totals)


def order_kernel(group_ref, pages, out):
    for r in range(SEQ):
        at = r % 2 * BLK
        out[group_ref[r]] = pages[r // 2, at : at + BLK, :]


def order_pages(group_of, pages):
    return pl.pallas_call(
        order_kernel,
        out_shape=jax.ShapeDtypeStruct((SEQ, BLK, 2 * HD), BF16),
        in_specs=[SM, VM],
        out_specs=VM,
        cost_estimate=cost(2),
        compiler_params=params(),
        name="order_pages",
    )(group_of, pages)


def output_kernel(len_ref, x_hbm, dt_ref, bc_ref, rate_ref, skip_ref, *refs):
    enters, y_hbm, (ebig, both, mix, enter, x_buf, y_buf, sem, out_sem) = refs[:ROW], refs[ROW], refs[ROW + 1 :]
    for c in block_copies(x_hbm, x_buf, sem):
        c.start()
    spread_matrix(ebig)
    y = lax.rem(lax.axis_index("seq"), ROW)
    for o in range(ROW):
        enter[lax.rem(y + ROW - o, ROW)] = enters[o][:STATE_ROWS, :]
    rows = lax.broadcasted_iota(jnp.int32, (BLK, BLK), 0)
    cols = lax.broadcasted_iota(jnp.int32, (BLK, BLK), 1)
    for p in range(2):
        live, step, rel, mid = decays(len_ref, dt_ref, rate_ref, p)
        factors = [jnp.exp(-rel) * step, jnp.exp(rel) * live, jnp.broadcast_to(skip_ref[...] * live, (NS, HEADS))]
        for at, v in zip((0, BLK, 2 * BLK), factors):
            high, low = halves(v)
            both[p, at : at + v.shape[0], :HEADS] = high
            both[p, at : at + v.shape[0], HEADS:] = low
        scores = lax.dot_general(
            bc_ref[p, :, NS:], bc_ref[p, :, :NS], (((1,), (1,)), ((), ())), preferred_element_type=F32
        )
        mix[p] = jnp.where(rows >= cols, scores, 0.0).astype(BF16)
    for p in range(2):

        def body(j, carry):
            block_copy(x_hbm, x_buf, sem, p, j).wait()
            at = pl.ds(pl.multiple_of(j * WC, WC), WC)
            ej = spread_rows(ebig, j)
            x = x_buf[p, :, at].astype(F32)
            factor = jnp.dot(both[p], ej, preferred_element_type=F32)
            xp = (x * factor[:BLK]).astype(BF16)
            first = (p * 2 + lax.rem(j, 2)) * CHUNKS * NS
            entering = enter[lax.div(j, 2), pl.ds(pl.multiple_of(first, CHUNKS * NS), CHUNKS * NS), :]
            entering = jnp.concatenate([entering[i * NS : (i + 1) * NS] for i in range(CHUNKS)], axis=1)
            total = jnp.dot(mix[p], xp, preferred_element_type=F32) + jnp.dot(
                bc_ref[p, :, NS:], entering, preferred_element_type=F32
            )
            y_buf[p, :, at] = (factor[BLK : 2 * BLK] * total + factor[2 * BLK : 2 * BLK + 1] * x).astype(BF16)
            block_copy(y_hbm, y_buf, out_sem, p, j, out=True).start()
            return carry

        lax.fori_loop(0, STEPS, body, 0)
    for c in block_copies(y_hbm, y_buf, out_sem, out=True):
        c.wait()


def block_outputs(lengths, x_in, dt_raw, bc_in, rate, skip, entering):
    return pl.pallas_call(
        output_kernel,
        out_shape=jax.ShapeDtypeStruct((2, BLK, WIDTH), BF16),
        in_specs=[SM, ANY] + [VM] * (4 + ROW),
        out_specs=ANY,
        scratch_shapes=[
            pltpu.VMEM((3 * HEADS, WC), BF16),
            pltpu.VMEM((2, 2 * BLK + NS, 2 * HEADS), BF16),
            pltpu.VMEM((2, BLK, BLK), BF16),
            pltpu.VMEM((ROW, STATE_ROWS, LANE), BF16),
            pltpu.VMEM((2, BLK, WIDTH), BF16),
            pltpu.VMEM((2, BLK, WIDTH), BF16),
            pltpu.SemaphoreType.DMA((2 * STEPS,)),
            pltpu.SemaphoreType.DMA((2 * STEPS,)),
        ],
        cost_estimate=cost(12),
        compiler_params=params(),
        name="block_outputs",
    )(lengths, x_in, dt_raw, bc_in, rate, skip, *entering)


def my_prompt(group_ref):
    mine = lax.axis_index("seq")
    prompt = jnp.int32(0)
    for r in range(SEQ):
        prompt = jnp.where(group_ref[r] == mine, r, prompt)
    return prompt


def attend_kernel(
    group_ref, len_ref, slot_ref, recv, q_ref, fresh, pool, out_ref, zeros, sem
):
    prompt = my_prompt(group_ref)
    length = len_ref[prompt]
    zeros[...] = jnp.zeros(zeros.shape, BF16)

    def page_copy(s, live):
        at = pl.ds(pl.multiple_of(slot_ref[prompt, s] * BLK, BLK), BLK)
        source = recv.at[s] if live else zeros
        return pltpu.make_async_copy(source, pool.at[0, at, :], sem.at[s])

    for s in range(SEQ):

        @pl.when(length > s * BLK)
        def _():
            page_copy(s, True).start()

        @pl.when(length <= s * BLK)
        def _():
            page_copy(s, False).start()

    q = q_ref[...]
    scale = HD**-0.5
    contract = (((1,), (1,)), ((), ()))
    rows = lax.broadcasted_iota(jnp.int32, (q.shape[0], fresh.shape[0]), 0)
    cols = lax.broadcasted_iota(jnp.int32, (q.shape[0], fresh.shape[0]), 1)
    new = lax.dot_general(q, fresh[:, :HD], contract, preferred_element_type=F32) * scale
    new = jnp.where(cols <= (rows & 3), new, -1e30)
    peak = jnp.max(new, axis=1, keepdims=True)
    old = []
    for s in range(SEQ):
        part = lax.dot_general(q, recv[s, :, :HD], contract, preferred_element_type=F32) * scale
        part = jnp.where(length > s * BLK, part, -1e30)
        old.append(part)
        peak = jnp.maximum(peak, jnp.max(part, axis=1, keepdims=True))
    prob = jnp.exp(new - peak)
    total = jnp.sum(prob, axis=1, keepdims=True)
    mixed = jnp.dot(prob.astype(BF16), fresh[:, HD:], preferred_element_type=F32)
    for s in range(SEQ):
        prob = jnp.exp(old[s] - peak)
        total = total + jnp.sum(prob, axis=1, keepdims=True)
        mixed = mixed + jnp.dot(prob.astype(BF16), recv[s, :, HD:], preferred_element_type=F32)
    result = mixed / total
    steps = out_ref.shape[1]
    for h in range(q.shape[0] // steps):
        out_ref[0, :, h * HD : (h + 1) * HD] = result[h * steps : (h + 1) * steps].astype(BF16)
    for s in range(SEQ):
        page_copy(s, True).wait()


def attend(group_of, lengths, slot_of, recv, queries, fresh):
    return pl.pallas_call(
        attend_kernel,
        out_shape=[
            jax.ShapeDtypeStruct((1, SEQ * BLK, 2 * HD), BF16),
            jax.ShapeDtypeStruct((1, 4, WC), BF16),
        ],
        in_specs=[SM, SM, SM, VM, VM, VM],
        out_specs=[ANY, VM],
        scratch_shapes=[pltpu.VMEM((BLK, 2 * HD), BF16), pltpu.SemaphoreType.DMA((SEQ,))],
        cost_estimate=cost(5),
        compiler_params=params(),
        name="attend",
    )(group_of, lengths, slot_of, recv, queries, fresh)


def decode_kernel(inputs, bct_ref, rate_ref, skip_ref, *refs):
    finals, outs, (fin, res) = refs[:ROW], refs[ROW : ROW + TP], refs[ROW + TP :]
    me = lax.axis_index("tp")
    y = lax.rem(lax.axis_index("seq"), ROW)
    for o in range(ROW):
        fin[lax.rem(y + ROW - o, ROW)] = finals[o][STATE_ROWS:, :]
    heads = WC // HP
    rows = lax.broadcasted_iota(jnp.int32, (heads, WC), 0)
    cols = lax.broadcasted_iota(jnp.int32, (heads, WC), 1)
    spread = jnp.where(rows == (cols >> 6), 1.0, 0.0).astype(F32)
    raw = [inputs[t, DEC_T : DEC_T + 16, :].astype(F32)[:4, :heads] for t in range(TP)]
    step = softplus(jnp.concatenate(raw, axis=0))
    rates = jnp.concatenate([jnp.broadcast_to(rate_ref[t : t + 1], (4, heads)) for t in range(TP)], axis=0)
    small = jnp.concatenate([step, jnp.exp(-step * rates), skip_ref[...]], axis=0)
    wide = jnp.dot(small, spread, precision=highest, preferred_element_type=F32)

    def unfold(rows):
        return jnp.concatenate([rows[q * 4 : (q + 1) * 4] for q in range(4)], axis=1)

    sums = [jnp.zeros((1, 1), F32)] * 4
    for t in range(TP):
        x = unfold(inputs[t, DEC_X : DEC_X + 16, :].astype(F32))
        z = unfold(inputs[t, DEC_Z : DEC_Z + 16, :].astype(F32))
        gate = z / (1.0 + jnp.exp(-z))
        chunks = [t * CHUNKS + i for i in range(CHUNKS)]
        state = jnp.concatenate(
            [fin[k // PARTS, k % PARTS * NS : (k % PARTS + 1) * NS, :].astype(F32) for k in chunks], axis=1
        )
        skip = wide[8 * TP + t : 8 * TP + t + 1]
        for k in range(4):
            b_col = bct_ref[:NS, k : k + 1]
            c_col = bct_ref[NS:, k : k + 1]
            wide_step = wide[4 * t + k : 4 * t + k + 1]
            fade = wide[4 * TP + 4 * t + k : 4 * TP + 4 * t + k + 1]
            state = fade * state + b_col * (wide_step * x[k : k + 1])
            read = jnp.sum(c_col * state, axis=0, keepdims=True) + skip * x[k : k + 1]
            v = read * gate[k : k + 1]
            res[t, NS + k : NS + k + 1, :] = v
            sums[k] = sums[k] + jnp.sum(v * v, axis=1, keepdims=True)
        res[t, :NS, :] = state
    factor = jnp.concatenate([lax.rsqrt(sums[k] / WIDTH + 1e-05) for k in range(4)], axis=0)
    for t in range(TP):
        res[t, NS : NS + 4, :] = res[t, NS : NS + 4, :] * factor
        res[t, NS + 4 :, :] = jnp.zeros((4, WC), F32)
    for o in range(TP):
        outs[o][...] = res[lax.rem(me + o, TP)]


def decode(inputs, bct, rate, skip, finals):
    return pl.pallas_call(
        decode_kernel,
        out_shape=[jax.ShapeDtypeStruct((NS + 8, WC), F32)] * TP,
        in_specs=[VM] * (4 + ROW),
        out_specs=[VM] * TP,
        scratch_shapes=[
            pltpu.VMEM((ROW, FINAL_ROWS, LANE), BF16),
            pltpu.VMEM((TP, NS + 8, WC), F32),
        ],
        cost_estimate=cost(4),
        compiler_params=params(),
        name="decode",
    )(inputs, bct, rate, skip, *finals)


def pick_kernel(group_ref, gain_ref, *refs):
    results, (state_ref, out_ref) = refs[:TP], refs[TP:]
    holder = lax.div(my_prompt(group_ref), 2)
    distance = lax.rem(lax.axis_index("tp") + TP - holder, TP)
    for o in range(TP):

        @pl.when(distance == o)
        def _():
            state_ref[0] = results[o][:NS, :]
            out_ref[0] = (results[o][NS : NS + 4, :] * gain_ref[...].astype(F32)).astype(BF16)


def pick(group_of, gain, results):
    return pl.pallas_call(
        pick_kernel,
        out_shape=[
            jax.ShapeDtypeStruct((1, NS, WC), F32),
            jax.ShapeDtypeStruct((1, 4, WC), BF16),
        ],
        in_specs=[SM] + [VM] * (1 + TP),
        out_specs=[VM] * 2,
        cost_estimate=cost(1),
        compiler_params=params(),
        name="pick",
    )(group_of, gain, *results)


def rotate(arrays):
    return [arrays[0]] + [
        lax.ppermute(arrays[o], "tp", [(i, (i + o) % TP) for i in range(TP)]) for o in range(1, TP)
    ]


def along_y(arrays):
    moves = [[(x * ROW + y, x * ROW + (y + o) % ROW) for x in range(ROW) for y in range(ROW)] for o in range(ROW)]
    return [arrays[0]] + [lax.ppermute(arrays[o], "seq", moves[o]) for o in range(1, ROW)]


def along_x(arrays):
    moves = [[(i, (i + o * ROW) % SEQ) for i in range(SEQ)] for o in range(ROW)]
    return [arrays[0]] + [lax.ppermute(arrays[o], "seq", moves[o]) for o in range(1, ROW)]


def shards(
    x_in, dt_raw, bc_in, decay_rate, skip_gain, kv_pre, lengths, group_of, slot_of,
    dec_x, dec_dt, dec_bc, dec_z, norm_gain, dec_q, dec_kv,
):
    rate = decay_rate.reshape(1, HEADS)
    skip = skip_gain.reshape(1, HEADS)
    bct = jnp.transpose(dec_bc[0].astype(F32))
    queries = jnp.transpose(dec_q.reshape(4, -1, HD), (1, 0, 2)).reshape(-1, HD)
    fresh = jnp.concatenate([dec_kv[0], jnp.zeros((12, 2 * HD), BF16)], axis=0)
    gain = norm_gain.reshape(1, -1)

    sent, token = split_heads(kv_pre, dec_x, dec_z, dec_dt)
    pages = lax.all_to_all(sent, "tp", split_axis=0, concat_axis=0, tiled=True)
    early_lengths, token = lax.optimization_barrier((lengths, token))
    blocks = along_y(local_states(early_lengths, x_in, dt_raw, bc_in, rate))
    totals = along_x([row_totals(blocks)] * ROW)
    pages, totals = lax.optimization_barrier((pages, totals))
    entering = along_y(enter_states(group_of, blocks, totals))
    recv = lax.all_to_all(order_pages(group_of, pages), "seq", split_axis=0, concat_axis=0, tiled=True)
    results = decode(pages, bct, decay_rate.reshape(TP, -1), skip_gain.reshape(TP, -1), entering)
    dec_state, dec_mamba = pick(group_of, gain, rotate(results))
    y_pre = block_outputs(lengths, x_in, dt_raw, bc_in, rate, skip, entering)
    kv_pool, dec_attn = attend(group_of, lengths, slot_of, recv, queries, fresh)
    return (y_pre, kv_pool, dec_mamba, dec_state, dec_attn)


def solution(mesh):
    return jax.shard_map(
        shards,
        mesh=mesh,
        in_specs=(
            P("tp", "seq", None),
            P("tp", "seq", None),
            P("tp", "seq", None),
            P(),
            P(),
            P("tp", "seq", None),
            P(),
            P(),
            P(),
            P("seq", None, "tp"),
            P("seq", None, "tp"),
            P("seq", None, None),
            P("seq", None, "tp"),
            P("tp"),
            P("seq", None, "tp"),
            P("seq", None, "tp"),
        ),
        out_specs=(
            P("tp", "seq", None),
            P("seq", None, "tp"),
            P("seq", None, "tp"),
            P("seq", None, "tp"),
            P("seq", None, "tp"),
        ),
        check_vma=False,
    )
```

time: 500 us -> 119 us (0.24)
  local copies, waits for them, and re-layouts: 167 us -> 10.8 us
  waiting for transfers between devices: 108 us -> 36.5 us
  other arithmetic: 70.3 us -> 0.01 us
  blocking collectives: 62.2 us -> 0 us
  matrix products: 51.4 us -> 0 us
  Pallas kernels: 0 us -> 32.1 us
  starting transfers between devices: 17.4 us -> 35.9 us
  between operations: 19 us -> 1.04 us
    psum x1 -> x0, waiting for transfers between devices: 77.3 us -> none  [broadcast(): return lax.psum(jnp.where(mine, value, jnp.zeros_like(value)), axis)]
    select_n x24 -> x0, other arithmetic: 57.1 us -> none  [the longest x15 49.4 us: step(): jnp.where(position < mine, new, old)]
    dot_general x15 -> x0, matrix products: 51.4 us -> none  [the longest x2 22.5 us: block_output(): jnp.einsum('hts,shp->thp', weights, x_heads, preferred_element_type=jnp.f...]
    all_gather x1 -> x0, blocking collectives: 46.2 us -> none  [prefix(): pieces = jax.tree.map(lambda part: lax.all_gather(part, axis), value)]
    ppermute x0 -> x16, waiting for transfers between devices: none -> 36.5 us  [the longest x6 29.4 us: along_y(): lax.ppermute(arrays[o], 'seq', moves[o])]
    dynamic_slice x39 -> x0, local copies, waits for them, and re-layouts: 34.3 us -> none  [the longest x30 28.5 us: step(): longer = join(total, jax.tree.map(lambda part: part[position], pieces))]
    pallas_call x0 -> x9, Pallas kernels: none -> 32.1 us  [the longest x1 15.1 us: block_outputs(): pl.pallas_call(output_kernel, out_shape=jax.ShapeDtypeStruct((2, BLK, WID...]
    all_to_all x3 -> x2, waiting for transfers between devices: 24.6 us -> 0.01 us  [the longest x1 0.01 us: shards(): pages = lax.all_to_all(sent, 'tp', split_axis=0, concat_axis=0, tiled=True)]
  transfers between devices with their start and end apart: 5 -> 18, of which waited for: 3 -> 8; matrix products, arithmetic and copies ran while one was open for 25% -> 0% of each run, Pallas kernels for 0% -> 22%
where the time goes in v1:
time: 119 us; the launch traced here: 116 us
  waiting for transfers between devices  36.5 us (31%)
  starting transfers between devices  35.9 us (30%)
  Pallas kernels  32.1 us (27%)
  local copies, waits for them, and re-layouts  10.8 us (9%)
    ppermute x6, waiting for transfers between devices, along_y(): lax.ppermute(arrays[o], 'seq', moves[o])  29.4 us
    pallas_call x1, Pallas kernels, block_outputs(): pl.pallas_call(output_kernel, out_shape=jax.ShapeDtypeStruct((2, BLK, WID...  15.1 us
    ppermute x6, starting transfers between devices, along_y(): lax.ppermute(arrays[o], 'seq', moves[o])  11.9 us
    unnamed x47, local copies, waits for them, and re-layouts  10.5 us
    ppermute x7, starting transfers between devices, rotate(): lax.ppermute(arrays[o], 'tp', [(i, (i + o) % TP) for i in range(TP)])  7.45 us
    ppermute x3, waiting for transfers between devices, along_x(): lax.ppermute(arrays[o], 'seq', moves[o])  6.98 us
    all_to_all x1, starting transfers between devices, shards(): lax.all_to_all(order_pages(group_of, pages), 'seq', split_axis=0, concat_...  6.53 us
    all_to_all x1, starting transfers between devices, shards(): pages = lax.all_to_all(sent, 'tp', split_axis=0, concat_axis=0, tiled=True)  5.54 us
  transfers between devices with their start and end apart: 18, of which 8 were waited for; matrix products, arithmetic and copies ran while one was open for 0% of the time, Pallas kernels for 22%

profile of v1, /device:TPU:0, one launch (start us, length us, event | category | flops | bytes accessed | tf_op | source)
XLA Modules:
  0.0 116.4 jit_solution(7067092035362151610)
XLA Ops:
  0.6 1.6 %copy-done.2 = bf16[2,256,2048]{2,1,0:T(8,128)(2,1)S(1)} copy-done((bf16[2,256,2048]{2,1,0:T(8,128)(2,1)S(1)}, bf16[2,256,2048]{2,1,0:T(8,128)(2,1)}, u32[]{:S(2)}) %copy-start.2) | copy-done | bytes 2097176
  2.2 0.7 copy-done.10
  2.9 0.7 copy-done.11
  3.6 0.7 copy-done.18
  4.3 1.1 split_heads.1
  5.5 1.4 %copy-done.1 = bf16[8,560,256]{2,1,0:T(8,128)(2,1)} copy-done((bf16[8,560,256]{2,1,0:T(8,128)(2,1)}, bf16[8,560,256]{2,1,0:T(8,128)(2,1)S(1)}, u32[]{:S(2)}) %copy-start.1) | copy-done | bytes 2293784
  6.8 5.5 %all-to-all-start = ((bf16[8,560,256]{2,1,0:T(8,128)(2,1)}), bf16[8,560,256]{2,1,0:T(8,128)(2,1)S(1)}, u32[]{:S(2)}, u32[]{:S(2)}) async-start(bf16[8,560,256]{2,1,0:T(8,128)(2,1)} %copy-done.1), calls=%async_computation | async-start | bytes 4587520 | tf_op jit(solution)/shard_map/all_to_all | solution.py:577
  12.4 0.1 copy.22.bc_ref
  12.6 5.3 %local_states.1 = (bf16[528,128]{1,0:T(8,128)(2,1)S(1)}, bf16[528,128]{1,0:T(8,128)(2,1)S(1)}, bf16[528,128]{1,0:T(8,128)(2,1)S(1)}, bf16[528,128]{1,0:T(8,128)(2,1)S(1)}) custom-call(s32[16]{0:T(128)S(1)} %copy-done.16, bf16[2,256,8192]{2,1,0:T(8,128)(2,1)} %x_hbm.3, bf16[2,256,128]{2,1,0:T(8,128)(2,1)S(1)} %copy-done.3, ...), custom_call_target="tpu_custom_call" | custom-call | bytes 18000000 | tf_op jit(solution)/shard_map/local_states/pallas_call | solution.py:172
  17.8 1.6 %collective-permute-start = (bf16[528,128]{1,0:T(8,128)(2,1)S(1)}, bf16[528,128]{1,0:T(8,128)(2,1)S(1)}, u32[]{:S(2)}, u32[]{:S(2)}) collective-permute-start(bf16[528,128]{1,0:T(8,128)(2,1)S(1)} %get-tuple-element.32), channel_id=1, source_target_pairs={{0,8},{8,16},{16,24},{24,0},{32,40},{40,48},{48,56},{56,32},{64,72... | collective-permute-start | bytes 405512 | tf_op jit(solution)/shard_map/ppermute | solution.py:557
  19.5 2.9 %collective-permute-start.1 = (bf16[528,128]{1,0:T(8,128)(2,1)S(1)}, bf16[528,128]{1,0:T(8,128)(2,1)S(1)}, u32[]{:S(2)}, u32[]{:S(2)}) collective-permute-start(bf16[528,128]{1,0:T(8,128)(2,1)S(1)} %get-tuple-element.33), channel_id=1, source_target_pairs={{0,16},{8,24},{16,0},{24,8},{32,48},{40,56},{48,32},{56,40},{64,80... | collective-permute-start | bytes 405512 | tf_op jit(solution)/shard_map/ppermute | solution.py:557
  22.4 1.3 %collective-permute-start.2 = (bf16[528,128]{1,0:T(8,128)(2,1)S(1)}, bf16[528,128]{1,0:T(8,128)(2,1)S(1)}, u32[]{:S(2)}, u32[]{:S(2)}) collective-permute-start(bf16[528,128]{1,0:T(8,128)(2,1)S(1)} %get-tuple-element.34), channel_id=1, source_target_pairs={{0,24},{8,0},{16,8},{24,16},{32,56},{40,32},{48,40},{56,48},{64,88... | collective-permute-start | bytes 405512 | tf_op jit(solution)/shard_map/ppermute | solution.py:557
  23.7 1.4 %collective-permute-done.refs_1_ = bf16[528,128]{1,0:T(8,128)(2,1)S(1)} collective-permute-done((bf16[528,128]{1,0:T(8,128)(2,1)S(1)}, bf16[528,128]{1,0:T(8,128)(2,1)S(1)}, u32[]{:S(2)}, u32[]{:S(2)}) %collective-permute-start) | collective-permute-done | bytes 135200 | tf_op jit(solution)/shard_map/ppermute | solution.py:557
  25.2 4.1 %collective-permute-done.1.refs_2_ = bf16[528,128]{1,0:T(8,128)(2,1)S(1)} collective-permute-done((bf16[528,128]{1,0:T(8,128)(2,1)S(1)}, bf16[528,128]{1,0:T(8,128)(2,1)S(1)}, u32[]{:S(2)}, u32[]{:S(2)}) %collective-permute-start.1) | collective-permute-done | bytes 135200 | tf_op jit(solution)/shard_map/ppermute | solution.py:557
  29.2 0.3 row_totals.1.refs_4_
  29.6 2.8 %collective-permute-start.5 = (bf16[528,128]{1,0:T(8,128)(2,1)S(1)}, bf16[528,128]{1,0:T(8,128)(2,1)S(1)}, u32[]{:S(2)}, u32[]{:S(2)}) collective-permute-start(bf16[528,128]{1,0:T(8,128)(2,1)S(1)} %row_totals.1.refs_4_), channel_id=1, source_target_pairs={{0,96},{8,104},{16,112},{24,120},{32,0},{40,8},{48,16},{56,24},{64... | collective-permute-start | bytes 405512 | tf_op jit(solution)/shard_map/ppermute | solution.py:562
  32.4 0.8 collective-permute-start.4
  33.2 0.9 collective-permute-start.3
  34.1 3.9 %collective-permute-done.5.refs_7_ = bf16[528,128]{1,0:T(8,128)(2,1)S(1)} collective-permute-done((bf16[528,128]{1,0:T(8,128)(2,1)S(1)}, bf16[528,128]{1,0:T(8,128)(2,1)S(1)}, u32[]{:S(2)}, u32[]{:S(2)}) %collective-permute-start.5) | collective-permute-done | bytes 135200 | tf_op jit(solution)/shard_map/ppermute | solution.py:562
  38.0 2.3 %collective-permute-done.4.refs_6_ = bf16[528,128]{1,0:T(8,128)(2,1)S(1)} collective-permute-done((bf16[528,128]{1,0:T(8,128)(2,1)S(1)}, bf16[528,128]{1,0:T(8,128)(2,1)S(1)}, u32[]{:S(2)}, u32[]{:S(2)}) %collective-permute-start.4) | collective-permute-done | bytes 135200 | tf_op jit(solution)/shard_map/ppermute | solution.py:562
  40.3 0.7 copy-done.6
  41.0 0.8 collective-permute-done.3.refs_5_
  41.7 0.6 copy-done.8
  42.4 0.7 order_pages.1
  43.1 1.3 %copy-done = bf16[16,256,256]{2,1,0:T(8,128)(2,1)} copy-done((bf16[16,256,256]{2,1,0:T(8,128)(2,1)}, bf16[16,256,256]{2,1,0:T(8,128)(2,1)S(1)}, u32[]{:S(2)}) %copy-start) | copy-done | bytes 2097176
  44.4 6.5 %all-to-all-start.1 = ((bf16[16,256,256]{2,1,0:T(8,128)(2,1)}), bf16[16,256,256]{2,1,0:T(8,128)(2,1)}, u32[]{:S(2)}, u32[]{:S(2)}) async-start(bf16[16,256,256]{2,1,0:T(8,128)(2,1)} %copy-done), calls=%async_computation.1 | async-start | bytes 4194304 | tf_op jit(solution)/shard_map/all_to_all | solution.py:583
  51.0 0.1 reshape.38.rate_ref
  51.1 0.9 copy-done.5
  52.0 0.9 copy-done.7
  53.0 0.9 copy-done.9
  53.9 2.2 %enter_states.1 = (bf16[768,128]{1,0:T(8,128)(2,1)S(1)}, bf16[768,128]{1,0:T(8,128)(2,1)}, bf16[768,128]{1,0:T(8,128)(2,1)}, bf16[768,128]{1,0:T(8,128)(2,1)}) custom-call(s32[16]{0:T(128)S(1)} %copy-done.14, bf16[528,128]{1,0:T(8,128)(2,1)S(1)} %get-tuple-element.31.refs_0_, bf16[528,128]{1,0:T(8,128)(2,1)S(1)} %collective-permute-done.refs_1_, ...), custom_call_target="tpu_custom_call" | custom-call | bytes 6000000 | tf_op jit(solution)/shard_map/enter_states/pallas_call | solution.py:281
  56.0 1.9 %collective-permute-start.6 = (bf16[768,128]{1,0:T(8,128)(2,1)}, bf16[768,128]{1,0:T(8,128)(2,1)S(1)}, u32[]{:S(2)}, u32[]{:S(2)}) collective-permute-start(bf16[768,128]{1,0:T(8,128)(2,1)} %get-tuple-element.41), channel_id=1, source_target_pairs={{0,8},{8,16},{16,24},{24,0},{32,40},{40,48},{48,56},{56,32},{64,72... | collective-permute-start | bytes 589832 | tf_op jit(solution)/shard_map/ppermute | solution.py:557
  57.9 2.7 %collective-permute-start.7 = (bf16[768,128]{1,0:T(8,128)(2,1)}, bf16[768,128]{1,0:T(8,128)(2,1)S(1)}, u32[]{:S(2)}, u32[]{:S(2)}) collective-permute-start(bf16[768,128]{1,0:T(8,128)(2,1)} %get-tuple-element.42), channel_id=1, source_target_pairs={{0,16},{8,24},{16,0},{24,8},{32,48},{40,56},{48,32},{56,40},{64,80... | collective-permute-start | bytes 589832 | tf_op jit(solution)/shard_map/ppermute | solution.py:557
  60.6 1.5 %collective-permute-start.8 = (bf16[768,128]{1,0:T(8,128)(2,1)}, bf16[768,128]{1,0:T(8,128)(2,1)S(1)}, u32[]{:S(2)}, u32[]{:S(2)}) collective-permute-start(bf16[768,128]{1,0:T(8,128)(2,1)} %get-tuple-element.43), channel_id=1, source_target_pairs={{0,24},{8,0},{16,8},{24,16},{32,56},{40,32},{48,40},{56,48},{64,88... | collective-permute-start | bytes 589832 | tf_op jit(solution)/shard_map/ppermute | solution.py:557
  62.0 0.1 copy.24
  62.1 19.2 %collective-permute-done.6.refs_1_ = bf16[768,128]{1,0:T(8,128)(2,1)S(1)} collective-permute-done((bf16[768,128]{1,0:T(8,128)(2,1)}, bf16[768,128]{1,0:T(8,128)(2,1)S(1)}, u32[]{:S(2)}, u32[]{:S(2)}) %collective-permute-start.6) | collective-permute-done | bytes 196640 | tf_op jit(solution)/shard_map/ppermute | solution.py:557
  81.3 4.7 %collective-permute-done.7.refs_2_ = bf16[768,128]{1,0:T(8,128)(2,1)S(1)} collective-permute-done((bf16[768,128]{1,0:T(8,128)(2,1)}, bf16[768,128]{1,0:T(8,128)(2,1)S(1)}, u32[]{:S(2)}, u32[]{:S(2)}) %collective-permute-start.7) | collective-permute-done | bytes 196640 | tf_op jit(solution)/shard_map/ppermute | solution.py:557
  86.0 1.8 %decode.1 = (f32[24,1024]{1,0:T(8,128)S(1)}, f32[24,1024]{1,0:T(8,128)S(1)}, f32[24,1024]{1,0:T(8,128)S(1)}, f32[24,1024]{1,0:T(8,128)S(1)}, f32[24,1024]{1,0:T(...) custom-call(bf16[8,560,256]{2,1,0:T(8,128)(2,1)S(1)} %all-to-all-done.pages.inputs, ...), custom_call_target="tpu_custom_call" | custom-call | bytes 12000000 | tf_op jit(solution)/shard_map/decode/pallas_call | solution.py:507
  87.8 0.6 collective-permute-start.10
  88.5 1.4 %collective-permute-start.11 = (f32[24,1024]{1,0:T(8,128)S(1)}, f32[24,1024]{1,0:T(8,128)S(1)}, u32[]{:S(2)}, u32[]{:S(2)}) collective-permute-start(f32[24,1024]{1,0:T(8,128)S(1)} %get-tuple-element.49), channel_id=1, source_target_pairs={{0,3},{1,4},{2,5},{3,6},{4,7},{5,0},{6,1},{7,2},{8,11},{9,12},{10,... | collective-permute-start | bytes 294920 | tf_op jit(solution)/shard_map/ppermute | solution.py:551
  89.8 2.7 %collective-permute-start.12 = (f32[24,1024]{1,0:T(8,128)S(1)}, f32[24,1024]{1,0:T(8,128)S(1)}, u32[]{:S(2)}, u32[]{:S(2)}) collective-permute-start(f32[24,1024]{1,0:T(8,128)S(1)} %get-tuple-element.50), channel_id=1, source_target_pairs={{0,4},{1,5},{2,6},{3,7},{4,0},{5,1},{6,2},{7,3},{8,12},{9,13},{10,... | collective-permute-start | bytes 294920 | tf_op jit(solution)/shard_map/ppermute | solution.py:551
  92.5 1.0 collective-permute-start.13
  93.5 1.1 collective-permute-start.14
  94.6 0.1 collective-permute-done.10.refs_2_
  94.7 0.7 collective-permute-start.15
  95.4 15.1 %block_outputs.1 = bf16[2,256,8192]{2,1,0:T(8,128)(2,1)} custom-call(s32[16]{0:T(128)S(1)} %copy-done.16, bf16[2,256,8192]{2,1,0:T(8,128)(2,1)} %x_hbm.3, bf16[2,256,128]{2,1,0:T(8,128)(2,1)S(1)} %copy-done.3, bf16[2,256,32]{2,1,0:T(8,128)(2,1)S(1)} %copy.22.bc_ref, f32[1,128]{1,0:T(1,128)S(1)} %bitcast.15, f32[1,128]{1,0:T(1,128)S(1)} %bitcast.16, ...), custom_call_target="tpu_custom_call" | custom-call | bytes 36000000 | tf_op jit(solution)/shard_map/block_outputs/pallas_call | solution.py:362
  110.6 1.2 %pick.1 = (f32[1,16,1024]{2,1,0:T(8,128)}, bf16[1,4,1024]{2,1,0:T(4,128)(2,1)}) custom-call(s32[16]{0:T(128)S(1)} %copy-done.14, bf16[1,1024]{1,0:T(2,128)(2,1)S(1)} %reshape.37.gain_ref, f32[24,1024]{1,0:T(8,128)S(1)} %get-tuple-element.46.refs_0_, f32[24,1024]{1,0:T(8,128)S(1)} %collective-permute-done.9.refs_1_, ...), custom_call_target="tpu_custom_call" | custom-call | bytes 3000000 | tf_op jit(solution)/shard_map/pick/pallas_call | solution.py:535
  111.9 4.3 %attend.1 = (bf16[1,4096,256]{2,1,0:T(8,128)(2,1)}, bf16[1,4,1024]{2,1,0:T(4,128)(2,1)}) custom-call(s32[16]{0:T(128)S(1)} %copy-done.14, s32[16]{0:T(128)S(1)} %copy-done.16, s32[16,16]{1,0:T(8,128)S(1)} %copy-done.12, bf16[16,256,256]{2,1,0:T(8,128)(2,1)} %all-to-all-done.1.recv, bf16[32,128]{1,0:T(8,128)(2,1)S(1)} %bitcast.13, ...), custom_call_target="tpu_custom_call" | custom-call | bytes 15000000 | tf_op jit(solution)/shard_map/attend/pallas_call | solution.py:443
  (50 shorter events, 0.2 us)
Async XLA Ops:
  0.6 1.6 %copy-start.2 = (bf16[2,256,2048]{2,1,0:T(8,128)(2,1)S(1)}, bf16[2,256,2048]{2,1,0:T(8,128)(2,1)}, u32[]{:S(2)}) copy-start(bf16[2,256,2048]{2,1,0:T(8,128)(2,1)} %kv_ref.1) | copy-start | bytes 6291460
  2.2 0.7 copy-start.10
  2.9 0.7 copy-start.11
  3.6 0.7 copy-start.18
  5.5 1.4 %copy-start.1 = (bf16[8,560,256]{2,1,0:T(8,128)(2,1)}, bf16[8,560,256]{2,1,0:T(8,128)(2,1)S(1)}, u32[]{:S(2)}) copy-start(bf16[8,560,256]{2,1,0:T(8,128)(2,1)S(1)} %get-tuple-element.35) | copy-start | bytes 6881284
  6.8 5.6 %copy-start.19 = (bf16[2,256,32]{1,2,0:T(8,128)(2,1)S(1)}, bf16[2,256,32]{1,2,0:T(8,128)(2,1)}, u32[]{:S(2)}) copy-start(bf16[2,256,32]{1,2,0:T(8,128)(2,1)} %param.18) | copy-start | bytes 98308
  6.8 5.7 %copy-start.3 = (bf16[2,256,128]{2,1,0:T(8,128)(2,1)S(1)}, bf16[2,256,128]{2,1,0:T(8,128)(2,1)}, u32[]{:S(2)}) copy-start(bf16[2,256,128]{2,1,0:T(8,128)(2,1)} %dt_ref.5) | copy-start | bytes 393220
  6.8 5.7 %copy-start.15 = (f32[128]{0:T(128)S(1)}, f32[128]{0:T(128)}, u32[]{:S(2)}) copy-start(f32[128]{0:T(128)} %param.19) | copy-start | bytes 1540
  6.8 5.7 %copy-start.16 = (s32[16]{0:T(128)S(1)}, s32[16]{0:T(128)}, u32[]{:S(2)}) copy-start(s32[16]{0:T(128)} %len_ref.4) | copy-start | bytes 196
  6.8 35.5 %all-to-all-start = ((bf16[8,560,256]{2,1,0:T(8,128)(2,1)}), bf16[8,560,256]{2,1,0:T(8,128)(2,1)S(1)}, u32[]{:S(2)}, u32[]{:S(2)}) async-start(bf16[8,560,256]{2,1,0:T(8,128)(2,1)} %copy-done.1), calls=%async_computation | async-start | bytes 4587520 | tf_op jit(solution)/shard_map/all_to_all | solution.py:577
  12.6 29.8 %copy-start.14 = (s32[16]{0:T(128)S(1)}, s32[16]{0:T(128)}, u32[]{:S(2)}) copy-start(s32[16]{0:T(128)} %group_ref.7) | copy-start | bytes 196
  17.8 7.3 %collective-permute-start = (bf16[528,128]{1,0:T(8,128)(2,1)S(1)}, bf16[528,128]{1,0:T(8,128)(2,1)S(1)}, u32[]{:S(2)}, u32[]{:S(2)}) collective-permute-start(bf16[528,128]{1,0:T(8,128)(2,1)S(1)} %get-tuple-element.32), channel_id=1, source_target_pairs={{0,8},{8,16},{16,24},{24,0},{32,40},{40,48},{48,56},{56,32},{64,72... | collective-permute-start | bytes 405512 | tf_op jit(solution)/shard_map/ppermute | solution.py:557
  19.5 9.8 %collective-permute-start.1 = (bf16[528,128]{1,0:T(8,128)(2,1)S(1)}, bf16[528,128]{1,0:T(8,128)(2,1)S(1)}, u32[]{:S(2)}, u32[]{:S(2)}) collective-permute-start(bf16[528,128]{1,0:T(8,128)(2,1)S(1)} %get-tuple-element.33), channel_id=1, source_target_pairs={{0,16},{8,24},{16,0},{24,8},{32,48},{40,56},{48,32},{56,40},{64,80... | collective-permute-start | bytes 405512 | tf_op jit(solution)/shard_map/ppermute | solution.py:557
  22.4 6.9 %collective-permute-start.2 = (bf16[528,128]{1,0:T(8,128)(2,1)S(1)}, bf16[528,128]{1,0:T(8,128)(2,1)S(1)}, u32[]{:S(2)}, u32[]{:S(2)}) collective-permute-start(bf16[528,128]{1,0:T(8,128)(2,1)S(1)} %get-tuple-element.34), channel_id=1, source_target_pairs={{0,24},{8,0},{16,8},{24,16},{32,56},{40,32},{48,40},{56,48},{64,88... | collective-permute-start | bytes 405512 | tf_op jit(solution)/shard_map/ppermute | solution.py:557
  29.6 8.5 %collective-permute-start.5 = (bf16[528,128]{1,0:T(8,128)(2,1)S(1)}, bf16[528,128]{1,0:T(8,128)(2,1)S(1)}, u32[]{:S(2)}, u32[]{:S(2)}) collective-permute-start(bf16[528,128]{1,0:T(8,128)(2,1)S(1)} %row_totals.1.refs_4_), channel_id=1, source_target_pairs={{0,96},{8,104},{16,112},{24,120},{32,0},{40,8},{48,16},{56,24},{64... | collective-permute-start | bytes 405512 | tf_op jit(solution)/shard_map/ppermute | solution.py:562
  32.4 7.9 %collective-permute-start.4 = (bf16[528,128]{1,0:T(8,128)(2,1)S(1)}, bf16[528,128]{1,0:T(8,128)(2,1)S(1)}, u32[]{:S(2)}, u32[]{:S(2)}) collective-permute-start(bf16[528,128]{1,0:T(8,128)(2,1)S(1)} %row_totals.1.refs_4_), channel_id=1, source_target_pairs={{0,64},{8,72},{16,80},{24,88},{32,96},{40,104},{48,112},{56,120},{... | collective-permute-start | bytes 405512 | tf_op jit(solution)/shard_map/ppermute | solution.py:562
  33.2 8.5 %collective-permute-start.3 = (bf16[528,128]{1,0:T(8,128)(2,1)S(1)}, bf16[528,128]{1,0:T(8,128)(2,1)S(1)}, u32[]{:S(2)}, u32[]{:S(2)}) collective-permute-start(bf16[528,128]{1,0:T(8,128)(2,1)S(1)} %row_totals.1.refs_4_), channel_id=1, source_target_pairs={{0,32},{8,40},{16,48},{24,56},{32,64},{40,72},{48,80},{56,88},{64,... | collective-permute-start | bytes 405512 | tf_op jit(solution)/shard_map/ppermute | solution.py:562
  38.0 6.4 %copy-start.4 = (bf16[528,128]{1,0:T(8,128)(2,1)}, bf16[528,128]{1,0:T(8,128)(2,1)S(1)}, u32[]{:S(2)}) copy-start(bf16[528,128]{1,0:T(8,128)(2,1)S(1)} %collective-permute-done.5.refs_7_) | copy-start | bytes 405508
  40.3 0.7 copy-start.6
  41.7 0.6 copy-start.8
  43.1 1.3 %copy-start = (bf16[16,256,256]{2,1,0:T(8,128)(2,1)}, bf16[16,256,256]{2,1,0:T(8,128)(2,1)S(1)}, u32[]{:S(2)}) copy-start(bf16[16,256,256]{2,1,0:T(8,128)(2,1)S(1)} %order_pages.1) | copy-start | bytes 6291460
  44.4 6.6 %copy-start.17 = (f32[128]{0:T(128)S(1)}, f32[128]{0:T(128)}, u32[]{:S(2)}) copy-start(f32[128]{0:T(128)} %param.20) | copy-start | bytes 1540
  44.4 17.6 %copy-start.22 = (bf16[1,4,32]{2,1,0:T(4,128)(2,1)S(1)}, bf16[1,4,32]{2,1,0:T(4,128)(2,1)}, u32[]{:S(2)}) copy-start(bf16[1,4,32]{2,1,0:T(4,128)(2,1)} %param.27) | copy-start | bytes 772
  44.4 67.4 %all-to-all-start.1 = ((bf16[16,256,256]{2,1,0:T(8,128)(2,1)}), bf16[16,256,256]{2,1,0:T(8,128)(2,1)}, u32[]{:S(2)}, u32[]{:S(2)}) async-start(bf16[16,256,256]{2,1,0:T(8,128)(2,1)} %copy-done), calls=%async_computation.1 | async-start | bytes 4194304 | tf_op jit(solution)/shard_map/all_to_all | solution.py:583
  50.9 44.4 %copy-start.20 = (bf16[1024]{0:T(1024)(128)(2,1)S(1)}, bf16[1024]{0:T(1024)(128)(2,1)}, u32[]{:S(2)}) copy-start(bf16[1024]{0:T(1024)(128)(2,1)} %param.29) | copy-start | bytes 6148
  51.0 44.4 %copy-start.21 = (bf16[1,4,256]{2,1,0:T(4,128)(2,1)S(1)}, bf16[1,4,256]{2,1,0:T(4,128)(2,1)}, u32[]{:S(2)}) copy-start(bf16[1,4,256]{2,1,0:T(4,128)(2,1)} %param.31) | copy-start | bytes 6148
  51.1 0.9 copy-start.5
  52.0 0.9 copy-start.7
  52.9 0.9 copy-start.9
  56.0 25.3 %collective-permute-start.6 = (bf16[768,128]{1,0:T(8,128)(2,1)}, bf16[768,128]{1,0:T(8,128)(2,1)S(1)}, u32[]{:S(2)}, u32[]{:S(2)}) collective-permute-start(bf16[768,128]{1,0:T(8,128)(2,1)} %get-tuple-element.41), channel_id=1, source_target_pairs={{0,8},{8,16},{16,24},{24,0},{32,40},{40,48},{48,56},{56,32},{64,72... | collective-permute-start | bytes 589832 | tf_op jit(solution)/shard_map/ppermute | solution.py:557
  57.9 28.1 %collective-permute-start.7 = (bf16[768,128]{1,0:T(8,128)(2,1)}, bf16[768,128]{1,0:T(8,128)(2,1)S(1)}, u32[]{:S(2)}, u32[]{:S(2)}) collective-permute-start(bf16[768,128]{1,0:T(8,128)(2,1)} %get-tuple-element.42), channel_id=1, source_target_pairs={{0,16},{8,24},{16,0},{24,8},{32,48},{40,56},{48,32},{56,40},{64,80... | collective-permute-start | bytes 589832 | tf_op jit(solution)/shard_map/ppermute | solution.py:557
  60.6 25.4 %collective-permute-start.8 = (bf16[768,128]{1,0:T(8,128)(2,1)}, bf16[768,128]{1,0:T(8,128)(2,1)S(1)}, u32[]{:S(2)}, u32[]{:S(2)}) collective-permute-start(bf16[768,128]{1,0:T(8,128)(2,1)} %get-tuple-element.43), channel_id=1, source_target_pairs={{0,24},{8,0},{16,8},{24,16},{32,56},{40,32},{48,40},{56,48},{64,88... | collective-permute-start | bytes 589832 | tf_op jit(solution)/shard_map/ppermute | solution.py:557
  87.8 5.7 %collective-permute-start.9 = (f32[24,1024]{1,0:T(8,128)S(1)}, f32[24,1024]{1,0:T(8,128)S(1)}, u32[]{:S(2)}, u32[]{:S(2)}) collective-permute-start(f32[24,1024]{1,0:T(8,128)S(1)} %get-tuple-element.47), channel_id=1, source_target_pairs={{0,1},{1,2},{2,3},{3,4},{4,5},{5,6},{6,7},{7,0},{8,9},{9,10},{10,1... | collective-permute-start | bytes 294920 | tf_op jit(solution)/shard_map/ppermute | solution.py:551
  87.8 6.9 %collective-permute-start.10 = (f32[24,1024]{1,0:T(8,128)S(1)}, f32[24,1024]{1,0:T(8,128)S(1)}, u32[]{:S(2)}, u32[]{:S(2)}) collective-permute-start(f32[24,1024]{1,0:T(8,128)S(1)} %get-tuple-element.48), channel_id=1, source_target_pairs={{0,2},{1,3},{2,4},{3,5},{4,6},{5,7},{6,0},{7,1},{8,10},{9,11},{10,... | collective-permute-start | bytes 294920 | tf_op jit(solution)/shard_map/ppermute | solution.py:551
  88.5 22.1 %collective-permute-start.11 = (f32[24,1024]{1,0:T(8,128)S(1)}, f32[24,1024]{1,0:T(8,128)S(1)}, u32[]{:S(2)}, u32[]{:S(2)}) collective-permute-start(f32[24,1024]{1,0:T(8,128)S(1)} %get-tuple-element.49), channel_id=1, source_target_pairs={{0,3},{1,4},{2,5},{3,6},{4,7},{5,0},{6,1},{7,2},{8,11},{9,12},{10,... | collective-permute-start | bytes 294920 | tf_op jit(solution)/shard_map/ppermute | solution.py:551
  89.8 20.7 %collective-permute-start.12 = (f32[24,1024]{1,0:T(8,128)S(1)}, f32[24,1024]{1,0:T(8,128)S(1)}, u32[]{:S(2)}, u32[]{:S(2)}) collective-permute-start(f32[24,1024]{1,0:T(8,128)S(1)} %get-tuple-element.50), channel_id=1, source_target_pairs={{0,4},{1,5},{2,6},{3,7},{4,0},{5,1},{6,2},{7,3},{8,12},{9,13},{10,... | collective-permute-start | bytes 294920 | tf_op jit(solution)/shard_map/ppermute | solution.py:551
  92.5 18.0 %collective-permute-start.13 = (f32[24,1024]{1,0:T(8,128)S(1)}, f32[24,1024]{1,0:T(8,128)S(1)}, u32[]{:S(2)}, u32[]{:S(2)}) collective-permute-start(f32[24,1024]{1,0:T(8,128)S(1)} %get-tuple-element.51), channel_id=1, source_target_pairs={{0,5},{1,6},{2,7},{3,0},{4,1},{5,2},{6,3},{7,4},{8,13},{9,14},{10,... | collective-permute-start | bytes 294920 | tf_op jit(solution)/shard_map/ppermute | solution.py:551
  93.5 17.1 %collective-permute-start.14 = (f32[24,1024]{1,0:T(8,128)S(1)}, f32[24,1024]{1,0:T(8,128)S(1)}, u32[]{:S(2)}, u32[]{:S(2)}) collective-permute-start(f32[24,1024]{1,0:T(8,128)S(1)} %get-tuple-element.52), channel_id=1, source_target_pairs={{0,6},{1,7},{2,0},{3,1},{4,2},{5,3},{6,4},{7,5},{8,14},{9,15},{10,... | collective-permute-start | bytes 294920 | tf_op jit(solution)/shard_map/ppermute | solution.py:551
  94.7 15.9 %collective-permute-start.15 = (f32[24,1024]{1,0:T(8,128)S(1)}, f32[24,1024]{1,0:T(8,128)S(1)}, u32[]{:S(2)}, u32[]{:S(2)}) collective-permute-start(f32[24,1024]{1,0:T(8,128)S(1)} %get-tuple-element.53), channel_id=1, source_target_pairs={{0,7},{1,0},{2,1},{3,2},{4,3},{5,4},{6,5},{7,6},{8,15},{9,8},{10,9... | collective-permute-start | bytes 294920 | tf_op jit(solution)/shard_map/ppermute | solution.py:551
  95.4 16.4 %copy-start.12 = (s32[16,16]{1,0:T(8,128)S(1)}, s32[16,16]{1,0:T(8,128)}, u32[]{:S(2)}) copy-start(s32[16,16]{1,0:T(8,128)} %slot_ref.1) | copy-start | bytes 3076
  95.4 16.4 %copy-start.13 = (bf16[1,4,1024]{2,1,0:T(4,128)(2,1)S(1)}, bf16[1,4,1024]{2,1,0:T(4,128)(2,1)}, u32[]{:S(2)}) copy-start(bf16[1,4,1024]{2,1,0:T(4,128)(2,1)} %param.30) | copy-start | bytes 24580

commit v2 on v1

--- a/solution.py
+++ b/solution.py
@@ -21,7 +21,7 @@
 PARTS = WIDTH // (ROW * LANE)
 STATE_ROWS = 2 * PARTS * NS
 FINAL_ROWS = PARTS * NS
-DEC_X, DEC_Z, DEC_T = 2 * BLK, 2 * BLK + 16, 2 * BLK + 32
+DEC_X = 2 * BLK
 PAGE_ROWS = 2 * BLK + 48
 F32 = jnp.float32
 BF16 = jnp.bfloat16
@@ -32,7 +32,7 @@
 SM = pl.BlockSpec(memory_space=pltpu.SMEM)
 
 
-def params(mib=48):
+def params(mib=44):
     return pltpu.CompilerParams(vmem_limit_bytes=mib * MIB)
 
 
@@ -49,43 +49,42 @@
     return high, (v - high.astype(F32)).astype(BF16)
 
 
-def split_kernel(kv_ref, x_ref, z_ref, dt_ref, out_ref, token_ref):
-    out_ref[0, :BLK, :] = kv_ref[0]
-    out_ref[0, BLK : 2 * BLK, :] = kv_ref[1]
-
-    def fold(rows):
-        rows = rows.astype(F32)
-        return jnp.concatenate([rows[:, q * 256 : (q + 1) * 256] for q in range(4)], axis=0)
-
-    out_ref[0, DEC_X : DEC_X + 16, :] = fold(x_ref[0]).astype(BF16)
-    out_ref[0, DEC_Z : DEC_Z + 16, :] = fold(z_ref[0]).astype(BF16)
-    steps = dt_ref[0].astype(F32)
-    steps = jnp.concatenate([steps, jnp.zeros((steps.shape[0], 256 - steps.shape[1]), F32)], axis=1)
-    steps = jnp.concatenate([steps, jnp.zeros((12, 256), F32)], axis=0)
-    out_ref[0, DEC_T : DEC_T + 16, :] = steps.astype(BF16)
-    token_ref[0] = 0
-
-
-def split_heads(kv_pre, dec_x, dec_z, dec_dt):
-    whole = lambda h: (0, 0, 0)
-    return pl.pallas_call(
-        split_kernel,
-        grid=(TP,),
-        out_shape=[
-            jax.ShapeDtypeStruct((TP, PAGE_ROWS, 2 * HD), BF16),
-            jax.ShapeDtypeStruct((1,), jnp.int32),
-        ],
-        in_specs=[
-            pl.BlockSpec((2, BLK, 2 * HD), lambda h: (0, 0, h)),
-            pl.BlockSpec((1, 4, WC), whole),
-            pl.BlockSpec((1, 4, WC), whole),
-            pl.BlockSpec((1, 4, WC // HP), whole),
-        ],
-        out_specs=[pl.BlockSpec((1, PAGE_ROWS, 2 * HD), lambda h: (h, 0, 0)), SM],
-        cost_estimate=cost(2),
-        compiler_params=params(),
-        name="split_heads",
-    )(kv_pre, dec_x, dec_z, dec_dt)
+def fetch(pairs, sem, first=0):
+    copies = [pltpu.make_async_copy(src, dst, sem.at[first + n]) for n, (src, dst) in enumerate(pairs)]
+    for c in copies:
+        c.start()
+    return copies
+
+
+def split_start(kv, x_hbm, z_hbm, dt_hbm, out, buf, x_buf, z_buf, dt_buf, rows, sem, out_sem):
+    small = fetch([(x_hbm.at[0], x_buf), (z_hbm.at[0], z_buf), (dt_hbm.at[0], dt_buf)], sem, 2 * TP)
+    parts = [(i, pl.ds(q * BLK // 4, BLK // 4)) for i in range(2) for q in range(4)]
+    arrive = fetch([(kv.at[part], buf.at[part]) for part in parts], sem)
+
+    def fold(part):
+        part = part.astype(F32)
+        return jnp.concatenate([part[:, q * 256 : (q + 1) * 256] for q in range(4)], axis=0)
+
+    def finish():
+        for c in small:
+            c.wait()
+        rows[:16, :] = fold(x_buf[...]).astype(BF16)
+        rows[16:32, :] = fold(z_buf[...]).astype(BF16)
+        steps = dt_buf[...].astype(F32)
+        steps = jnp.concatenate([steps, jnp.zeros((steps.shape[0], 256 - steps.shape[1]), F32)], axis=1)
+        steps = jnp.concatenate([steps, jnp.zeros((12, 256), F32)], axis=0)
+        rows[32:, :] = steps.astype(BF16)
+        leave = fetch([(rows, out.at[h, pl.ds(DEC_X, 48), :]) for h in range(TP)], out_sem)
+        for i in range(2):
+            for c in arrive[4 * i : 4 * i + 4]:
+                c.wait()
+            heads = [(h, pl.ds(h * 2 * HD, 2 * HD)) for h in range(TP)]
+            leave += fetch(
+                [(buf.at[i, :, cols], out.at[h, pl.ds(i * BLK, BLK), :]) for h, cols in heads], out_sem, TP * (1 + i)
+            )
+        return leave
+
+    return finish
 
 
 def spread_matrix(ebig):
@@ -127,10 +126,19 @@
     return pltpu.make_async_copy(*(ends[::-1] if out else ends), sem.at[p * STEPS + j])
 
 
-def local_kernel(len_ref, x_hbm, dt_ref, bc_ref, rate_ref, *refs):
-    outs, (stage, ft, bt, x_buf, sem) = refs[:ROW], refs[ROW:]
+def local_kernel(len_ref, x_hbm, dt_hbm, bc_hbm, rate_hbm, kv, dx_hbm, dz_hbm, ddt_hbm, *refs):
+    outs, split, (stage, ft, bt, x_buf, dt_ref, bc_ref, rate_ref, sem), rest = (
+        refs[:ROW],
+        refs[ROW],
+        refs[ROW + 1 : ROW + 9],
+        refs[ROW + 9 :],
+    )
+    small = fetch([(dt_hbm, dt_ref), (bc_hbm, bc_ref), (rate_hbm, rate_ref)], sem, 2 * STEPS)
+    finish = split_start(kv, dx_hbm, dz_hbm, ddt_hbm, split, *rest)
     for c in block_copies(x_hbm, x_buf, sem):
         c.start()
+    for c in small:
+        c.wait()
     lane = lax.broadcasted_iota(jnp.int32, (NS, LANE), 1)
     row = lax.broadcasted_iota(jnp.int32, (NS, HEADS), 0)
     heads = WC // HP
@@ -138,12 +146,14 @@
     for p in range(2):
         live, step, rel, mid = decays(len_ref, dt_ref, rate_ref, p)
         ft[p] = jnp.transpose(jnp.exp(-rel) * step)
-        bt[p] = jnp.transpose(bc_ref[p].astype(F32))[:NS]
+        bt[p] = bc_ref[p, :NS, :].astype(F32)
         high, low = halves(jnp.exp(mid))
         dec = jnp.where(row == p, high.astype(F32), jnp.where(row == 2 + p, low.astype(F32), dec))
     for s in range(ROW):
         stage[s, STATE_ROWS:, :] = dec.astype(BF16)
     for p in range(2):
+        if p == 1:
+            leave = finish()
 
         def body(j, carry):
             quarter, part = lax.div(j, 2), lax.rem(j, 2)
@@ -166,25 +176,38 @@
     y = lax.rem(lax.axis_index("seq"), ROW)
     for o in range(ROW):
         outs[o][...] = stage[lax.rem(y + o, ROW)]
-
-
-def local_states(lengths, x_in, dt_raw, bc_in, rate):
+    for c in leave:
+        c.wait()
+
+
+def local_states(lengths, x_in, dt_raw, bc_in, rate, kv_pre, dec_x, dec_z, dec_dt):
     return pl.pallas_call(
         local_kernel,
-        out_shape=[jax.ShapeDtypeStruct((STATE_ROWS + NS, LANE), BF16)] * ROW,
-        in_specs=[SM, ANY, VM, VM, VM],
-        out_specs=[VM] * ROW,
+        out_shape=[jax.ShapeDtypeStruct((STATE_ROWS + NS, LANE), BF16)] * ROW
+        + [jax.ShapeDtypeStruct((TP, PAGE_ROWS, 2 * HD), BF16)],
+        in_specs=[SM] + [ANY] * 8,
+        out_specs=[VM] * ROW + [ANY],
         scratch_shapes=[
             pltpu.VMEM((ROW, STATE_ROWS + NS, LANE), BF16),
             pltpu.VMEM((2, HEADS, BLK), F32),
             pltpu.VMEM((2, NS, BLK), F32),
             pltpu.VMEM((2, BLK, WIDTH), BF16),
-            pltpu.SemaphoreType.DMA((2 * STEPS,)),
+            pltpu.VMEM((2, BLK, HEADS), BF16),
+            pltpu.VMEM((2, 2 * NS, BLK), BF16),
+            pltpu.VMEM((1, HEADS), F32),
+            pltpu.SemaphoreType.DMA((2 * STEPS + 3,)),
+            pltpu.VMEM((2, BLK, TP * 2 * HD), BF16),
+            pltpu.VMEM((4, WC), BF16),
+            pltpu.VMEM((4, WC), BF16),
+            pltpu.VMEM((4, WC // HP), BF16),
+            pltpu.VMEM((48, 2 * HD), BF16),
+            pltpu.SemaphoreType.DMA((2 * TP + 3,)),
+            pltpu.SemaphoreType.DMA((3 * TP,)),
         ],
         cost_estimate=cost(6),
-        compiler_params=params(),
+        compiler_params=params(60),
         name="local_states",
-    )(lengths, x_in, dt_raw, bc_in, rate)
+    )(lengths, x_in, dt_raw, bc_in, rate, kv_pre, dec_x, dec_z, dec_dt)
 
 
 def place(arrays, scratch, me):
@@ -313,26 +336,42 @@
     )(group_of, pages)
 
 
-def output_kernel(len_ref, x_hbm, dt_ref, bc_ref, rate_ref, skip_ref, *refs):
-    enters, y_hbm, (ebig, both, mix, enter, x_buf, y_buf, sem, out_sem) = refs[:ROW], refs[ROW], refs[ROW + 1 :]
+def spread(values, j, i):
+    lanes = lax.broadcasted_iota(jnp.int32, values.shape, 1)
+    return jnp.take_along_axis(values, j * (WC // HP) + 2 * i + (lanes >> 6), axis=1)
+
+
+GATHERED = 8
+
+
+def output_kernel(len_ref, x_hbm, dt_hbm, bc_hbm, rate_hbm, skip_hbm, *refs):
+    enters, y_hbm, (after, ebig, both, mix, enter, x_buf, y_buf, dt_ref, bc_ref, rate_ref, skip_ref, c_rows, sem, out_sem) = (
+        refs[:ROW],
+        refs[ROW],
+        refs[ROW + 1 :],
+    )
+    y = lax.rem(lax.axis_index("seq"), ROW)
+    pairs = [(dt_hbm, dt_ref), (bc_hbm, bc_ref), (rate_hbm, rate_ref), (skip_hbm, skip_ref)]
+    pairs += [(enters[o].at[pl.ds(0, STATE_ROWS), :], enter.at[lax.rem(y + ROW - o, ROW)]) for o in range(ROW)]
+    small = fetch(pairs, sem, 2 * STEPS)
     for c in block_copies(x_hbm, x_buf, sem):
         c.start()
     spread_matrix(ebig)
-    y = lax.rem(lax.axis_index("seq"), ROW)
-    for o in range(ROW):
-        enter[lax.rem(y + ROW - o, ROW)] = enters[o][:STATE_ROWS, :]
+    for c in small:
+        c.wait()
     rows = lax.broadcasted_iota(jnp.int32, (BLK, BLK), 0)
     cols = lax.broadcasted_iota(jnp.int32, (BLK, BLK), 1)
     for p in range(2):
         live, step, rel, mid = decays(len_ref, dt_ref, rate_ref, p)
-        factors = [jnp.exp(-rel) * step, jnp.exp(rel) * live, jnp.broadcast_to(skip_ref[...] * live, (NS, HEADS))]
-        for at, v in zip((0, BLK, 2 * BLK), factors):
+        after[p] = jnp.exp(rel) * live
+        factors = [jnp.exp(-rel) * step, jnp.broadcast_to(skip_ref[...] * live, (NS, HEADS)), jnp.exp(rel) * live]
+        for at, v in zip((0, BLK, BLK + NS), factors):
             high, low = halves(v)
             both[p, at : at + v.shape[0], :HEADS] = high
             both[p, at : at + v.shape[0], HEADS:] = low
-        scores = lax.dot_general(
-            bc_ref[p, :, NS:], bc_ref[p, :, :NS], (((1,), (1,)), ((), ())), preferred_element_type=F32
-        )
+        maps = jnp.transpose(bc_ref[p].astype(F32)).astype(BF16)
+        c_rows[p] = maps[:, NS:]
+        scores = jnp.dot(c_rows[p], bc_ref[p, :NS, :], preferred_element_type=F32)
         mix[p] = jnp.where(rows >= cols, scores, 0.0).astype(BF16)
     for p in range(2):
 
@@ -341,15 +380,19 @@
             at = pl.ds(pl.multiple_of(j * WC, WC), WC)
             ej = spread_rows(ebig, j)
             x = x_buf[p, :, at].astype(F32)
-            factor = jnp.dot(both[p], ej, preferred_element_type=F32)
+            factor = jnp.dot(both[p, : BLK + NS, :], ej, preferred_element_type=F32)
             xp = (x * factor[:BLK]).astype(BF16)
             first = (p * 2 + lax.rem(j, 2)) * CHUNKS * NS
             entering = enter[lax.div(j, 2), pl.ds(pl.multiple_of(first, CHUNKS * NS), CHUNKS * NS), :]
             entering = jnp.concatenate([entering[i * NS : (i + 1) * NS] for i in range(CHUNKS)], axis=1)
             total = jnp.dot(mix[p], xp, preferred_element_type=F32) + jnp.dot(
-                bc_ref[p, :, NS:], entering, preferred_element_type=F32
+                c_rows[p], entering, preferred_element_type=F32
             )
-            y_buf[p, :, at] = (factor[BLK : 2 * BLK] * total + factor[2 * BLK : 2 * BLK + 1] * x).astype(BF16)
+            scales = [spread(after[p], j, i) for i in range(GATHERED)]
+            if GATHERED < CHUNKS:
+                scales.append(jnp.dot(both[p, BLK + NS :, :], ej[:, GATHERED * LANE :], preferred_element_type=F32))
+            scale = jnp.concatenate(scales, axis=1)
+            y_buf[p, :, at] = (scale * total + factor[BLK : BLK + 1] * x).astype(BF16)
             block_copy(y_hbm, y_buf, out_sem, p, j, out=True).start()
             return carry
 
@@ -362,20 +405,26 @@
     return pl.pallas_call(
         output_kernel,
         out_shape=jax.ShapeDtypeStruct((2, BLK, WIDTH), BF16),
-        in_specs=[SM, ANY] + [VM] * (4 + ROW),
+        in_specs=[SM] + [ANY] * (5 + ROW),
         out_specs=ANY,
         scratch_shapes=[
+            pltpu.VMEM((2, BLK, HEADS), F32),
             pltpu.VMEM((3 * HEADS, WC), BF16),
             pltpu.VMEM((2, 2 * BLK + NS, 2 * HEADS), BF16),
             pltpu.VMEM((2, BLK, BLK), BF16),
             pltpu.VMEM((ROW, STATE_ROWS, LANE), BF16),
             pltpu.VMEM((2, BLK, WIDTH), BF16),
             pltpu.VMEM((2, BLK, WIDTH), BF16),
-            pltpu.SemaphoreType.DMA((2 * STEPS,)),
+            pltpu.VMEM((2, BLK, HEADS), BF16),
+            pltpu.VMEM((2, 2 * NS, BLK), BF16),
+            pltpu.VMEM((1, HEADS), F32),
+            pltpu.VMEM((1, HEADS), F32),
+            pltpu.VMEM((2, BLK, NS), BF16),
+            pltpu.SemaphoreType.DMA((2 * STEPS + 4 + ROW,)),
             pltpu.SemaphoreType.DMA((2 * STEPS,)),
         ],
         cost_estimate=cost(12),
-        compiler_params=params(),
+        compiler_params=params(60),
         name="block_outputs",
     )(lengths, x_in, dt_raw, bc_in, rate, skip, *entering)
 
@@ -389,7 +438,7 @@
 
 
 def attend_kernel(
-    group_ref, len_ref, slot_ref, recv, q_ref, fresh, pool, out_ref, zeros, sem
+    group_ref, len_ref, slot_ref, recv, q_ref, fresh_ref, pool, out_ref, zeros, sem
 ):
     prompt = my_prompt(group_ref)
     length = len_ref[prompt]
@@ -410,7 +459,10 @@
         def _():
             page_copy(s, False).start()
 
-    q = q_ref[...]
+    q = q_ref[0].astype(F32)
+    q = jnp.concatenate([q[:, h * HD : (h + 1) * HD] for h in range(WC // HD)], axis=0).astype(BF16)
+    fresh = fresh_ref[0].astype(F32)
+    fresh = jnp.concatenate([fresh, jnp.zeros((12, 2 * HD), F32)], axis=0).astype(BF16)
     scale = HD**-0.5
     contract = (((1,), (1,)), ((), ()))
     rows = lax.broadcasted_iota(jnp.int32, (q.shape[0], fresh.shape[0]), 0)
@@ -455,20 +507,30 @@
     )(group_of, lengths, slot_of, recv, queries, fresh)
 
 
-def decode_kernel(inputs, bct_ref, rate_ref, skip_ref, *refs):
-    finals, outs, (fin, res) = refs[:ROW], refs[ROW : ROW + TP], refs[ROW + TP :]
-    me = lax.axis_index("tp")
+def decode_kernel(inputs, maps_ref, rate_ref, skip_ref, *refs):
+    finals, (own, other, fin, res) = refs[:ROW], refs[ROW:]
+    core = lax.rem(lax.axis_index("tp"), 2)
     y = lax.rem(lax.axis_index("seq"), ROW)
     for o in range(ROW):
         fin[lax.rem(y + ROW - o, ROW)] = finals[o][STATE_ROWS:, :]
+    maps = maps_ref[0].astype(F32)
+    eye = lax.broadcasted_iota(jnp.int32, (NS, NS), 0) == lax.broadcasted_iota(jnp.int32, (NS, NS), 1)
+
+    def column(k, at):
+        return jnp.sum(jnp.where(eye, maps[k : k + 1, at : at + NS], 0.0), axis=1, keepdims=True)
+
+    b_cols = [column(k, 0) for k in range(4)]
+    c_cols = [column(k, NS) for k in range(4)]
     heads = WC // HP
     rows = lax.broadcasted_iota(jnp.int32, (heads, WC), 0)
     cols = lax.broadcasted_iota(jnp.int32, (heads, WC), 1)
     spread = jnp.where(rows == (cols >> 6), 1.0, 0.0).astype(F32)
-    raw = [inputs[t, DEC_T : DEC_T + 16, :].astype(F32)[:4, :heads] for t in range(TP)]
+    raw = [inputs[t, DEC_X + 32 : DEC_X + 48, :].astype(F32)[:4, :heads] for t in range(TP)]
     step = softplus(jnp.concatenate(raw, axis=0))
-    rates = jnp.concatenate([jnp.broadcast_to(rate_ref[t : t + 1], (4, heads)) for t in range(TP)], axis=0)
-    small = jnp.concatenate([step, jnp.exp(-step * rates), skip_ref[...]], axis=0)
+    parts = [slice(t * heads, (t + 1) * heads) for t in range(TP)]
+    rates = jnp.concatenate([jnp.broadcast_to(rate_ref[:, part], (4, heads)) for part in parts], axis=0)
+    skips = jnp.concatenate([skip_ref[:, part] for part in parts], axis=0)
+    small = jnp.concatenate([step, jnp.exp(-step * rates), skips], axis=0)
     wide = jnp.dot(small, spread, precision=highest, preferred_element_type=F32)
 
     def unfold(rows):
@@ -477,7 +539,7 @@
     sums = [jnp.zeros((1, 1), F32)] * 4
     for t in range(TP):
         x = unfold(inputs[t, DEC_X : DEC_X + 16, :].astype(F32))
-        z = unfold(inputs[t, DEC_Z : DEC_Z + 16, :].astype(F32))
+        z = unfold(inputs[t, DEC_X + 16 : DEC_X + 32, :].astype(F32))
         gate = z / (1.0 + jnp.exp(-z))
         chunks = [t * CHUNKS + i for i in range(CHUNKS)]
         state = jnp.concatenate(
@@ -485,12 +547,10 @@
         )
         skip = wide[8 * TP + t : 8 * TP + t + 1]
         for k in range(4):
-            b_col = bct_ref[:NS, k : k + 1]
-            c_col = bct_ref[NS:, k : k + 1]
             wide_step = wide[4 * t + k : 4 * t + k + 1]
             fade = wide[4 * TP + 4 * t + k : 4 * TP + 4 * t + k + 1]
-            state = fade * state + b_col * (wide_step * x[k : k + 1])
-            read = jnp.sum(c_col * state, axis=0, keepdims=True) + skip * x[k : k + 1]
+            state = fade * state + b_cols[k] * (wide_step * x[k : k + 1])
+            read = jnp.sum(c_cols[k] * state, axis=0, keepdims=True) + skip * x[k : k + 1]
             v = read * gate[k : k + 1]
             res[t, NS + k : NS + k + 1, :] = v
             sums[k] = sums[k] + jnp.sum(v * v, axis=1, keepdims=True)
@@ -499,16 +559,17 @@
     for t in range(TP):
         res[t, NS : NS + 4, :] = res[t, NS : NS + 4, :] * factor
         res[t, NS + 4 :, :] = jnp.zeros((4, WC), F32)
-    for o in range(TP):
-        outs[o][...] = res[lax.rem(me + o, TP)]
-
-
-def decode(inputs, bct, rate, skip, finals):
+    for z in range(ROW):
+        own[z] = res[2 * z + core]
+        other[z] = res[2 * z + 1 - core]
+
+
+def decode(inputs, maps, rate, skip, finals):
     return pl.pallas_call(
         decode_kernel,
-        out_shape=[jax.ShapeDtypeStruct((NS + 8, WC), F32)] * TP,
+        out_shape=[jax.ShapeDtypeStruct((ROW, NS + 8, WC), F32)] * 2,
         in_specs=[VM] * (4 + ROW),
-        out_specs=[VM] * TP,
+        out_specs=[VM] * 2,
         scratch_shapes=[
             pltpu.VMEM((ROW, FINAL_ROWS, LANE), BF16),
             pltpu.VMEM((TP, NS + 8, WC), F32),
@@ -516,14 +577,35 @@
         cost_estimate=cost(4),
         compiler_params=params(),
         name="decode",
-    )(inputs, bct, rate, skip, *finals)
+    )(inputs, maps, rate, skip, *finals)
+
+
+def side_kernel(group_ref, own, other, *outs):
+    me = lax.axis_index("tp")
+    z, core = lax.div(me, 2), lax.rem(me, 2)
+    mine = lax.rem(lax.div(my_prompt(group_ref), 2), 2) == core
+    for o in range(ROW):
+        at = lax.rem(z + o, ROW)
+        outs[o][...] = jnp.where(mine, own[at], other[at])
+
+
+def choose_side(group_of, own, other):
+    return pl.pallas_call(
+        side_kernel,
+        out_shape=[jax.ShapeDtypeStruct((NS + 8, WC), F32)] * ROW,
+        in_specs=[SM, VM, VM],
+        out_specs=[VM] * ROW,
+        cost_estimate=cost(1),
+        compiler_params=params(),
+        name="choose_side",
+    )(group_of, own, other)
 
 
 def pick_kernel(group_ref, gain_ref, *refs):
-    results, (state_ref, out_ref) = refs[:TP], refs[TP:]
-    holder = lax.div(my_prompt(group_ref), 2)
-    distance = lax.rem(lax.axis_index("tp") + TP - holder, TP)
-    for o in range(TP):
+    results, (state_ref, out_ref) = refs[:ROW], refs[ROW:]
+    holder = lax.div(my_prompt(group_ref), 4)
+    distance = lax.rem(lax.div(lax.axis_index("tp"), 2) + ROW - holder, ROW)
+    for o in range(ROW):
 
         @pl.when(distance == o)
         def _():
@@ -538,7 +620,7 @@
             jax.ShapeDtypeStruct((1, NS, WC), F32),
             jax.ShapeDtypeStruct((1, 4, WC), BF16),
         ],
-        in_specs=[SM] + [VM] * (1 + TP),
+        in_specs=[SM] + [VM] * (1 + ROW),
         out_specs=[VM] * 2,
         cost_estimate=cost(1),
         compiler_params=params(),
@@ -546,10 +628,9 @@
     )(group_of, gain, *results)
 
 
-def rotate(arrays):
-    return [arrays[0]] + [
-        lax.ppermute(arrays[o], "tp", [(i, (i + o) % TP) for i in range(TP)]) for o in range(1, TP)
-    ]
+def along_z(arrays):
+    moves = [[(i, (i + 2 * o) % TP) for i in range(TP)] for o in range(ROW)]
+    return [arrays[0]] + [lax.ppermute(arrays[o], "tp", moves[o]) for o in range(1, ROW)]
 
 
 def along_y(arrays):
@@ -568,23 +649,23 @@
 ):
     rate = decay_rate.reshape(1, HEADS)
     skip = skip_gain.reshape(1, HEADS)
-    bct = jnp.transpose(dec_bc[0].astype(F32))
-    queries = jnp.transpose(dec_q.reshape(4, -1, HD), (1, 0, 2)).reshape(-1, HD)
-    fresh = jnp.concatenate([dec_kv[0], jnp.zeros((12, 2 * HD), BF16)], axis=0)
     gain = norm_gain.reshape(1, -1)
-
-    sent, token = split_heads(kv_pre, dec_x, dec_z, dec_dt)
+    maps = jnp.swapaxes(bc_in, 1, 2)
+
+    *local, sent = local_states(lengths, x_in, dt_raw, maps, rate, kv_pre, dec_x, dec_z, dec_dt)
     pages = lax.all_to_all(sent, "tp", split_axis=0, concat_axis=0, tiled=True)
-    early_lengths, token = lax.optimization_barrier((lengths, token))
-    blocks = along_y(local_states(early_lengths, x_in, dt_raw, bc_in, rate))
+    blocks = along_y(local)
     totals = along_x([row_totals(blocks)] * ROW)
-    pages, totals = lax.optimization_barrier((pages, totals))
+    pages, unused = lax.optimization_barrier((pages, totals))
     entering = along_y(enter_states(group_of, blocks, totals))
-    recv = lax.all_to_all(order_pages(group_of, pages), "seq", split_axis=0, concat_axis=0, tiled=True)
-    results = decode(pages, bct, decay_rate.reshape(TP, -1), skip_gain.reshape(TP, -1), entering)
-    dec_state, dec_mamba = pick(group_of, gain, rotate(results))
-    y_pre = block_outputs(lengths, x_in, dt_raw, bc_in, rate, skip, entering)
-    kv_pool, dec_attn = attend(group_of, lengths, slot_of, recv, queries, fresh)
+    ordered, entering = lax.optimization_barrier((order_pages(group_of, pages), entering))
+    recv = lax.all_to_all(ordered, "seq", split_axis=0, concat_axis=0, tiled=True)
+    own, other = decode(pages, dec_bc, rate, skip, entering)
+    other = lax.ppermute(other, "tp", [(i, i ^ 1) for i in range(TP)])
+    results = along_z(choose_side(group_of, own, other))
+    dec_state, dec_mamba = pick(group_of, gain, results)
+    y_pre = block_outputs(lengths, x_in, dt_raw, maps, rate, skip, entering)
+    kv_pool, dec_attn = attend(group_of, lengths, slot_of, recv, dec_q, dec_kv)
     return (y_pre, kv_pool, dec_mamba, dec_state, dec_attn)
 
 

time: 119 us -> 91 us (0.76); the launches traced: 116 us -> 90.7 us
  waiting for transfers between devices: 36.5 us -> 25.2 us
  local copies, waits for them, and re-layouts: 10.8 us -> 1.4 us
  starting transfers between devices: 35.9 us -> 30.5 us
    ppermute x6, waiting for transfers between devices: 29.4 us -> 11.3 us  [along_y(): lax.ppermute(arrays[o], 'seq', moves[o])]
    unnamed x47 -> x36, local copies, waits for them, and re-layouts: 10.5 us -> 1.39 us
    all_to_all x1, waiting for transfers between devices: 0.01 us -> 4.67 us  [shards(): lax.all_to_all(ordered, 'seq', split_axis=0, concat_axis=0, tiled=True)]
    pallas_call x1, Pallas kernels: 5.26 us -> 7.78 us  [local_states(): pl.pallas_call(local_kernel, out_shape=[jax.ShapeDtypeStruct((STATE_ROWS...]
    ppermute x7 -> x4, starting transfers between devices: 7.45 us -> 5.21 us  [the longest x3 5.12 us: along_z(): lax.ppermute(arrays[o], 'tp', moves[o])]
    all_to_all x1, starting transfers between devices: 6.53 us -> 4.45 us  [shards(): lax.all_to_all(ordered, 'seq', split_axis=0, concat_axis=0, tiled=True)]
    ppermute x7 -> x4, waiting for transfers between devices: 0.13 us -> 1.72 us  [the longest x1 1.71 us: shards(): other = lax.ppermute(other, 'tp', [(i, i ^ 1) for i in range(TP)])]
  transfers between devices with their start and end apart: 18 -> 15, of which waited for: 8 -> 9; matrix products, arithmetic and copies ran while one was open for 0% -> 0% of each run, Pallas kernels for 22% -> 23%
where the time goes in v2:
time: 91 us; the launch traced here: 90.7 us
  Pallas kernels  32.6 us (36%)
  starting transfers between devices  30.5 us (34%)
  waiting for transfers between devices  25.2 us (28%)
  local copies, waits for them, and re-layouts  1.4 us (2%)
    pallas_call x1, Pallas kernels, block_outputs(): pl.pallas_call(output_kernel, out_shape=jax.ShapeDtypeStruct((2, BLK, WID...  14.1 us
    ppermute x6, waiting for transfers between devices, along_y(): lax.ppermute(arrays[o], 'seq', moves[o])  11.3 us
    ppermute x6, starting transfers between devices, along_y(): lax.ppermute(arrays[o], 'seq', moves[o])  10.8 us
    pallas_call x1, Pallas kernels, local_states(): pl.pallas_call(local_kernel, out_shape=[jax.ShapeDtypeStruct((STATE_ROWS...  7.78 us
    ppermute x3, waiting for transfers between devices, along_x(): lax.ppermute(arrays[o], 'seq', moves[o])  7.58 us
    all_to_all x1, starting transfers between devices, shards(): pages = lax.all_to_all(sent, 'tp', split_axis=0, concat_axis=0, tiled=True)  5.54 us
    ppermute x3, starting transfers between devices, along_z(): lax.ppermute(arrays[o], 'tp', moves[o])  5.12 us
    all_to_all x1, waiting for transfers between devices, shards(): lax.all_to_all(ordered, 'seq', split_axis=0, concat_axis=0, tiled=True)  4.67 us
  transfers between devices with their start and end apart: 15, of which 9 were waited for; matrix products, arithmetic and copies ran while one was open for 0% of the time, Pallas kernels for 23%

profile of v2, /device:TPU:0, one launch (start us, length us, event | category | flops | bytes accessed | tf_op | source)
XLA Modules:
  0.0 90.7 jit_solution(152618413904145562)
XLA Ops:
  0.6 7.8 %local_states.1 = (bf16[528,128]{1,0:T(8,128)(2,1)}, bf16[528,128]{1,0:T(8,128)(2,1)}, bf16[528,128]{1,0:T(8,128)(2,1)}, bf16[528,128]{1,0:T(8,128)(2,1)}, bf16[8,560,256]{2,1,0:T(8,128)(2,1)}) custom-call(s32[16]{0:T(128)} %len_ref.5, bf16[2,256,8192]{2,1,0:T(8,128)(2,1)} %x_hbm.3, bf16[2,256,128]{2,1,0:T(8,128)(2,1)} %dt_hbm.3, ...), custom_call_target="tpu_custom_call" | custom-call | bytes 18000000 | tf_op jit(solution)/shard_map/local_states/pallas_call | solution.py:184
  8.4 0.0 copy-start.17
  8.5 0.0 copy-start.5
  8.5 0.0 copy-start.6
  8.5 5.5 %all-to-all-start = ((bf16[8,560,256]{2,1,0:T(8,128)(2,1)}), bf16[8,560,256]{2,1,0:T(8,128)(2,1)S(1)}, u32[]{:S(2)}, u32[]{:S(2)}) async-start(bf16[8,560,256]{2,1,0:T(8,128)(2,1)} %get-tuple-element.30), calls=%async_computation | async-start | bytes 4587520 | tf_op jit(solution)/shard_map/all_to_all | solution.py:656
  14.0 1.6 %collective-permute-start = (bf16[528,128]{1,0:T(8,128)(2,1)S(1)}, bf16[528,128]{1,0:T(8,128)(2,1)S(1)}, u32[]{:S(2)}, u32[]{:S(2)}) collective-permute-start(bf16[528,128]{1,0:T(8,128)(2,1)S(1)} %copy-done.17), channel_id=1, source_target_pairs={{0,8},{8,16},{16,24},{24,0},{32,40},{40,48},{48,56},{56,32},{64,72... | collective-permute-start | bytes 405512 | tf_op jit(solution)/shard_map/ppermute | solution.py:638
  15.7 2.9 %collective-permute-start.1 = (bf16[528,128]{1,0:T(8,128)(2,1)S(1)}, bf16[528,128]{1,0:T(8,128)(2,1)S(1)}, u32[]{:S(2)}, u32[]{:S(2)}) collective-permute-start(bf16[528,128]{1,0:T(8,128)(2,1)S(1)} %copy-done.16), channel_id=1, source_target_pairs={{0,16},{8,24},{16,0},{24,8},{32,48},{40,56},{48,32},{56,40},{64,80... | collective-permute-start | bytes 405512 | tf_op jit(solution)/shard_map/ppermute | solution.py:638
  18.6 1.3 %collective-permute-start.2 = (bf16[528,128]{1,0:T(8,128)(2,1)S(1)}, bf16[528,128]{1,0:T(8,128)(2,1)S(1)}, u32[]{:S(2)}, u32[]{:S(2)}) collective-permute-start(bf16[528,128]{1,0:T(8,128)(2,1)S(1)} %copy-done.15), channel_id=1, source_target_pairs={{0,24},{8,0},{16,8},{24,16},{32,56},{40,32},{48,40},{56,48},{64,88... | collective-permute-start | bytes 405512 | tf_op jit(solution)/shard_map/ppermute | solution.py:638
  19.9 1.4 %collective-permute-done.refs_1_ = bf16[528,128]{1,0:T(8,128)(2,1)S(1)} collective-permute-done((bf16[528,128]{1,0:T(8,128)(2,1)S(1)}, bf16[528,128]{1,0:T(8,128)(2,1)S(1)}, u32[]{:S(2)}, u32[]{:S(2)}) %collective-permute-start) | collective-permute-done | bytes 135200 | tf_op jit(solution)/shard_map/ppermute | solution.py:638
  21.3 4.1 %collective-permute-done.1.refs_2_ = bf16[528,128]{1,0:T(8,128)(2,1)S(1)} collective-permute-done((bf16[528,128]{1,0:T(8,128)(2,1)S(1)}, bf16[528,128]{1,0:T(8,128)(2,1)S(1)}, u32[]{:S(2)}, u32[]{:S(2)}) %collective-permute-start.1) | collective-permute-done | bytes 135200 | tf_op jit(solution)/shard_map/ppermute | solution.py:638
  25.4 0.0 collective-permute-done.2.refs_3_
  25.4 0.3 row_totals.1.refs_4_
  25.7 2.8 %collective-permute-start.5 = (bf16[528,128]{1,0:T(8,128)(2,1)S(1)}, bf16[528,128]{1,0:T(8,128)(2,1)S(1)}, u32[]{:S(2)}, u32[]{:S(2)}) collective-permute-start(bf16[528,128]{1,0:T(8,128)(2,1)S(1)} %row_totals.1.refs_4_), channel_id=1, source_target_pairs={{0,96},{8,104},{16,112},{24,120},{32,0},{40,8},{48,16},{56,24},{64... | collective-permute-start | bytes 405512 | tf_op jit(solution)/shard_map/ppermute | solution.py:643
  28.6 0.8 collective-permute-start.4
  29.4 0.9 collective-permute-start.3
  30.2 3.9 %collective-permute-done.5.refs_7_ = bf16[528,128]{1,0:T(8,128)(2,1)S(1)} collective-permute-done((bf16[528,128]{1,0:T(8,128)(2,1)S(1)}, bf16[528,128]{1,0:T(8,128)(2,1)S(1)}, u32[]{:S(2)}, u32[]{:S(2)}) %collective-permute-start.5) | collective-permute-done | bytes 135200 | tf_op jit(solution)/shard_map/ppermute | solution.py:643
  34.1 2.3 %collective-permute-done.4.refs_6_ = bf16[528,128]{1,0:T(8,128)(2,1)S(1)} collective-permute-done((bf16[528,128]{1,0:T(8,128)(2,1)S(1)}, bf16[528,128]{1,0:T(8,128)(2,1)S(1)}, u32[]{:S(2)}, u32[]{:S(2)}) %collective-permute-start.4) | collective-permute-done | bytes 135200 | tf_op jit(solution)/shard_map/ppermute | solution.py:643
  36.4 1.4 %collective-permute-done.3.refs_5_ = bf16[528,128]{1,0:T(8,128)(2,1)S(1)} collective-permute-done((bf16[528,128]{1,0:T(8,128)(2,1)S(1)}, bf16[528,128]{1,0:T(8,128)(2,1)S(1)}, u32[]{:S(2)}, u32[]{:S(2)}) %collective-permute-start.3) | collective-permute-done | bytes 135200 | tf_op jit(solution)/shard_map/ppermute | solution.py:643
  37.8 2.0 %enter_states.1 = (bf16[768,128]{1,0:T(8,128)(2,1)S(1)}, bf16[768,128]{1,0:T(8,128)(2,1)}, bf16[768,128]{1,0:T(8,128)(2,1)S(1)}, bf16[768,128]{1,0:T(8,128)(2,1)S(1)}) custom-call(s32[16]{0:T(128)S(1)} %copy-done.6, bf16[528,128]{1,0:T(8,128)(2,1)S(1)} %copy-done.5, bf16[528,128]{1,0:T(8,128)(2,1)S(1)} %collective-permute-done.refs_1_, ...), custom_call_target="tpu_custom_call" | custom-call | bytes 6000000 | tf_op jit(solution)/shard_map/enter_states/pallas_call | solution.py:304
  39.9 0.9 collective-permute-start.6
  40.7 2.8 %collective-permute-start.7 = (bf16[768,128]{1,0:T(8,128)(2,1)S(1)}, bf16[768,128]{1,0:T(8,128)(2,1)S(1)}, u32[]{:S(2)}, u32[]{:S(2)}) collective-permute-start(bf16[768,128]{1,0:T(8,128)(2,1)S(1)} %get-tuple-element.38), channel_id=1, source_target_pairs={{0,16},{8,24},{16,0},{24,8},{32,48},{40,56},{48,32},{56,40},{64,80... | collective-permute-start | bytes 589832 | tf_op jit(solution)/shard_map/ppermute | solution.py:638
  43.6 1.2 %collective-permute-start.8 = (bf16[768,128]{1,0:T(8,128)(2,1)S(1)}, bf16[768,128]{1,0:T(8,128)(2,1)S(1)}, u32[]{:S(2)}, u32[]{:S(2)}) collective-permute-start(bf16[768,128]{1,0:T(8,128)(2,1)S(1)} %get-tuple-element.39), channel_id=1, source_target_pairs={{0,24},{8,0},{16,8},{24,16},{32,56},{40,32},{48,40},{56,48},{64,88... | collective-permute-start | bytes 589832 | tf_op jit(solution)/shard_map/ppermute | solution.py:638
  44.7 0.0 all-to-all-done.pages.inputs
  44.7 0.7 order_pages.1
  45.4 0.0 copy-start
  45.4 1.3 %copy-done = bf16[16,256,256]{2,1,0:T(8,128)(2,1)} copy-done((bf16[16,256,256]{2,1,0:T(8,128)(2,1)}, bf16[16,256,256]{2,1,0:T(8,128)(2,1)S(1)}, u32[]{:S(2)}) %copy-start) | copy-done | bytes 2097176
  46.8 1.5 %collective-permute-done.6.refs_1_ = bf16[768,128]{1,0:T(8,128)(2,1)S(1)} collective-permute-done((bf16[768,128]{1,0:T(8,128)(2,1)}, bf16[768,128]{1,0:T(8,128)(2,1)S(1)}, u32[]{:S(2)}, u32[]{:S(2)}) %collective-permute-start.6) | collective-permute-done | bytes 196640 | tf_op jit(solution)/shard_map/ppermute | solution.py:638
  48.2 4.3 %collective-permute-done.7.refs_2_ = bf16[768,128]{1,0:T(8,128)(2,1)S(1)} collective-permute-done((bf16[768,128]{1,0:T(8,128)(2,1)S(1)}, bf16[768,128]{1,0:T(8,128)(2,1)S(1)}, u32[]{:S(2)}, u32[]{:S(2)}) %collective-permute-start.7) | collective-permute-done | bytes 196640 | tf_op jit(solution)/shard_map/ppermute | solution.py:638
  52.6 0.0 collective-permute-done.8.refs_3_
  52.6 4.4 %all-to-all-start.1 = ((bf16[16,256,256]{2,1,0:T(8,128)(2,1)}), bf16[16,256,256]{2,1,0:T(8,128)(2,1)}, u32[]{:S(2)}, u32[]{:S(2)}) async-start(bf16[16,256,256]{2,1,0:T(8,128)(2,1)} %copy-done), calls=%async_computation.1 | async-start | bytes 4194304 | tf_op jit(solution)/shard_map/all_to_all | solution.py:662
  57.0 0.0 copy-start.14
  57.1 1.6 %decode.1 = (f32[4,24,1024]{2,1,0:T(8,128)S(1)}, f32[4,24,1024]{2,1,0:T(8,128)S(1)}) custom-call(bf16[8,560,256]{2,1,0:T(8,128)(2,1)S(1)} %all-to-all-done.pages.inputs, bf16[1,4,32]{2,1,0:T(4,128)(2,1)S(1)} %copy-done.13, f32[1,128]{1,0:T(1,128)S(1)} %bitcast.5, f32[1,128]{1,0:T(1,128)S(1)} %bitcast.7, bf16[768,128]{1,0:T(8,128)(2,1)S(1)} %get-tuple-element.40.refs_0_, ...), custom_call_target="tpu_custom_call" | custom-call | bytes 12000000 | tf_op jit(solution)/shard_map/decode/pallas_call | solution.py:568
  58.7 0.1 collective-permute-start.9
  58.8 1.7 %collective-permute-done.9.other = f32[4,24,1024]{2,1,0:T(8,128)S(1)} collective-permute-done((f32[4,24,1024]{2,1,0:T(8,128)S(1)}, f32[4,24,1024]{2,1,0:T(8,128)S(1)}, u32[]{:S(2)}, u32[]{:S(2)}) %collective-permute-start.9) | collective-permute-done | bytes 393248 | tf_op jit(solution)/shard_map/ppermute | solution.py:664
  60.5 0.6 choose_side.1
  61.1 1.0 %collective-permute-start.10 = (f32[24,1024]{1,0:T(8,128)S(1)}, f32[24,1024]{1,0:T(8,128)S(1)}, u32[]{:S(2)}, u32[]{:S(2)}) collective-permute-start(f32[24,1024]{1,0:T(8,128)S(1)} %get-tuple-element.49), channel_id=1, source_target_pairs={{0,2},{1,3},{2,4},{3,5},{4,6},{5,7},{6,0},{7,1},{8,10},{9,11},{10,... | collective-permute-start | bytes 294920 | tf_op jit(solution)/shard_map/ppermute | solution.py:633
  62.1 2.7 %collective-permute-start.11 = (f32[24,1024]{1,0:T(8,128)S(1)}, f32[24,1024]{1,0:T(8,128)S(1)}, u32[]{:S(2)}, u32[]{:S(2)}) collective-permute-start(f32[24,1024]{1,0:T(8,128)S(1)} %get-tuple-element.50), channel_id=1, source_target_pairs={{0,4},{1,5},{2,6},{3,7},{4,0},{5,1},{6,2},{7,3},{8,12},{9,13},{10,... | collective-permute-start | bytes 294920 | tf_op jit(solution)/shard_map/ppermute | solution.py:633
  64.8 1.5 %collective-permute-start.12 = (f32[24,1024]{1,0:T(8,128)S(1)}, f32[24,1024]{1,0:T(8,128)S(1)}, u32[]{:S(2)}, u32[]{:S(2)}) collective-permute-start(f32[24,1024]{1,0:T(8,128)S(1)} %get-tuple-element.51), channel_id=1, source_target_pairs={{0,6},{1,7},{2,0},{3,1},{4,2},{5,3},{6,4},{7,5},{8,14},{9,15},{10,... | collective-permute-start | bytes 294920 | tf_op jit(solution)/shard_map/ppermute | solution.py:633
  66.3 0.0 copy-start.8
  66.3 0.0 copy-start.9
  66.3 0.0 copy-start.11
  66.3 14.1 %block_outputs.1 = bf16[2,256,8192]{2,1,0:T(8,128)(2,1)} custom-call(s32[16]{0:T(128)} %len_ref.5, bf16[2,256,8192]{2,1,0:T(8,128)(2,1)} %x_hbm.3, bf16[2,256,128]{2,1,0:T(8,128)(2,1)} %dt_hbm.3, bf16[2,32,256]{2,1,0:T(8,128)(2,1)} %bitcast.9, f32[1,128]{1,0:T(1,128)} %bitcast.4, f32[1,128]{1,0:T(1,128)} %bitcast.6, bf16[768,128]{1,0:T(8,128)(2,1)} %copy-done.1, ...), custom_call_target="tpu_custom_call" | custom-call | bytes 36000000 | tf_op jit(solution)/shard_map/block_outputs/pallas_call | solution.py:405
  80.4 0.0 collective-permute-done.10.refs_1_
  80.4 0.0 collective-permute-done.11.refs_2_
  80.4 0.0 collective-permute-done.12.refs_3_
  80.4 1.2 %pick.1 = (f32[1,16,1024]{2,1,0:T(8,128)}, bf16[1,4,1024]{2,1,0:T(4,128)(2,1)}) custom-call(s32[16]{0:T(128)S(1)} %copy-done.6, bf16[1,1024]{1,0:T(2,128)(2,1)S(1)} %reshape.21.gain_ref, f32[24,1024]{1,0:T(8,128)S(1)} %get-tuple-element.48.refs_0_, f32[24,1024]{1,0:T(8,128)S(1)} %collective-permute-done.10.refs_1_, ...), custom_call_target="tpu_custom_call" | custom-call | bytes 3000000 | tf_op jit(solution)/shard_map/pick/pallas_call | solution.py:617
  81.7 4.7 %all-to-all-done.1.recv = bf16[16,256,256]{2,1,0:T(8,128)(2,1)} async-done(((bf16[16,256,256]{2,1,0:T(8,128)(2,1)}), bf16[16,256,256]{2,1,0:T(8,128)(2,1)}, u32[]{:S(2)}, u32[]{:S(2)}) %all-to-all-start.1) | async-done | bytes 2097184 | tf_op jit(solution)/shard_map/all_to_all | solution.py:662
  86.4 4.3 %attend.1 = (bf16[1,4096,256]{2,1,0:T(8,128)(2,1)}, bf16[1,4,1024]{2,1,0:T(4,128)(2,1)}) custom-call(s32[16]{0:T(128)S(1)} %copy-done.6, s32[16]{0:T(128)S(1)} %copy-done.9, s32[16,16]{1,0:T(8,128)S(1)} %copy-done.7, bf16[16,256,256]{2,1,0:T(8,128)(2,1)} %all-to-all-done.1.recv, bf16[1,4,1024]{2,1,0:T(4,128)(2,1)S(1)} %copy-done.8, ...), custom_call_target="tpu_custom_call" | custom-call | bytes 15000000 | tf_op jit(solution)/shard_map/attend/pallas_call | solution.py:495
  (28 shorter events, 0.1 us)
Async XLA Ops:
  8.4 5.6 %copy-start.17 = (bf16[528,128]{1,0:T(8,128)(2,1)S(1)}, bf16[528,128]{1,0:T(8,128)(2,1)}, u32[]{:S(2)}) copy-start(bf16[528,128]{1,0:T(8,128)(2,1)} %get-tuple-element.32) | copy-start | bytes 405508
  8.4 7.2 %copy-start.16 = (bf16[528,128]{1,0:T(8,128)(2,1)S(1)}, bf16[528,128]{1,0:T(8,128)(2,1)}, u32[]{:S(2)}) copy-start(bf16[528,128]{1,0:T(8,128)(2,1)} %get-tuple-element.33) | copy-start | bytes 405508
  8.4 10.1 %copy-start.15 = (bf16[528,128]{1,0:T(8,128)(2,1)S(1)}, bf16[528,128]{1,0:T(8,128)(2,1)}, u32[]{:S(2)}) copy-start(bf16[528,128]{1,0:T(8,128)(2,1)} %get-tuple-element.34) | copy-start | bytes 405508
  8.5 16.9 %copy-start.5 = (bf16[528,128]{1,0:T(8,128)(2,1)S(1)}, bf16[528,128]{1,0:T(8,128)(2,1)}, u32[]{:S(2)}) copy-start(bf16[528,128]{1,0:T(8,128)(2,1)} %get-tuple-element.31.refs_0_) | copy-start | bytes 405508
  8.5 29.4 %copy-start.6 = (s32[16]{0:T(128)S(1)}, s32[16]{0:T(128)}, u32[]{:S(2)}) copy-start(s32[16]{0:T(128)} %group_ref.9) | copy-start | bytes 196
  8.5 36.3 %all-to-all-start = ((bf16[8,560,256]{2,1,0:T(8,128)(2,1)}), bf16[8,560,256]{2,1,0:T(8,128)(2,1)S(1)}, u32[]{:S(2)}, u32[]{:S(2)}) async-start(bf16[8,560,256]{2,1,0:T(8,128)(2,1)} %get-tuple-element.30), calls=%async_computation | async-start | bytes 4587520 | tf_op jit(solution)/shard_map/all_to_all | solution.py:656
  14.0 7.3 %collective-permute-start = (bf16[528,128]{1,0:T(8,128)(2,1)S(1)}, bf16[528,128]{1,0:T(8,128)(2,1)S(1)}, u32[]{:S(2)}, u32[]{:S(2)}) collective-permute-start(bf16[528,128]{1,0:T(8,128)(2,1)S(1)} %copy-done.17), channel_id=1, source_target_pairs={{0,8},{8,16},{16,24},{24,0},{32,40},{40,48},{48,56},{56,32},{64,72... | collective-permute-start | bytes 405512 | tf_op jit(solution)/shard_map/ppermute | solution.py:638
  15.7 9.7 %collective-permute-start.1 = (bf16[528,128]{1,0:T(8,128)(2,1)S(1)}, bf16[528,128]{1,0:T(8,128)(2,1)S(1)}, u32[]{:S(2)}, u32[]{:S(2)}) collective-permute-start(bf16[528,128]{1,0:T(8,128)(2,1)S(1)} %copy-done.16), channel_id=1, source_target_pairs={{0,16},{8,24},{16,0},{24,8},{32,48},{40,56},{48,32},{56,40},{64,80... | collective-permute-start | bytes 405512 | tf_op jit(solution)/shard_map/ppermute | solution.py:638
  18.6 6.8 %collective-permute-start.2 = (bf16[528,128]{1,0:T(8,128)(2,1)S(1)}, bf16[528,128]{1,0:T(8,128)(2,1)S(1)}, u32[]{:S(2)}, u32[]{:S(2)}) collective-permute-start(bf16[528,128]{1,0:T(8,128)(2,1)S(1)} %copy-done.15), channel_id=1, source_target_pairs={{0,24},{8,0},{16,8},{24,16},{32,56},{40,32},{48,40},{56,48},{64,88... | collective-permute-start | bytes 405512 | tf_op jit(solution)/shard_map/ppermute | solution.py:638
  25.7 8.4 %collective-permute-start.5 = (bf16[528,128]{1,0:T(8,128)(2,1)S(1)}, bf16[528,128]{1,0:T(8,128)(2,1)S(1)}, u32[]{:S(2)}, u32[]{:S(2)}) collective-permute-start(bf16[528,128]{1,0:T(8,128)(2,1)S(1)} %row_totals.1.refs_4_), channel_id=1, source_target_pairs={{0,96},{8,104},{16,112},{24,120},{32,0},{40,8},{48,16},{56,24},{64... | collective-permute-start | bytes 405512 | tf_op jit(solution)/shard_map/ppermute | solution.py:643
  28.6 7.8 %collective-permute-start.4 = (bf16[528,128]{1,0:T(8,128)(2,1)S(1)}, bf16[528,128]{1,0:T(8,128)(2,1)S(1)}, u32[]{:S(2)}, u32[]{:S(2)}) collective-permute-start(bf16[528,128]{1,0:T(8,128)(2,1)S(1)} %row_totals.1.refs_4_), channel_id=1, source_target_pairs={{0,64},{8,72},{16,80},{24,88},{32,96},{40,104},{48,112},{56,120},{... | collective-permute-start | bytes 405512 | tf_op jit(solution)/shard_map/ppermute | solution.py:643
  29.4 8.5 %collective-permute-start.3 = (bf16[528,128]{1,0:T(8,128)(2,1)S(1)}, bf16[528,128]{1,0:T(8,128)(2,1)S(1)}, u32[]{:S(2)}, u32[]{:S(2)}) collective-permute-start(bf16[528,128]{1,0:T(8,128)(2,1)S(1)} %row_totals.1.refs_4_), channel_id=1, source_target_pairs={{0,32},{8,40},{16,48},{24,56},{32,64},{40,72},{48,80},{56,88},{64,... | collective-permute-start | bytes 405512 | tf_op jit(solution)/shard_map/ppermute | solution.py:643
  39.8 17.2 %copy-start.1 = (bf16[768,128]{1,0:T(8,128)(2,1)}, bf16[768,128]{1,0:T(8,128)(2,1)S(1)}, u32[]{:S(2)}) copy-start(bf16[768,128]{1,0:T(8,128)(2,1)S(1)} %get-tuple-element.40.refs_0_) | copy-start | bytes 589828
  39.9 8.4 %collective-permute-start.6 = (bf16[768,128]{1,0:T(8,128)(2,1)}, bf16[768,128]{1,0:T(8,128)(2,1)S(1)}, u32[]{:S(2)}, u32[]{:S(2)}) collective-permute-start(bf16[768,128]{1,0:T(8,128)(2,1)} %get-tuple-element.37), channel_id=1, source_target_pairs={{0,8},{8,16},{16,24},{24,0},{32,40},{40,48},{48,56},{56,32},{64,72... | collective-permute-start | bytes 589832 | tf_op jit(solution)/shard_map/ppermute | solution.py:638
  40.7 11.8 %collective-permute-start.7 = (bf16[768,128]{1,0:T(8,128)(2,1)S(1)}, bf16[768,128]{1,0:T(8,128)(2,1)S(1)}, u32[]{:S(2)}, u32[]{:S(2)}) collective-permute-start(bf16[768,128]{1,0:T(8,128)(2,1)S(1)} %get-tuple-element.38), channel_id=1, source_target_pairs={{0,16},{8,24},{16,0},{24,8},{32,48},{40,56},{48,32},{56,40},{64,80... | collective-permute-start | bytes 589832 | tf_op jit(solution)/shard_map/ppermute | solution.py:638
  43.6 9.0 %collective-permute-start.8 = (bf16[768,128]{1,0:T(8,128)(2,1)S(1)}, bf16[768,128]{1,0:T(8,128)(2,1)S(1)}, u32[]{:S(2)}, u32[]{:S(2)}) collective-permute-start(bf16[768,128]{1,0:T(8,128)(2,1)S(1)} %get-tuple-element.39), channel_id=1, source_target_pairs={{0,24},{8,0},{16,8},{24,16},{32,56},{40,32},{48,40},{56,48},{64,88... | collective-permute-start | bytes 589832 | tf_op jit(solution)/shard_map/ppermute | solution.py:638
  45.4 1.3 %copy-start = (bf16[16,256,256]{2,1,0:T(8,128)(2,1)}, bf16[16,256,256]{2,1,0:T(8,128)(2,1)S(1)}, u32[]{:S(2)}) copy-start(bf16[16,256,256]{2,1,0:T(8,128)(2,1)S(1)} %order_pages.1) | copy-start | bytes 6291460
  46.8 10.3 %copy-start.10 = (f32[128]{0:T(128)S(1)}, f32[128]{0:T(128)}, u32[]{:S(2)}) copy-start(f32[128]{0:T(128)} %param.19) | copy-start | bytes 1540
  46.8 10.3 %copy-start.12 = (f32[128]{0:T(128)S(1)}, f32[128]{0:T(128)}, u32[]{:S(2)}) copy-start(f32[128]{0:T(128)} %param.20) | copy-start | bytes 1540
  46.8 10.3 %copy-start.13 = (bf16[1,4,32]{2,1,0:T(4,128)(2,1)S(1)}, bf16[1,4,32]{2,1,0:T(4,128)(2,1)}, u32[]{:S(2)}) copy-start(bf16[1,4,32]{2,1,0:T(4,128)(2,1)} %maps_ref.1) | copy-start | bytes 772
  48.2 10.5 %copy-start.2 = (bf16[768,128]{1,0:T(8,128)(2,1)}, bf16[768,128]{1,0:T(8,128)(2,1)S(1)}, u32[]{:S(2)}) copy-start(bf16[768,128]{1,0:T(8,128)(2,1)S(1)} %collective-permute-done.6.refs_1_) | copy-start | bytes 589828
  52.6 6.1 %copy-start.3 = (bf16[768,128]{1,0:T(8,128)(2,1)}, bf16[768,128]{1,0:T(8,128)(2,1)S(1)}, u32[]{:S(2)}) copy-start(bf16[768,128]{1,0:T(8,128)(2,1)S(1)} %collective-permute-done.7.refs_2_) | copy-start | bytes 589828
  52.6 6.1 %copy-start.4 = (bf16[768,128]{1,0:T(8,128)(2,1)}, bf16[768,128]{1,0:T(8,128)(2,1)S(1)}, u32[]{:S(2)}) copy-start(bf16[768,128]{1,0:T(8,128)(2,1)S(1)} %collective-permute-done.8.refs_3_) | copy-start | bytes 589828
  52.6 33.7 %all-to-all-start.1 = ((bf16[16,256,256]{2,1,0:T(8,128)(2,1)}), bf16[16,256,256]{2,1,0:T(8,128)(2,1)}, u32[]{:S(2)}, u32[]{:S(2)}) async-start(bf16[16,256,256]{2,1,0:T(8,128)(2,1)} %copy-done), calls=%async_computation.1 | async-start | bytes 4194304 | tf_op jit(solution)/shard_map/all_to_all | solution.py:662
  57.0 9.2 %copy-start.14 = (bf16[1024]{0:T(1024)(128)(2,1)S(1)}, bf16[1024]{0:T(1024)(128)(2,1)}, u32[]{:S(2)}) copy-start(bf16[1024]{0:T(1024)(128)(2,1)} %param.29) | copy-start | bytes 6148
  58.7 1.8 %collective-permute-start.9 = (f32[4,24,1024]{2,1,0:T(8,128)S(1)}, f32[4,24,1024]{2,1,0:T(8,128)S(1)}, u32[]{:S(2)}, u32[]{:S(2)}) collective-permute-start(f32[4,24,1024]{2,1,0:T(8,128)S(1)} %get-tuple-element.47), channel_id=1, source_target_pairs={{0,1},{1,0},{2,3},{3,2},{4,5},{5,4},{6,7},{7,6},{8,9},{9,8},{10,11... | collective-permute-start | bytes 1179656 | tf_op jit(solution)/shard_map/ppermute | solution.py:664
  61.1 19.3 %collective-permute-start.10 = (f32[24,1024]{1,0:T(8,128)S(1)}, f32[24,1024]{1,0:T(8,128)S(1)}, u32[]{:S(2)}, u32[]{:S(2)}) collective-permute-start(f32[24,1024]{1,0:T(8,128)S(1)} %get-tuple-element.49), channel_id=1, source_target_pairs={{0,2},{1,3},{2,4},{3,5},{4,6},{5,7},{6,0},{7,1},{8,10},{9,11},{10,... | collective-permute-start | bytes 294920 | tf_op jit(solution)/shard_map/ppermute | solution.py:633
  62.1 18.3 %collective-permute-start.11 = (f32[24,1024]{1,0:T(8,128)S(1)}, f32[24,1024]{1,0:T(8,128)S(1)}, u32[]{:S(2)}, u32[]{:S(2)}) collective-permute-start(f32[24,1024]{1,0:T(8,128)S(1)} %get-tuple-element.50), channel_id=1, source_target_pairs={{0,4},{1,5},{2,6},{3,7},{4,0},{5,1},{6,2},{7,3},{8,12},{9,13},{10,... | collective-permute-start | bytes 294920 | tf_op jit(solution)/shard_map/ppermute | solution.py:633
  64.8 15.6 %collective-permute-start.12 = (f32[24,1024]{1,0:T(8,128)S(1)}, f32[24,1024]{1,0:T(8,128)S(1)}, u32[]{:S(2)}, u32[]{:S(2)}) collective-permute-start(f32[24,1024]{1,0:T(8,128)S(1)} %get-tuple-element.51), channel_id=1, source_target_pairs={{0,6},{1,7},{2,0},{3,1},{4,2},{5,3},{6,4},{7,5},{8,14},{9,15},{10,... | collective-permute-start | bytes 294920 | tf_op jit(solution)/shard_map/ppermute | solution.py:633
  66.3 20.1 %copy-start.7 = (s32[16,16]{1,0:T(8,128)S(1)}, s32[16,16]{1,0:T(8,128)}, u32[]{:S(2)}) copy-start(s32[16,16]{1,0:T(8,128)} %slot_ref.1) | copy-start | bytes 3076
  66.3 20.1 %copy-start.8 = (bf16[1,4,1024]{2,1,0:T(4,128)(2,1)S(1)}, bf16[1,4,1024]{2,1,0:T(4,128)(2,1)}, u32[]{:S(2)}) copy-start(bf16[1,4,1024]{2,1,0:T(4,128)(2,1)} %q_ref.1) | copy-start | bytes 24580
  66.3 20.0 %copy-start.9 = (s32[16]{0:T(128)S(1)}, s32[16]{0:T(128)}, u32[]{:S(2)}) copy-start(s32[16]{0:T(128)} %len_ref.5) | copy-start | bytes 196
  66.3 20.0 %copy-start.11 = (bf16[1,4,256]{2,1,0:T(4,128)(2,1)S(1)}, bf16[1,4,256]{2,1,0:T(4,128)(2,1)}, u32[]{:S(2)}) copy-start(bf16[1,4,256]{2,1,0:T(4,128)(2,1)} %fresh_ref.1) | copy-start | bytes 6148

commit v3 on v2

--- a/solution.py
+++ b/solution.py
@@ -26,6 +26,7 @@
 F32 = jnp.float32
 BF16 = jnp.bfloat16
 MIB = 1024 * 1024
+KV_PARTS = 2
 highest = lax.Precision.HIGHEST
 ANY = pl.BlockSpec(memory_space=pl.ANY)
 VM = pl.BlockSpec(memory_space=pltpu.VMEM)
@@ -58,7 +59,7 @@
 
 def split_start(kv, x_hbm, z_hbm, dt_hbm, out, buf, x_buf, z_buf, dt_buf, rows, sem, out_sem):
     small = fetch([(x_hbm.at[0], x_buf), (z_hbm.at[0], z_buf), (dt_hbm.at[0], dt_buf)], sem, 2 * TP)
-    parts = [(i, pl.ds(q * BLK // 4, BLK // 4)) for i in range(2) for q in range(4)]
+    parts = [(i, pl.ds(q * BLK // KV_PARTS, BLK // KV_PARTS)) for i in range(2) for q in range(KV_PARTS)]
     arrive = fetch([(kv.at[part], buf.at[part]) for part in parts], sem)
 
     def fold(part):
@@ -76,7 +77,7 @@
         rows[32:, :] = steps.astype(BF16)
         leave = fetch([(rows, out.at[h, pl.ds(DEC_X, 48), :]) for h in range(TP)], out_sem)
         for i in range(2):
-            for c in arrive[4 * i : 4 * i + 4]:
+            for c in arrive[KV_PARTS * i : KV_PARTS * (i + 1)]:
                 c.wait()
             heads = [(h, pl.ds(h * 2 * HD, 2 * HD)) for h in range(TP)]
             leave += fetch(
@@ -134,8 +135,11 @@
         refs[ROW + 9 :],
     )
     small = fetch([(dt_hbm, dt_ref), (bc_hbm, bc_ref), (rate_hbm, rate_ref)], sem, 2 * STEPS)
+    x_copies = block_copies(x_hbm, x_buf, sem)
+    for c in x_copies[:STEPS]:
+        c.start()
     finish = split_start(kv, dx_hbm, dz_hbm, ddt_hbm, split, *rest)
-    for c in block_copies(x_hbm, x_buf, sem):
+    for c in x_copies[STEPS:]:
         c.start()
     for c in small:
         c.wait()
@@ -174,8 +178,7 @@
 
         lax.fori_loop(0, STEPS, body, 0)
     y = lax.rem(lax.axis_index("seq"), ROW)
-    for o in range(ROW):
-        outs[o][...] = stage[lax.rem(y + o, ROW)]
+    leave += fetch([(stage.at[lax.rem(y + o, ROW)], outs[o]) for o in range(ROW)], sem, 2 * STEPS)
     for c in leave:
         c.wait()
 
@@ -186,7 +189,7 @@
         out_shape=[jax.ShapeDtypeStruct((STATE_ROWS + NS, LANE), BF16)] * ROW
         + [jax.ShapeDtypeStruct((TP, PAGE_ROWS, 2 * HD), BF16)],
         in_specs=[SM] + [ANY] * 8,
-        out_specs=[VM] * ROW + [ANY],
+        out_specs=[ANY] * (ROW + 1),
         scratch_shapes=[
             pltpu.VMEM((ROW, STATE_ROWS + NS, LANE), BF16),
             pltpu.VMEM((2, HEADS, BLK), F32),
@@ -195,7 +198,7 @@
             pltpu.VMEM((2, BLK, HEADS), BF16),
             pltpu.VMEM((2, 2 * NS, BLK), BF16),
             pltpu.VMEM((1, HEADS), F32),
-            pltpu.SemaphoreType.DMA((2 * STEPS + 3,)),
+            pltpu.SemaphoreType.DMA((2 * STEPS + ROW,)),
             pltpu.VMEM((2, BLK, TP * 2 * HD), BF16),
             pltpu.VMEM((4, WC), BF16),
             pltpu.VMEM((4, WC), BF16),
@@ -242,17 +245,8 @@
             half = decay_of(wide, b, p, c)
             state = half * (half * state + scr[b, at : at + NS, :].astype(F32))
         out[at : at + NS, :] = state.astype(BF16)
-    compact = [scr[b, STATE_ROWS:, :].astype(F32) for b in range(ROW)]
-    row = lax.broadcasted_iota(jnp.int32, (NS, LANE), 0)
-    dec = jnp.zeros((NS, LANE), F32)
-    for p in range(2):
-        all_rows = jnp.ones((1, LANE), F32)
-        for b in range(ROW):
-            half = compact[b][p : p + 1, :] + compact[b][2 + p : 3 + p, :]
-            all_rows = all_rows * (half * half)
-        high, low = halves(all_rows)
-        dec = jnp.where(row == p, high.astype(F32), jnp.where(row == 2 + p, low.astype(F32), dec))
-    out[STATE_ROWS:, :] = dec.astype(BF16)
+    once = [scr[b, STATE_ROWS:, :].astype(F32) for b in range(ROW)]
+    out[STATE_ROWS:, :] = compact_decays(once + once)
 
 
 def row_totals(blocks):
@@ -268,24 +262,65 @@
     )(*blocks)
 
 
-def enter_kernel(group_ref, *refs):
-    blocks, totals, outs = refs[:ROW], refs[ROW : 2 * ROW], refs[2 * ROW : 3 * ROW]
-    scr, rows, start, stage = refs[3 * ROW :]
+def compact_decays(parts):
+    row = lax.broadcasted_iota(jnp.int32, (NS, LANE), 0)
+    dec = jnp.zeros((NS, LANE), F32)
+    for p in range(2):
+        product = jnp.ones((1, LANE), F32)
+        for part in parts:
+            product = product * (part[p : p + 1, :] + part[2 + p : 3 + p, :])
+        high, low = halves(product)
+        dec = jnp.where(row == p, high.astype(F32), jnp.where(row == 2 + p, low.astype(F32), dec))
+    return dec.astype(BF16)
+
+
+def place_pair(own, near, scratch, x):
+    scratch[lax.rem(x, 2)] = own[...]
+    scratch[1 - lax.rem(x, 2)] = near[...]
+
+
+def pair_kernel(own, near, out, rows):
+    me = lax.axis_index("seq")
+    x, y = lax.div(me, ROW), lax.rem(me, ROW)
+    place_pair(own, near, rows, x)
+    wide = spread_decays([rows[1, STATE_ROWS:, :]], y)
+    for p, c, at in groups():
+        first, second = (rows[b, at : at + NS, :].astype(F32) for b in range(2))
+        out[at : at + NS, :] = (decay_of(wide, 0, p, c) * first + second).astype(BF16)
+    out[STATE_ROWS:, :] = compact_decays([rows[b, STATE_ROWS:, :].astype(F32) for b in range(2)])
+
+
+def pair_totals(own, near):
+    return pl.pallas_call(
+        pair_kernel,
+        out_shape=jax.ShapeDtypeStruct((STATE_ROWS + NS, LANE), BF16),
+        in_specs=[VM] * 2,
+        out_specs=VM,
+        scratch_shapes=[pltpu.VMEM((2, STATE_ROWS + NS, LANE), BF16)],
+        cost_estimate=cost(1),
+        compiler_params=params(),
+        name="pair_totals",
+    )(own, near)
+
+
+def enter_kernel(group_ref, own, near, far, *refs):
+    blocks, outs = refs[:ROW], refs[ROW : 2 * ROW]
+    scr, rows, final, stage = refs[2 * ROW :]
     me = lax.axis_index("seq")
     x, y = lax.div(me, ROW), lax.rem(me, ROW)
     place(blocks, scr, y)
-    place(totals, rows, x)
-    wide = spread_decays(
-        [scr[b, STATE_ROWS:, :] for b in range(ROW)] + [rows[b, STATE_ROWS:, :] for b in range(ROW)], y
-    )
+    place_pair(own, near, rows, x)
+    ends = [rows[0, STATE_ROWS:, :], rows[1, STATE_ROWS:, :], far[STATE_ROWS:, :]]
+    wide = spread_decays([scr[b, STATE_ROWS:, :] for b in range(ROW)] + ends + ends[:1], y)
+    late, odd = x >= 2, lax.rem(x, 2) == 1
     for p, c, at in groups():
-        state = jnp.zeros((NS, LANE), F32)
-        for b in range(ROW):
-            start[b, at : at + NS, :] = state
-            state = decay_of(wide, ROW + b, p, c) * state + rows[b, at : at + NS, :].astype(F32)
-        start[ROW, at : at + NS, :] = state
-    for p, c, at in groups():
-        state = start[x, at : at + NS, :]
+        first, second = (rows[b, at : at + NS, :].astype(F32) for b in range(2))
+        other = far[at : at + NS, :].astype(F32)
+        before = jnp.where(late, other, 0.0)
+        middle = decay_of(wide, ROW, p, c) * before + first
+        after = decay_of(wide, ROW + 1, p, c) * middle + second
+        final[at : at + NS, :] = jnp.where(late, after, decay_of(wide, ROW + 2, p, c) * after + other)
+        state = jnp.where(odd, middle, before)
         for b in range(ROW):
             half = decay_of(wide, b, p, c)
             entering = half * state
@@ -294,28 +329,28 @@
     second = group_ref[lax.axis_index("tp") * 2 + 1]
     for b in range(ROW):
         at = jnp.where(second == x * ROW + b, FINAL_ROWS, 0)
-        final = start[ROW, pl.ds(pl.multiple_of(at, FINAL_ROWS), FINAL_ROWS), :]
-        stage[b, STATE_ROWS:, :] = final.astype(BF16)
+        chosen = final[pl.ds(pl.multiple_of(at, FINAL_ROWS), FINAL_ROWS), :]
+        stage[b, STATE_ROWS:, :] = chosen.astype(BF16)
     for o in range(ROW):
         outs[o][...] = stage[lax.rem(y + o, ROW)]
 
 
-def enter_states(group_of, blocks, totals):
+def enter_states(group_of, own, near, far, blocks):
     return pl.pallas_call(
         enter_kernel,
         out_shape=[jax.ShapeDtypeStruct((STATE_ROWS + FINAL_ROWS, LANE), BF16)] * ROW,
-        in_specs=[SM] + [VM] * (2 * ROW),
+        in_specs=[SM] + [VM] * (3 + ROW),
         out_specs=[VM] * ROW,
         scratch_shapes=[
             pltpu.VMEM((ROW, STATE_ROWS + NS, LANE), BF16),
-            pltpu.VMEM((ROW, STATE_ROWS + NS, LANE), BF16),
-            pltpu.VMEM((ROW + 1, STATE_ROWS, LANE), F32),
+            pltpu.VMEM((2, STATE_ROWS + NS, LANE), BF16),
+            pltpu.VMEM((STATE_ROWS, LANE), F32),
             pltpu.VMEM((ROW, STATE_ROWS + FINAL_ROWS, LANE), BF16),
         ],
         cost_estimate=cost(2),
         compiler_params=params(),
         name="enter_states",
-    )(group_of, *blocks, *totals)
+    )(group_of, own, near, far, *blocks)
 
 
 def order_kernel(group_ref, pages, out):
@@ -424,7 +459,7 @@
             pltpu.SemaphoreType.DMA((2 * STEPS,)),
         ],
         cost_estimate=cost(12),
-        compiler_params=params(60),
+        compiler_params=params(54),
         name="block_outputs",
     )(lengths, x_in, dt_raw, bc_in, rate, skip, *entering)
 
@@ -438,14 +473,25 @@
 
 
 def attend_kernel(
-    group_ref, len_ref, slot_ref, recv, q_ref, fresh_ref, pool, out_ref, zeros, sem
+    table, recv, q_ref, fresh_ref, gain_ref, *refs
 ):
-    prompt = my_prompt(group_ref)
-    length = len_ref[prompt]
+    results, (pool, *outs), scratch = refs[:ROW], refs[ROW : ROW + 4], refs[ROW + 4 :]
+    zeros, best, out_ref, mamba_ref, out_sem, sem = scratch
+    prompt = my_prompt(table)
+    length = table[SEQ + prompt]
+    distance = lax.rem(lax.div(lax.axis_index("tp"), 2) + ROW - lax.div(prompt, 4), ROW)
+    for o in range(ROW):
+
+        @pl.when(distance == o)
+        def _():
+            best[...] = results[o][...]
+
+    mamba_ref[0] = (best[NS : NS + 4, :] * gain_ref[...].astype(F32)).astype(BF16)
+    ends = fetch([(best.at[pl.ds(0, NS), :], outs[1].at[0]), (mamba_ref, outs[2])], out_sem)
     zeros[...] = jnp.zeros(zeros.shape, BF16)
 
     def page_copy(s, live):
-        at = pl.ds(pl.multiple_of(slot_ref[prompt, s] * BLK, BLK), BLK)
+        at = pl.ds(pl.multiple_of(table[(2 + prompt) * SEQ + s] * BLK, BLK), BLK)
         source = recv.at[s] if live else zeros
         return pltpu.make_async_copy(source, pool.at[0, at, :], sem.at[s])
 
@@ -487,24 +533,36 @@
     steps = out_ref.shape[1]
     for h in range(q.shape[0] // steps):
         out_ref[0, :, h * HD : (h + 1) * HD] = result[h * steps : (h + 1) * steps].astype(BF16)
+    ends += fetch([(out_ref, outs[0])], out_sem, 2)
     for s in range(SEQ):
         page_copy(s, True).wait()
-
-
-def attend(group_of, lengths, slot_of, recv, queries, fresh):
+    for c in ends:
+        c.wait()
+
+
+def attend(table, recv, queries, fresh, gain, results):
     return pl.pallas_call(
         attend_kernel,
         out_shape=[
             jax.ShapeDtypeStruct((1, SEQ * BLK, 2 * HD), BF16),
             jax.ShapeDtypeStruct((1, 4, WC), BF16),
+            jax.ShapeDtypeStruct((1, NS, WC), F32),
+            jax.ShapeDtypeStruct((1, 4, WC), BF16),
         ],
-        in_specs=[SM, SM, SM, VM, VM, VM],
-        out_specs=[ANY, VM],
-        scratch_shapes=[pltpu.VMEM((BLK, 2 * HD), BF16), pltpu.SemaphoreType.DMA((SEQ,))],
+        in_specs=[SM] + [VM] * (4 + ROW),
+        out_specs=[ANY] * 4,
+        scratch_shapes=[
+            pltpu.VMEM((BLK, 2 * HD), BF16),
+            pltpu.VMEM((NS + 8, WC), F32),
+            pltpu.VMEM((1, 4, WC), BF16),
+            pltpu.VMEM((1, 4, WC), BF16),
+            pltpu.SemaphoreType.DMA((3,)),
+            pltpu.SemaphoreType.DMA((SEQ,)),
+        ],
         cost_estimate=cost(5),
-        compiler_params=params(),
+        compiler_params=params(54),
         name="attend",
-    )(group_of, lengths, slot_of, recv, queries, fresh)
+    )(table, recv, queries, fresh, gain, *results)
 
 
 def decode_kernel(inputs, maps_ref, rate_ref, skip_ref, *refs):
@@ -601,33 +659,6 @@
     )(group_of, own, other)
 
 
-def pick_kernel(group_ref, gain_ref, *refs):
-    results, (state_ref, out_ref) = refs[:ROW], refs[ROW:]
-    holder = lax.div(my_prompt(group_ref), 4)
-    distance = lax.rem(lax.div(lax.axis_index("tp"), 2) + ROW - holder, ROW)
-    for o in range(ROW):
-
-        @pl.when(distance == o)
-        def _():
-            state_ref[0] = results[o][:NS, :]
-            out_ref[0] = (results[o][NS : NS + 4, :] * gain_ref[...].astype(F32)).astype(BF16)
-
-
-def pick(group_of, gain, results):
-    return pl.pallas_call(
-        pick_kernel,
-        out_shape=[
-            jax.ShapeDtypeStruct((1, NS, WC), F32),
-            jax.ShapeDtypeStruct((1, 4, WC), BF16),
-        ],
-        in_specs=[SM] + [VM] * (1 + ROW),
-        out_specs=[VM] * 2,
-        cost_estimate=cost(1),
-        compiler_params=params(),
-        name="pick",
-    )(group_of, gain, *results)
-
-
 def along_z(arrays):
     moves = [[(i, (i + 2 * o) % TP) for i in range(TP)] for o in range(ROW)]
     return [arrays[0]] + [lax.ppermute(arrays[o], "tp", moves[o]) for o in range(1, ROW)]
@@ -635,11 +666,6 @@
 
 def along_y(arrays):
     moves = [[(x * ROW + y, x * ROW + (y + o) % ROW) for x in range(ROW) for y in range(ROW)] for o in range(ROW)]
-    return [arrays[0]] + [lax.ppermute(arrays[o], "seq", moves[o]) for o in range(1, ROW)]
-
-
-def along_x(arrays):
-    moves = [[(i, (i + o * ROW) % SEQ) for i in range(SEQ)] for o in range(ROW)]
     return [arrays[0]] + [lax.ppermute(arrays[o], "seq", moves[o]) for o in range(1, ROW)]
 
 
@@ -651,21 +677,26 @@
     skip = skip_gain.reshape(1, HEADS)
     gain = norm_gain.reshape(1, -1)
     maps = jnp.swapaxes(bc_in, 1, 2)
+    table = jnp.concatenate([group_of, lengths, slot_of.reshape(-1)])
 
     *local, sent = local_states(lengths, x_in, dt_raw, maps, rate, kv_pre, dec_x, dec_z, dec_dt)
     pages = lax.all_to_all(sent, "tp", split_axis=0, concat_axis=0, tiled=True)
     blocks = along_y(local)
-    totals = along_x([row_totals(blocks)] * ROW)
-    pages, unused = lax.optimization_barrier((pages, totals))
-    entering = along_y(enter_states(group_of, blocks, totals))
+    own = row_totals(blocks)
+    near = lax.ppermute(own, "seq", [(i, i ^ ROW) for i in range(SEQ)])
+    across = [(x * ROW + y, (ROW - 1 - x) * ROW + y) for x in range(ROW) for y in range(ROW)]
+    far = lax.ppermute(pair_totals(own, near), "seq", across)
+    pages, unused = lax.optimization_barrier((pages, far))
+    entering = along_y(enter_states(group_of, own, near, far, blocks))
     ordered, entering = lax.optimization_barrier((order_pages(group_of, pages), entering))
     recv = lax.all_to_all(ordered, "seq", split_axis=0, concat_axis=0, tiled=True)
     own, other = decode(pages, dec_bc, rate, skip, entering)
     other = lax.ppermute(other, "tp", [(i, i ^ 1) for i in range(TP)])
     results = along_z(choose_side(group_of, own, other))
-    dec_state, dec_mamba = pick(group_of, gain, results)
     y_pre = block_outputs(lengths, x_in, dt_raw, maps, rate, skip, entering)
-    kv_pool, dec_attn = attend(group_of, lengths, slot_of, recv, dec_q, dec_kv)
+    kv_pool, dec_attn, dec_state, dec_mamba = attend(
+        table, recv, dec_q, dec_kv, gain, results
+    )
     return (y_pre, kv_pool, dec_mamba, dec_state, dec_attn)
 
 

time: 91 us -> 88.3 us (0.970)
  waiting for transfers between devices: 25.2 us -> 19.8 us
  starting transfers between devices: 30.5 us -> 32.2 us
  local copies, waits for them, and re-layouts: 1.4 us -> 2.71 us
    all_to_all x1, waiting for transfers between devices: 4.67 us -> 2.12 us  [shards(): lax.all_to_all(ordered, 'seq', split_axis=0, concat_axis=0, tiled=True)]
    ppermute x6, waiting for transfers between devices: 11.3 us -> 9.35 us  [along_y(): lax.ppermute(arrays[o], 'seq', moves[o])]
    all_to_all x1, starting transfers between devices: 4.45 us -> 6.02 us  [shards(): lax.all_to_all(ordered, 'seq', split_axis=0, concat_axis=0, tiled=True)]
    pallas_call x1, Pallas kernels: 1.23 us -> 0.26 us  [pair_totals(): pl.pallas_call(pair_kernel, out_shape=jax.ShapeDtypeStruct((STATE_ROWS +...]
    unnamed x36 -> x40, local copies, waits for them, and re-layouts: 1.39 us -> 2.03 us
    ppermute x3 -> x2, waiting for transfers between devices: 7.58 us -> 7.13 us  [the longest x1 3.66 us: shards(): near = lax.ppermute(own, 'seq', [(i, i ^ ROW) for i in range(SEQ)])]
    ppermute x3 -> x2, starting transfers between devices: 4.51 us -> 4.4 us  [the longest x1 2.83 us: shards(): far = lax.ppermute(pair_totals(own, near), 'seq', across)]
  transfers between devices with their start and end apart: 15 -> 14, of which waited for: 9 -> 8; matrix products, arithmetic and copies ran while one was open for 0% -> 2% of each run, Pallas kernels for 23% -> 23%
where the time goes in v3:
time: 88.3 us; the launch traced here: 88 us
  starting transfers between devices  32.2 us (36%)
  Pallas kernels  31.7 us (36%)
  waiting for transfers between devices  19.8 us (22%)
  local copies, waits for them, and re-layouts  2.71 us (3%)
  between operations  0.89 us (1%)
    pallas_call x1, Pallas kernels, block_outputs(): pl.pallas_call(output_kernel, out_shape=jax.ShapeDtypeStruct((2, BLK, WID...  13.9 us
    ppermute x6, starting transfers between devices, along_y(): lax.ppermute(arrays[o], 'seq', moves[o])  11 us
    ppermute x6, waiting for transfers between devices, along_y(): lax.ppermute(arrays[o], 'seq', moves[o])  9.35 us
    pallas_call x1, Pallas kernels, local_states(): pl.pallas_call(local_kernel, out_shape=[jax.ShapeDtypeStruct((STATE_ROWS...  7.73 us
    all_to_all x1, starting transfers between devices, shards(): lax.all_to_all(ordered, 'seq', split_axis=0, concat_axis=0, tiled=True)  6.02 us
    all_to_all x1, starting transfers between devices, shards(): pages = lax.all_to_all(sent, 'tp', split_axis=0, concat_axis=0, tiled=True)  5.54 us
    ppermute x3, starting transfers between devices, along_z(): lax.ppermute(arrays[o], 'tp', moves[o])  5.19 us
    pallas_call x1, Pallas kernels, attend(): pl.pallas_call(attend_kernel, out_shape=[jax.ShapeDtypeStruct((1, SEQ * B...  3.92 us
  transfers between devices with their start and end apart: 14, of which 8 were waited for; matrix products, arithmetic and copies ran while one was open for 2% of the time, Pallas kernels for 23%

profile of v3, /device:TPU:0, one launch (start us, length us, event | category | flops | bytes accessed | tf_op | source)
XLA Modules:
  0.0 88.0 jit_solution(9240903317488620793)
XLA Ops:
  0.6 7.7 %local_states.1 = (bf16[528,128]{1,0:T(8,128)(2,1)}, bf16[528,128]{1,0:T(8,128)(2,1)}, bf16[528,128]{1,0:T(8,128)(2,1)}, bf16[528,128]{1,0:T(8,128)(2,1)}, bf16[8,560,256]{2,1,0:T(8,128)(2,1)}) custom-call(s32[16]{0:T(128)} %len_ref.3, bf16[2,256,8192]{2,1,0:T(8,128)(2,1)} %x_hbm.3, bf16[2,256,128]{2,1,0:T(8,128)(2,1)} %dt_hbm.3, ...), custom_call_target="tpu_custom_call" | custom-call | bytes 18000000 | tf_op jit(solution)/shard_map/local_states/pallas_call | solution.py:187
  8.4 0.0 copy-start.5
  8.4 0.0 copy-start.7
  8.4 5.5 %all-to-all-start = ((bf16[8,560,256]{2,1,0:T(8,128)(2,1)}), bf16[8,560,256]{2,1,0:T(8,128)(2,1)S(1)}, u32[]{:S(2)}, u32[]{:S(2)}) async-start(bf16[8,560,256]{2,1,0:T(8,128)(2,1)} %get-tuple-element.30), calls=%async_computation | async-start | bytes 4587520 | tf_op jit(solution)/shard_map/all_to_all | solution.py:683
  14.0 1.6 %collective-permute-start = (bf16[528,128]{1,0:T(8,128)(2,1)S(1)}, bf16[528,128]{1,0:T(8,128)(2,1)S(1)}, u32[]{:S(2)}, u32[]{:S(2)}) collective-permute-start(bf16[528,128]{1,0:T(8,128)(2,1)S(1)} %copy-done.19), channel_id=1, source_target_pairs={{0,8},{8,16},{16,24},{24,0},{32,40},{40,48},{48,56},{56,32},{64,72... | collective-permute-start | bytes 405512 | tf_op jit(solution)/shard_map/ppermute | solution.py:669
  15.6 2.9 %collective-permute-start.1 = (bf16[528,128]{1,0:T(8,128)(2,1)S(1)}, bf16[528,128]{1,0:T(8,128)(2,1)S(1)}, u32[]{:S(2)}, u32[]{:S(2)}) collective-permute-start(bf16[528,128]{1,0:T(8,128)(2,1)S(1)} %copy-done.18), channel_id=1, source_target_pairs={{0,16},{8,24},{16,0},{24,8},{32,48},{40,56},{48,32},{56,40},{64,80... | collective-permute-start | bytes 405512 | tf_op jit(solution)/shard_map/ppermute | solution.py:669
  18.5 1.3 %collective-permute-start.2 = (bf16[528,128]{1,0:T(8,128)(2,1)S(1)}, bf16[528,128]{1,0:T(8,128)(2,1)S(1)}, u32[]{:S(2)}, u32[]{:S(2)}) collective-permute-start(bf16[528,128]{1,0:T(8,128)(2,1)S(1)} %copy-done.17), channel_id=1, source_target_pairs={{0,24},{8,0},{16,8},{24,16},{32,56},{40,32},{48,40},{56,48},{64,88... | collective-permute-start | bytes 405512 | tf_op jit(solution)/shard_map/ppermute | solution.py:669
  19.9 1.4 %collective-permute-done.refs_1_ = bf16[528,128]{1,0:T(8,128)(2,1)S(1)} collective-permute-done((bf16[528,128]{1,0:T(8,128)(2,1)S(1)}, bf16[528,128]{1,0:T(8,128)(2,1)S(1)}, u32[]{:S(2)}, u32[]{:S(2)}) %collective-permute-start) | collective-permute-done | bytes 135200 | tf_op jit(solution)/shard_map/ppermute | solution.py:669
  21.2 4.1 %collective-permute-done.1.refs_2_ = bf16[528,128]{1,0:T(8,128)(2,1)S(1)} collective-permute-done((bf16[528,128]{1,0:T(8,128)(2,1)S(1)}, bf16[528,128]{1,0:T(8,128)(2,1)S(1)}, u32[]{:S(2)}, u32[]{:S(2)}) %collective-permute-start.1) | collective-permute-done | bytes 135200 | tf_op jit(solution)/shard_map/ppermute | solution.py:669
  25.3 0.0 collective-permute-done.2.refs_3_
  25.3 0.3 row_totals.1.own
  25.7 1.6 %collective-permute-start.3 = (bf16[528,128]{1,0:T(8,128)(2,1)S(1)}, bf16[528,128]{1,0:T(8,128)(2,1)S(1)}, u32[]{:S(2)}, u32[]{:S(2)}) collective-permute-start(bf16[528,128]{1,0:T(8,128)(2,1)S(1)} %row_totals.1.own), channel_id=1, source_target_pairs={{0,32},{8,40},{16,48},{24,56},{32,0},{40,8},{48,16},{56,24},{64,96... | collective-permute-start | bytes 405512 | tf_op jit(solution)/shard_map/ppermute | solution.py:686
  27.3 3.7 %collective-permute-done.3.near = bf16[528,128]{1,0:T(8,128)(2,1)S(1)} collective-permute-done((bf16[528,128]{1,0:T(8,128)(2,1)S(1)}, bf16[528,128]{1,0:T(8,128)(2,1)S(1)}, u32[]{:S(2)}, u32[]{:S(2)}) %collective-permute-start.3) | collective-permute-done | bytes 135200 | tf_op jit(solution)/shard_map/ppermute | solution.py:686
  30.9 0.3 pair_totals.1
  31.2 2.8 %collective-permute-start.4 = (bf16[528,128]{1,0:T(8,128)(2,1)S(1)}, bf16[528,128]{1,0:T(8,128)(2,1)S(1)}, u32[]{:S(2)}, u32[]{:S(2)}) collective-permute-start(bf16[528,128]{1,0:T(8,128)(2,1)S(1)} %pair_totals.1), channel_id=1, source_target_pairs={{0,96},{8,104},{16,112},{24,120},{32,64},{40,72},{48,80},{56,88},{... | collective-permute-start | bytes 405512 | tf_op jit(solution)/shard_map/ppermute | solution.py:688
  34.0 3.5 %collective-permute-done.4.far = bf16[528,128]{1,0:T(8,128)(2,1)S(1)} collective-permute-done((bf16[528,128]{1,0:T(8,128)(2,1)S(1)}, bf16[528,128]{1,0:T(8,128)(2,1)S(1)}, u32[]{:S(2)}, u32[]{:S(2)}) %collective-permute-start.4) | collective-permute-done | bytes 135200 | tf_op jit(solution)/shard_map/ppermute | solution.py:688
  37.5 1.9 %enter_states.1 = (bf16[768,128]{1,0:T(8,128)(2,1)S(1)}, bf16[768,128]{1,0:T(8,128)(2,1)}, bf16[768,128]{1,0:T(8,128)(2,1)S(1)}, bf16[768,128]{1,0:T(8,128)(2,1)S(1)}) custom-call(s32[16]{0:T(128)S(1)} %copy-done.7, bf16[528,128]{1,0:T(8,128)(2,1)S(1)} %row_totals.1.own, bf16[528,128]{1,0:T(8,128)(2,1)S(1)} %collective-permute-done.3.near, ...), custom_call_target="tpu_custom_call" | custom-call | bytes 6000000 | tf_op jit(solution)/shard_map/enter_states/pallas_call | solution.py:339
  39.4 1.1 %collective-permute-start.5 = (bf16[768,128]{1,0:T(8,128)(2,1)}, bf16[768,128]{1,0:T(8,128)(2,1)S(1)}, u32[]{:S(2)}, u32[]{:S(2)}) collective-permute-start(bf16[768,128]{1,0:T(8,128)(2,1)} %get-tuple-element.37), channel_id=1, source_target_pairs={{0,8},{8,16},{16,24},{24,0},{32,40},{40,48},{48,56},{56,32},{64,72... | collective-permute-start | bytes 589832 | tf_op jit(solution)/shard_map/ppermute | solution.py:669
  40.5 2.7 %collective-permute-start.6 = (bf16[768,128]{1,0:T(8,128)(2,1)S(1)}, bf16[768,128]{1,0:T(8,128)(2,1)S(1)}, u32[]{:S(2)}, u32[]{:S(2)}) collective-permute-start(bf16[768,128]{1,0:T(8,128)(2,1)S(1)} %get-tuple-element.38), channel_id=1, source_target_pairs={{0,16},{8,24},{16,0},{24,8},{32,48},{40,56},{48,32},{56,40},{64,80... | collective-permute-start | bytes 589832 | tf_op jit(solution)/shard_map/ppermute | solution.py:669
  43.2 1.3 %collective-permute-start.7 = (bf16[768,128]{1,0:T(8,128)(2,1)S(1)}, bf16[768,128]{1,0:T(8,128)(2,1)S(1)}, u32[]{:S(2)}, u32[]{:S(2)}) collective-permute-start(bf16[768,128]{1,0:T(8,128)(2,1)S(1)} %get-tuple-element.39), channel_id=1, source_target_pairs={{0,24},{8,0},{16,8},{24,16},{32,56},{40,32},{48,40},{56,48},{64,88... | collective-permute-start | bytes 589832 | tf_op jit(solution)/shard_map/ppermute | solution.py:669
  44.5 0.0 all-to-all-done.pages.inputs
  44.5 0.7 order_pages.1
  45.2 0.0 copy-start
  45.2 1.3 %copy-done = bf16[16,256,256]{2,1,0:T(8,128)(2,1)} copy-done((bf16[16,256,256]{2,1,0:T(8,128)(2,1)}, bf16[16,256,256]{2,1,0:T(8,128)(2,1)S(1)}, u32[]{:S(2)}) %copy-start) | copy-done | bytes 2097176
  46.5 1.8 %collective-permute-done.5.refs_1_ = bf16[768,128]{1,0:T(8,128)(2,1)S(1)} collective-permute-done((bf16[768,128]{1,0:T(8,128)(2,1)}, bf16[768,128]{1,0:T(8,128)(2,1)S(1)}, u32[]{:S(2)}, u32[]{:S(2)}) %collective-permute-start.5) | collective-permute-done | bytes 196640 | tf_op jit(solution)/shard_map/ppermute | solution.py:669
  48.3 2.1 %collective-permute-done.6.refs_2_ = bf16[768,128]{1,0:T(8,128)(2,1)S(1)} collective-permute-done((bf16[768,128]{1,0:T(8,128)(2,1)S(1)}, bf16[768,128]{1,0:T(8,128)(2,1)S(1)}, u32[]{:S(2)}, u32[]{:S(2)}) %collective-permute-start.6) | collective-permute-done | bytes 196640 | tf_op jit(solution)/shard_map/ppermute | solution.py:669
  50.4 0.0 collective-permute-done.7.refs_3_
  50.4 6.0 %all-to-all-start.1 = ((bf16[16,256,256]{2,1,0:T(8,128)(2,1)}), bf16[16,256,256]{2,1,0:T(8,128)(2,1)}, u32[]{:S(2)}, u32[]{:S(2)}) async-start(bf16[16,256,256]{2,1,0:T(8,128)(2,1)} %copy-done), calls=%async_computation.1 | async-start | bytes 4194304 | tf_op jit(solution)/shard_map/all_to_all | solution.py:692
  56.4 0.0 copy-start.14
  56.4 0.0 copy-start.16
  56.5 0.0 copy-start.15
  56.5 2.3 %decode.1 = (f32[4,24,1024]{2,1,0:T(8,128)S(1)}, f32[4,24,1024]{2,1,0:T(8,128)}) custom-call(bf16[8,560,256]{2,1,0:T(8,128)(2,1)S(1)} %all-to-all-done.pages.inputs, bf16[1,4,32]{2,1,0:T(4,128)(2,1)S(1)} %copy-done.10, f32[1,128]{1,0:T(1,128)S(1)} %bitcast.5, f32[1,128]{1,0:T(1,128)S(1)} %bitcast.7, bf16[768,128]{1,0:T(8,128)(2,1)S(1)} %get-tuple-element.40.refs_0_, ...), custom_call_target="tpu_custom_call" | custom-call | bytes 12000000 | tf_op jit(solution)/shard_map/decode/pallas_call | solution.py:626
  58.9 0.1 collective-permute-start.8
  59.0 0.1 reshape.24
  59.0 0.6 reshape.25.gain_ref
  59.6 1.2 %collective-permute-done.8.other = f32[4,24,1024]{2,1,0:T(8,128)S(1)} collective-permute-done((f32[4,24,1024]{2,1,0:T(8,128)}, f32[4,24,1024]{2,1,0:T(8,128)S(1)}, u32[]{:S(2)}, u32[]{:S(2)}) %collective-permute-start.8) | collective-permute-done | bytes 393248 | tf_op jit(solution)/shard_map/ppermute | solution.py:694
  60.9 0.6 choose_side.1
  61.5 0.6 copy-done.6
  62.1 0.9 %collective-permute-start.9 = (f32[24,1024]{1,0:T(8,128)S(1)}, f32[24,1024]{1,0:T(8,128)S(1)}, u32[]{:S(2)}, u32[]{:S(2)}) collective-permute-start(f32[24,1024]{1,0:T(8,128)S(1)} %get-tuple-element.48), channel_id=1, source_target_pairs={{0,2},{1,3},{2,4},{3,5},{4,6},{5,7},{6,0},{7,1},{8,10},{9,11},{10,... | collective-permute-start | bytes 294920 | tf_op jit(solution)/shard_map/ppermute | solution.py:664
  63.0 2.7 %collective-permute-start.10 = (f32[24,1024]{1,0:T(8,128)S(1)}, f32[24,1024]{1,0:T(8,128)S(1)}, u32[]{:S(2)}, u32[]{:S(2)}) collective-permute-start(f32[24,1024]{1,0:T(8,128)S(1)} %get-tuple-element.49), channel_id=1, source_target_pairs={{0,4},{1,5},{2,6},{3,7},{4,0},{5,1},{6,2},{7,3},{8,12},{9,13},{10,... | collective-permute-start | bytes 294920 | tf_op jit(solution)/shard_map/ppermute | solution.py:664
  65.7 1.6 %collective-permute-start.11 = (f32[24,1024]{1,0:T(8,128)S(1)}, f32[24,1024]{1,0:T(8,128)S(1)}, u32[]{:S(2)}, u32[]{:S(2)}) collective-permute-start(f32[24,1024]{1,0:T(8,128)S(1)} %get-tuple-element.50), channel_id=1, source_target_pairs={{0,6},{1,7},{2,0},{3,1},{4,2},{5,3},{6,4},{7,5},{8,14},{9,15},{10,... | collective-permute-start | bytes 294920 | tf_op jit(solution)/shard_map/ppermute | solution.py:664
  67.3 0.7 pad_add_fusion.table
  68.0 13.9 %block_outputs.1 = bf16[2,256,8192]{2,1,0:T(8,128)(2,1)} custom-call(s32[16]{0:T(128)} %len_ref.3, bf16[2,256,8192]{2,1,0:T(8,128)(2,1)} %x_hbm.3, bf16[2,256,128]{2,1,0:T(8,128)(2,1)} %dt_hbm.3, bf16[2,32,256]{2,1,0:T(8,128)(2,1)} %bitcast.9, f32[1,128]{1,0:T(1,128)} %bitcast.4, f32[1,128]{1,0:T(1,128)} %bitcast.6, bf16[768,128]{1,0:T(8,128)(2,1)} %copy-done.1, ...), custom_call_target="tpu_custom_call" | custom-call | bytes 36000000 | tf_op jit(solution)/shard_map/block_outputs/pallas_call | solution.py:440
  81.9 0.0 collective-permute-done.9.refs_1_
  81.9 0.0 collective-permute-done.10.refs_2_
  82.0 0.0 collective-permute-done.11.refs_3_
  82.0 2.1 %all-to-all-done.1.recv = bf16[16,256,256]{2,1,0:T(8,128)(2,1)} async-done(((bf16[16,256,256]{2,1,0:T(8,128)(2,1)}), bf16[16,256,256]{2,1,0:T(8,128)(2,1)}, u32[]{:S(2)}, u32[]{:S(2)}) %all-to-all-start.1) | async-done | bytes 2097184 | tf_op jit(solution)/shard_map/all_to_all | solution.py:692
  84.1 3.9 %attend.1 = (bf16[1,4096,256]{2,1,0:T(8,128)(2,1)}, bf16[1,4,1024]{2,1,0:T(4,128)(2,1)}, f32[1,16,1024]{2,1,0:T(8,128)}, bf16[1,4,1024]{2,1,0:T(4,128)(2,1)}) custom-call(s32[288]{0:T(512)} %pad_add_fusion.table, bf16[16,256,256]{2,1,0:T(8,128)(2,1)} %all-to-all-done.1.recv, bf16[1,4,1024]{2,1,0:T(4,128)(2,1)} %q_ref.1, bf16[1,4,256]{2,1,0:T(4,128)(2,1)} %fresh_ref.1, ...), custom_call_target="tpu_custom_call" | custom-call | bytes 15000000 | tf_op jit(solution)/shard_map/attend/pallas_call | solution.py:544
  (32 shorter events, 0.1 us)
Async XLA Ops:
  8.4 5.6 %copy-start.19 = (bf16[528,128]{1,0:T(8,128)(2,1)S(1)}, bf16[528,128]{1,0:T(8,128)(2,1)}, u32[]{:S(2)}) copy-start(bf16[528,128]{1,0:T(8,128)(2,1)} %get-tuple-element.32) | copy-start | bytes 405508
  8.4 7.2 %copy-start.18 = (bf16[528,128]{1,0:T(8,128)(2,1)S(1)}, bf16[528,128]{1,0:T(8,128)(2,1)}, u32[]{:S(2)}) copy-start(bf16[528,128]{1,0:T(8,128)(2,1)} %get-tuple-element.33) | copy-start | bytes 405508
  8.4 10.1 %copy-start.17 = (bf16[528,128]{1,0:T(8,128)(2,1)S(1)}, bf16[528,128]{1,0:T(8,128)(2,1)}, u32[]{:S(2)}) copy-start(bf16[528,128]{1,0:T(8,128)(2,1)} %get-tuple-element.34) | copy-start | bytes 405508
  8.4 16.9 %copy-start.5 = (bf16[528,128]{1,0:T(8,128)(2,1)S(1)}, bf16[528,128]{1,0:T(8,128)(2,1)}, u32[]{:S(2)}) copy-start(bf16[528,128]{1,0:T(8,128)(2,1)} %get-tuple-element.31.refs_0_) | copy-start | bytes 405508
  8.4 29.1 %copy-start.7 = (s32[16]{0:T(128)S(1)}, s32[16]{0:T(128)}, u32[]{:S(2)}) copy-start(s32[16]{0:T(128)} %group_ref.5) | copy-start | bytes 196
  8.4 36.1 %all-to-all-start = ((bf16[8,560,256]{2,1,0:T(8,128)(2,1)}), bf16[8,560,256]{2,1,0:T(8,128)(2,1)S(1)}, u32[]{:S(2)}, u32[]{:S(2)}) async-start(bf16[8,560,256]{2,1,0:T(8,128)(2,1)} %get-tuple-element.30), calls=%async_computation | async-start | bytes 4587520 | tf_op jit(solution)/shard_map/all_to_all | solution.py:683
  14.0 7.3 %collective-permute-start = (bf16[528,128]{1,0:T(8,128)(2,1)S(1)}, bf16[528,128]{1,0:T(8,128)(2,1)S(1)}, u32[]{:S(2)}, u32[]{:S(2)}) collective-permute-start(bf16[528,128]{1,0:T(8,128)(2,1)S(1)} %copy-done.19), channel_id=1, source_target_pairs={{0,8},{8,16},{16,24},{24,0},{32,40},{40,48},{48,56},{56,32},{64,72... | collective-permute-start | bytes 405512 | tf_op jit(solution)/shard_map/ppermute | solution.py:669
  15.6 9.7 %collective-permute-start.1 = (bf16[528,128]{1,0:T(8,128)(2,1)S(1)}, bf16[528,128]{1,0:T(8,128)(2,1)S(1)}, u32[]{:S(2)}, u32[]{:S(2)}) collective-permute-start(bf16[528,128]{1,0:T(8,128)(2,1)S(1)} %copy-done.18), channel_id=1, source_target_pairs={{0,16},{8,24},{16,0},{24,8},{32,48},{40,56},{48,32},{56,40},{64,80... | collective-permute-start | bytes 405512 | tf_op jit(solution)/shard_map/ppermute | solution.py:669
  18.5 6.8 %collective-permute-start.2 = (bf16[528,128]{1,0:T(8,128)(2,1)S(1)}, bf16[528,128]{1,0:T(8,128)(2,1)S(1)}, u32[]{:S(2)}, u32[]{:S(2)}) collective-permute-start(bf16[528,128]{1,0:T(8,128)(2,1)S(1)} %copy-done.17), channel_id=1, source_target_pairs={{0,24},{8,0},{16,8},{24,16},{32,56},{40,32},{48,40},{56,48},{64,88... | collective-permute-start | bytes 405512 | tf_op jit(solution)/shard_map/ppermute | solution.py:669
  25.7 5.2 %collective-permute-start.3 = (bf16[528,128]{1,0:T(8,128)(2,1)S(1)}, bf16[528,128]{1,0:T(8,128)(2,1)S(1)}, u32[]{:S(2)}, u32[]{:S(2)}) collective-permute-start(bf16[528,128]{1,0:T(8,128)(2,1)S(1)} %row_totals.1.own), channel_id=1, source_target_pairs={{0,32},{8,40},{16,48},{24,56},{32,0},{40,8},{48,16},{56,24},{64,96... | collective-permute-start | bytes 405512 | tf_op jit(solution)/shard_map/ppermute | solution.py:686
  31.2 6.3 %collective-permute-start.4 = (bf16[528,128]{1,0:T(8,128)(2,1)S(1)}, bf16[528,128]{1,0:T(8,128)(2,1)S(1)}, u32[]{:S(2)}, u32[]{:S(2)}) collective-permute-start(bf16[528,128]{1,0:T(8,128)(2,1)S(1)} %pair_totals.1), channel_id=1, source_target_pairs={{0,96},{8,104},{16,112},{24,120},{32,64},{40,72},{48,80},{56,88},{... | collective-permute-start | bytes 405512 | tf_op jit(solution)/shard_map/ppermute | solution.py:688
  39.4 17.1 %copy-start.1 = (bf16[768,128]{1,0:T(8,128)(2,1)}, bf16[768,128]{1,0:T(8,128)(2,1)S(1)}, u32[]{:S(2)}) copy-start(bf16[768,128]{1,0:T(8,128)(2,1)S(1)} %get-tuple-element.40.refs_0_) | copy-start | bytes 589828
  39.4 8.9 %collective-permute-start.5 = (bf16[768,128]{1,0:T(8,128)(2,1)}, bf16[768,128]{1,0:T(8,128)(2,1)S(1)}, u32[]{:S(2)}, u32[]{:S(2)}) collective-permute-start(bf16[768,128]{1,0:T(8,128)(2,1)} %get-tuple-element.37), channel_id=1, source_target_pairs={{0,8},{8,16},{16,24},{24,0},{32,40},{40,48},{48,56},{56,32},{64,72... | collective-permute-start | bytes 589832 | tf_op jit(solution)/shard_map/ppermute | solution.py:669
  40.5 9.9 %collective-permute-start.6 = (bf16[768,128]{1,0:T(8,128)(2,1)S(1)}, bf16[768,128]{1,0:T(8,128)(2,1)S(1)}, u32[]{:S(2)}, u32[]{:S(2)}) collective-permute-start(bf16[768,128]{1,0:T(8,128)(2,1)S(1)} %get-tuple-element.38), channel_id=1, source_target_pairs={{0,16},{8,24},{16,0},{24,8},{32,48},{40,56},{48,32},{56,40},{64,80... | collective-permute-start | bytes 589832 | tf_op jit(solution)/shard_map/ppermute | solution.py:669
  43.2 7.2 %collective-permute-start.7 = (bf16[768,128]{1,0:T(8,128)(2,1)S(1)}, bf16[768,128]{1,0:T(8,128)(2,1)S(1)}, u32[]{:S(2)}, u32[]{:S(2)}) collective-permute-start(bf16[768,128]{1,0:T(8,128)(2,1)S(1)} %get-tuple-element.39), channel_id=1, source_target_pairs={{0,24},{8,0},{16,8},{24,16},{32,56},{40,32},{48,40},{56,48},{64,88... | collective-permute-start | bytes 589832 | tf_op jit(solution)/shard_map/ppermute | solution.py:669
  45.2 1.3 %copy-start = (bf16[16,256,256]{2,1,0:T(8,128)(2,1)}, bf16[16,256,256]{2,1,0:T(8,128)(2,1)S(1)}, u32[]{:S(2)}) copy-start(bf16[16,256,256]{2,1,0:T(8,128)(2,1)S(1)} %order_pages.1) | copy-start | bytes 6291460
  46.5 10.0 %copy-start.8 = (f32[128]{0:T(128)S(1)}, f32[128]{0:T(128)}, u32[]{:S(2)}) copy-start(f32[128]{0:T(128)} %param.19) | copy-start | bytes 1540
  46.5 10.0 %copy-start.9 = (f32[128]{0:T(128)S(1)}, f32[128]{0:T(128)}, u32[]{:S(2)}) copy-start(f32[128]{0:T(128)} %param.20) | copy-start | bytes 1540
  46.5 10.0 %copy-start.10 = (bf16[1,4,32]{2,1,0:T(4,128)(2,1)S(1)}, bf16[1,4,32]{2,1,0:T(4,128)(2,1)}, u32[]{:S(2)}) copy-start(bf16[1,4,32]{2,1,0:T(4,128)(2,1)} %maps_ref.1) | copy-start | bytes 772
  48.3 10.6 %copy-start.2 = (bf16[768,128]{1,0:T(8,128)(2,1)}, bf16[768,128]{1,0:T(8,128)(2,1)S(1)}, u32[]{:S(2)}) copy-start(bf16[768,128]{1,0:T(8,128)(2,1)S(1)} %collective-permute-done.5.refs_1_) | copy-start | bytes 589828
  50.4 8.5 %copy-start.3 = (bf16[768,128]{1,0:T(8,128)(2,1)}, bf16[768,128]{1,0:T(8,128)(2,1)S(1)}, u32[]{:S(2)}) copy-start(bf16[768,128]{1,0:T(8,128)(2,1)S(1)} %collective-permute-done.6.refs_2_) | copy-start | bytes 589828
  50.4 8.5 %copy-start.4 = (bf16[768,128]{1,0:T(8,128)(2,1)}, bf16[768,128]{1,0:T(8,128)(2,1)S(1)}, u32[]{:S(2)}) copy-start(bf16[768,128]{1,0:T(8,128)(2,1)S(1)} %collective-permute-done.7.refs_3_) | copy-start | bytes 589828
  50.4 33.7 %all-to-all-start.1 = ((bf16[16,256,256]{2,1,0:T(8,128)(2,1)}), bf16[16,256,256]{2,1,0:T(8,128)(2,1)}, u32[]{:S(2)}, u32[]{:S(2)}) async-start(bf16[16,256,256]{2,1,0:T(8,128)(2,1)} %copy-done), calls=%async_computation.1 | async-start | bytes 4194304 | tf_op jit(solution)/shard_map/all_to_all | solution.py:692
  56.4 2.5 %copy-start.14 = (s32[16,16]{1,0:T(8,128)S(1)}, s32[16,16]{1,0:T(8,128)}, u32[]{:S(2)}) copy-start(s32[16,16]{1,0:T(8,128)} %param.24) | copy-start | bytes 3076
  56.4 2.6 %copy-start.16 = (bf16[1024]{0:T(1024)(128)(2,1)S(1)}, bf16[1024]{0:T(1024)(128)(2,1)}, u32[]{:S(2)}) copy-start(bf16[1024]{0:T(1024)(128)(2,1)} %param.29) | copy-start | bytes 6148
  56.5 10.9 %copy-start.15 = (s32[16]{0:T(128)S(1)}, s32[16]{0:T(128)}, u32[]{:S(2)}) copy-start(s32[16]{0:T(128)} %len_ref.3) | copy-start | bytes 196
  58.9 2.0 %collective-permute-start.8 = (f32[4,24,1024]{2,1,0:T(8,128)}, f32[4,24,1024]{2,1,0:T(8,128)S(1)}, u32[]{:S(2)}, u32[]{:S(2)}) collective-permute-start(f32[4,24,1024]{2,1,0:T(8,128)} %get-tuple-element.46), channel_id=1, source_target_pairs={{0,1},{1,0},{2,3},{3,2},{4,5},{5,4},{6,7},{7,6},{8,9},{9,8},{10,11... | collective-permute-start | bytes 1179656 | tf_op jit(solution)/shard_map/ppermute | solution.py:694
  61.5 0.6 copy-start.6
  62.1 19.8 %collective-permute-start.9 = (f32[24,1024]{1,0:T(8,128)S(1)}, f32[24,1024]{1,0:T(8,128)S(1)}, u32[]{:S(2)}, u32[]{:S(2)}) collective-permute-start(f32[24,1024]{1,0:T(8,128)S(1)} %get-tuple-element.48), channel_id=1, source_target_pairs={{0,2},{1,3},{2,4},{3,5},{4,6},{5,7},{6,0},{7,1},{8,10},{9,11},{10,... | collective-permute-start | bytes 294920 | tf_op jit(solution)/shard_map/ppermute | solution.py:664
  63.0 18.9 %collective-permute-start.10 = (f32[24,1024]{1,0:T(8,128)S(1)}, f32[24,1024]{1,0:T(8,128)S(1)}, u32[]{:S(2)}, u32[]{:S(2)}) collective-permute-start(f32[24,1024]{1,0:T(8,128)S(1)} %get-tuple-element.49), channel_id=1, source_target_pairs={{0,4},{1,5},{2,6},{3,7},{4,0},{5,1},{6,2},{7,3},{8,12},{9,13},{10,... | collective-permute-start | bytes 294920 | tf_op jit(solution)/shard_map/ppermute | solution.py:664
  65.7 16.3 %collective-permute-start.11 = (f32[24,1024]{1,0:T(8,128)S(1)}, f32[24,1024]{1,0:T(8,128)S(1)}, u32[]{:S(2)}, u32[]{:S(2)}) collective-permute-start(f32[24,1024]{1,0:T(8,128)S(1)} %get-tuple-element.50), channel_id=1, source_target_pairs={{0,6},{1,7},{2,0},{3,1},{4,2},{5,3},{6,4},{7,5},{8,14},{9,15},{10,... | collective-permute-start | bytes 294920 | tf_op jit(solution)/shard_map/ppermute | solution.py:664
  81.9 2.2 %copy-start.11 = (f32[24,1024]{1,0:T(8,128)}, f32[24,1024]{1,0:T(8,128)S(1)}, u32[]{:S(2)}) copy-start(f32[24,1024]{1,0:T(8,128)S(1)} %collective-permute-done.9.refs_1_) | copy-start | bytes 294916
  82.0 2.2 %copy-start.12 = (f32[24,1024]{1,0:T(8,128)}, f32[24,1024]{1,0:T(8,128)S(1)}, u32[]{:S(2)}) copy-start(f32[24,1024]{1,0:T(8,128)S(1)} %collective-permute-done.10.refs_2_) | copy-start | bytes 294916
  82.0 2.1 %copy-start.13 = (f32[24,1024]{1,0:T(8,128)}, f32[24,1024]{1,0:T(8,128)S(1)}, u32[]{:S(2)}) copy-start(f32[24,1024]{1,0:T(8,128)S(1)} %collective-permute-done.11.refs_3_) | copy-start | bytes 294916

commit v4 on v3

--- a/solution.py
+++ b/solution.py
@@ -560,7 +560,7 @@
             pltpu.SemaphoreType.DMA((SEQ,)),
         ],
         cost_estimate=cost(5),
-        compiler_params=params(54),
+        compiler_params=params(),
         name="attend",
     )(table, recv, queries, fresh, gain, *results)
 

time: 88.3 us -> 88.3 us (level)
  waiting for transfers between devices: 19.8 us -> 21.4 us
  local copies, waits for them, and re-layouts: 2.71 us -> 1.48 us
    all_to_all x1, waiting for transfers between devices: 2.12 us -> 3.15 us  [shards(): lax.all_to_all(ordered, 'seq', split_axis=0, concat_axis=0, tiled=True)]
    unnamed x40 -> x36, local copies, waits for them, and re-layouts: 2.03 us -> 1.39 us
  transfers between devices with their start and end apart: 14 -> 14, of which waited for: 8 -> 8; matrix products, arithmetic and copies ran while one was open for 2% -> 0% of each run, Pallas kernels for 23% -> 23%
where the time goes in v4:
time: 88.3 us; the launch traced here: 87.9 us
  starting transfers between devices  32.3 us (37%)
  Pallas kernels  31.8 us (36%)
  waiting for transfers between devices  21.4 us (24%)
  local copies, waits for them, and re-layouts  1.48 us (2%)
    pallas_call x1, Pallas kernels, block_outputs(): pl.pallas_call(output_kernel, out_shape=jax.ShapeDtypeStruct((2, BLK, WID...  14.1 us
    ppermute x6, starting transfers between devices, along_y(): lax.ppermute(arrays[o], 'seq', moves[o])  11 us
    ppermute x6, waiting for transfers between devices, along_y(): lax.ppermute(arrays[o], 'seq', moves[o])  9.34 us
    pallas_call x1, Pallas kernels, local_states(): pl.pallas_call(local_kernel, out_shape=[jax.ShapeDtypeStruct((STATE_ROWS...  7.73 us
    all_to_all x1, starting transfers between devices, shards(): lax.all_to_all(ordered, 'seq', split_axis=0, concat_axis=0, tiled=True)  6.03 us
    all_to_all x1, starting transfers between devices, shards(): pages = lax.all_to_all(sent, 'tp', split_axis=0, concat_axis=0, tiled=True)  5.54 us
    ppermute x3, starting transfers between devices, along_z(): lax.ppermute(arrays[o], 'tp', moves[o])  5.26 us
    pallas_call x1, Pallas kernels, attend(): pl.pallas_call(attend_kernel, out_shape=[jax.ShapeDtypeStruct((1, SEQ * B...  3.82 us
  transfers between devices with their start and end apart: 14, of which 8 were waited for; matrix products, arithmetic and copies ran while one was open for 0% of the time, Pallas kernels for 23%

profile of v4, /device:TPU:0, one launch (start us, length us, event | category | flops | bytes accessed | tf_op | source)
XLA Modules:
  0.0 87.9 jit_solution(7509943568004638922)
XLA Ops:
  0.6 7.7 %local_states.1 = (bf16[528,128]{1,0:T(8,128)(2,1)}, bf16[528,128]{1,0:T(8,128)(2,1)}, bf16[528,128]{1,0:T(8,128)(2,1)}, bf16[528,128]{1,0:T(8,128)(2,1)}, bf16[8,560,256]{2,1,0:T(8,128)(2,1)}) custom-call(s32[16]{0:T(128)} %len_ref.3, bf16[2,256,8192]{2,1,0:T(8,128)(2,1)} %x_hbm.3, bf16[2,256,128]{2,1,0:T(8,128)(2,1)} %dt_hbm.3, ...), custom_call_target="tpu_custom_call" | custom-call | bytes 18000000 | tf_op jit(solution)/shard_map/local_states/pallas_call | solution.py:187
  8.4 0.0 copy-start.5
  8.4 0.0 copy-start.6
  8.4 5.5 %all-to-all-start = ((bf16[8,560,256]{2,1,0:T(8,128)(2,1)}), bf16[8,560,256]{2,1,0:T(8,128)(2,1)S(1)}, u32[]{:S(2)}, u32[]{:S(2)}) async-start(bf16[8,560,256]{2,1,0:T(8,128)(2,1)} %get-tuple-element.30), calls=%async_computation | async-start | bytes 4587520 | tf_op jit(solution)/shard_map/all_to_all | solution.py:683
  14.0 0.0 copy-done.17
  14.0 1.6 %collective-permute-start = (bf16[528,128]{1,0:T(8,128)(2,1)S(1)}, bf16[528,128]{1,0:T(8,128)(2,1)S(1)}, u32[]{:S(2)}, u32[]{:S(2)}) collective-permute-start(bf16[528,128]{1,0:T(8,128)(2,1)S(1)} %copy-done.17), channel_id=1, source_target_pairs={{0,8},{8,16},{16,24},{24,0},{32,40},{40,48},{48,56},{56,32},{64,72... | collective-permute-start | bytes 405512 | tf_op jit(solution)/shard_map/ppermute | solution.py:669
  15.6 2.9 %collective-permute-start.1 = (bf16[528,128]{1,0:T(8,128)(2,1)S(1)}, bf16[528,128]{1,0:T(8,128)(2,1)S(1)}, u32[]{:S(2)}, u32[]{:S(2)}) collective-permute-start(bf16[528,128]{1,0:T(8,128)(2,1)S(1)} %copy-done.16), channel_id=1, source_target_pairs={{0,16},{8,24},{16,0},{24,8},{32,48},{40,56},{48,32},{56,40},{64,80... | collective-permute-start | bytes 405512 | tf_op jit(solution)/shard_map/ppermute | solution.py:669
  18.5 0.0 copy-done.15
  18.5 1.3 %collective-permute-start.2 = (bf16[528,128]{1,0:T(8,128)(2,1)S(1)}, bf16[528,128]{1,0:T(8,128)(2,1)S(1)}, u32[]{:S(2)}, u32[]{:S(2)}) collective-permute-start(bf16[528,128]{1,0:T(8,128)(2,1)S(1)} %copy-done.15), channel_id=1, source_target_pairs={{0,24},{8,0},{16,8},{24,16},{32,56},{40,32},{48,40},{56,48},{64,88... | collective-permute-start | bytes 405512 | tf_op jit(solution)/shard_map/ppermute | solution.py:669
  19.9 1.4 %collective-permute-done.refs_1_ = bf16[528,128]{1,0:T(8,128)(2,1)S(1)} collective-permute-done((bf16[528,128]{1,0:T(8,128)(2,1)S(1)}, bf16[528,128]{1,0:T(8,128)(2,1)S(1)}, u32[]{:S(2)}, u32[]{:S(2)}) %collective-permute-start) | collective-permute-done | bytes 135200 | tf_op jit(solution)/shard_map/ppermute | solution.py:669
  21.2 4.1 %collective-permute-done.1.refs_2_ = bf16[528,128]{1,0:T(8,128)(2,1)S(1)} collective-permute-done((bf16[528,128]{1,0:T(8,128)(2,1)S(1)}, bf16[528,128]{1,0:T(8,128)(2,1)S(1)}, u32[]{:S(2)}, u32[]{:S(2)}) %collective-permute-start.1) | collective-permute-done | bytes 135200 | tf_op jit(solution)/shard_map/ppermute | solution.py:669
  25.3 0.0 collective-permute-done.2.refs_3_
  25.3 0.3 row_totals.1.own
  25.7 1.6 %collective-permute-start.3 = (bf16[528,128]{1,0:T(8,128)(2,1)S(1)}, bf16[528,128]{1,0:T(8,128)(2,1)S(1)}, u32[]{:S(2)}, u32[]{:S(2)}) collective-permute-start(bf16[528,128]{1,0:T(8,128)(2,1)S(1)} %row_totals.1.own), channel_id=1, source_target_pairs={{0,32},{8,40},{16,48},{24,56},{32,0},{40,8},{48,16},{56,24},{64,96... | collective-permute-start | bytes 405512 | tf_op jit(solution)/shard_map/ppermute | solution.py:686
  27.2 3.7 %collective-permute-done.3.near = bf16[528,128]{1,0:T(8,128)(2,1)S(1)} collective-permute-done((bf16[528,128]{1,0:T(8,128)(2,1)S(1)}, bf16[528,128]{1,0:T(8,128)(2,1)S(1)}, u32[]{:S(2)}, u32[]{:S(2)}) %collective-permute-start.3) | collective-permute-done | bytes 135200 | tf_op jit(solution)/shard_map/ppermute | solution.py:686
  30.9 0.3 pair_totals.1
  31.2 2.8 %collective-permute-start.4 = (bf16[528,128]{1,0:T(8,128)(2,1)S(1)}, bf16[528,128]{1,0:T(8,128)(2,1)S(1)}, u32[]{:S(2)}, u32[]{:S(2)}) collective-permute-start(bf16[528,128]{1,0:T(8,128)(2,1)S(1)} %pair_totals.1), channel_id=1, source_target_pairs={{0,96},{8,104},{16,112},{24,120},{32,64},{40,72},{48,80},{56,88},{... | collective-permute-start | bytes 405512 | tf_op jit(solution)/shard_map/ppermute | solution.py:688
  34.0 3.5 %collective-permute-done.4.far = bf16[528,128]{1,0:T(8,128)(2,1)S(1)} collective-permute-done((bf16[528,128]{1,0:T(8,128)(2,1)S(1)}, bf16[528,128]{1,0:T(8,128)(2,1)S(1)}, u32[]{:S(2)}, u32[]{:S(2)}) %collective-permute-start.4) | collective-permute-done | bytes 135200 | tf_op jit(solution)/shard_map/ppermute | solution.py:688
  37.5 1.9 %enter_states.1 = (bf16[768,128]{1,0:T(8,128)(2,1)S(1)}, bf16[768,128]{1,0:T(8,128)(2,1)}, bf16[768,128]{1,0:T(8,128)(2,1)S(1)}, bf16[768,128]{1,0:T(8,128)(2,1)S(1)}) custom-call(s32[16]{0:T(128)S(1)} %copy-done.6, bf16[528,128]{1,0:T(8,128)(2,1)S(1)} %row_totals.1.own, bf16[528,128]{1,0:T(8,128)(2,1)S(1)} %collective-permute-done.3.near, ...), custom_call_target="tpu_custom_call" | custom-call | bytes 6000000 | tf_op jit(solution)/shard_map/enter_states/pallas_call | solution.py:339
  39.4 1.1 %collective-permute-start.5 = (bf16[768,128]{1,0:T(8,128)(2,1)}, bf16[768,128]{1,0:T(8,128)(2,1)S(1)}, u32[]{:S(2)}, u32[]{:S(2)}) collective-permute-start(bf16[768,128]{1,0:T(8,128)(2,1)} %get-tuple-element.37), channel_id=1, source_target_pairs={{0,8},{8,16},{16,24},{24,0},{32,40},{40,48},{48,56},{56,32},{64,72... | collective-permute-start | bytes 589832 | tf_op jit(solution)/shard_map/ppermute | solution.py:669
  40.5 2.7 %collective-permute-start.6 = (bf16[768,128]{1,0:T(8,128)(2,1)S(1)}, bf16[768,128]{1,0:T(8,128)(2,1)S(1)}, u32[]{:S(2)}, u32[]{:S(2)}) collective-permute-start(bf16[768,128]{1,0:T(8,128)(2,1)S(1)} %get-tuple-element.38), channel_id=1, source_target_pairs={{0,16},{8,24},{16,0},{24,8},{32,48},{40,56},{48,32},{56,40},{64,80... | collective-permute-start | bytes 589832 | tf_op jit(solution)/shard_map/ppermute | solution.py:669
  43.1 1.3 %collective-permute-start.7 = (bf16[768,128]{1,0:T(8,128)(2,1)S(1)}, bf16[768,128]{1,0:T(8,128)(2,1)S(1)}, u32[]{:S(2)}, u32[]{:S(2)}) collective-permute-start(bf16[768,128]{1,0:T(8,128)(2,1)S(1)} %get-tuple-element.39), channel_id=1, source_target_pairs={{0,24},{8,0},{16,8},{24,16},{32,56},{40,32},{48,40},{56,48},{64,88... | collective-permute-start | bytes 589832 | tf_op jit(solution)/shard_map/ppermute | solution.py:669
  44.5 0.0 all-to-all-done.pages.inputs
  44.5 0.7 order_pages.1
  45.2 0.0 copy-start
  45.2 1.3 %copy-done = bf16[16,256,256]{2,1,0:T(8,128)(2,1)} copy-done((bf16[16,256,256]{2,1,0:T(8,128)(2,1)}, bf16[16,256,256]{2,1,0:T(8,128)(2,1)S(1)}, u32[]{:S(2)}) %copy-start) | copy-done | bytes 2097176
  46.5 1.8 %collective-permute-done.5.refs_1_ = bf16[768,128]{1,0:T(8,128)(2,1)S(1)} collective-permute-done((bf16[768,128]{1,0:T(8,128)(2,1)}, bf16[768,128]{1,0:T(8,128)(2,1)S(1)}, u32[]{:S(2)}, u32[]{:S(2)}) %collective-permute-start.5) | collective-permute-done | bytes 196640 | tf_op jit(solution)/shard_map/ppermute | solution.py:669
  48.3 2.1 %collective-permute-done.6.refs_2_ = bf16[768,128]{1,0:T(8,128)(2,1)S(1)} collective-permute-done((bf16[768,128]{1,0:T(8,128)(2,1)S(1)}, bf16[768,128]{1,0:T(8,128)(2,1)S(1)}, u32[]{:S(2)}, u32[]{:S(2)}) %collective-permute-start.6) | collective-permute-done | bytes 196640 | tf_op jit(solution)/shard_map/ppermute | solution.py:669
  50.4 0.0 collective-permute-done.7.refs_3_
  50.4 6.0 %all-to-all-start.1 = ((bf16[16,256,256]{2,1,0:T(8,128)(2,1)}), bf16[16,256,256]{2,1,0:T(8,128)(2,1)}, u32[]{:S(2)}, u32[]{:S(2)}) async-start(bf16[16,256,256]{2,1,0:T(8,128)(2,1)} %copy-done), calls=%async_computation.1 | async-start | bytes 4194304 | tf_op jit(solution)/shard_map/all_to_all | solution.py:692
  56.4 0.0 copy-start.12
  56.4 0.0 copy-start.14
  56.4 0.0 copy-start.13
  56.5 2.3 %decode.1 = (f32[4,24,1024]{2,1,0:T(8,128)S(1)}, f32[4,24,1024]{2,1,0:T(8,128)}) custom-call(bf16[8,560,256]{2,1,0:T(8,128)(2,1)S(1)} %all-to-all-done.pages.inputs, bf16[1,4,32]{2,1,0:T(4,128)(2,1)S(1)} %copy-done.11, f32[1,128]{1,0:T(1,128)S(1)} %bitcast.5, f32[1,128]{1,0:T(1,128)S(1)} %bitcast.7, bf16[768,128]{1,0:T(8,128)(2,1)S(1)} %get-tuple-element.40.refs_0_, ...), custom_call_target="tpu_custom_call" | custom-call | bytes 12000000 | tf_op jit(solution)/shard_map/decode/pallas_call | solution.py:626
  58.8 0.1 collective-permute-start.8
  58.9 0.1 reshape.24
  59.0 1.8 %collective-permute-done.8.other = f32[4,24,1024]{2,1,0:T(8,128)S(1)} collective-permute-done((f32[4,24,1024]{2,1,0:T(8,128)}, f32[4,24,1024]{2,1,0:T(8,128)S(1)}, u32[]{:S(2)}, u32[]{:S(2)}) %collective-permute-start.8) | collective-permute-done | bytes 393248 | tf_op jit(solution)/shard_map/ppermute | solution.py:694
  60.8 0.6 choose_side.1
  61.5 1.0 %collective-permute-start.9 = (f32[24,1024]{1,0:T(8,128)S(1)}, f32[24,1024]{1,0:T(8,128)S(1)}, u32[]{:S(2)}, u32[]{:S(2)}) collective-permute-start(f32[24,1024]{1,0:T(8,128)S(1)} %get-tuple-element.48), channel_id=1, source_target_pairs={{0,2},{1,3},{2,4},{3,5},{4,6},{5,7},{6,0},{7,1},{8,10},{9,11},{10,... | collective-permute-start | bytes 294920 | tf_op jit(solution)/shard_map/ppermute | solution.py:664
  62.4 2.7 %collective-permute-start.10 = (f32[24,1024]{1,0:T(8,128)S(1)}, f32[24,1024]{1,0:T(8,128)S(1)}, u32[]{:S(2)}, u32[]{:S(2)}) collective-permute-start(f32[24,1024]{1,0:T(8,128)S(1)} %get-tuple-element.49), channel_id=1, source_target_pairs={{0,4},{1,5},{2,6},{3,7},{4,0},{5,1},{6,2},{7,3},{8,12},{9,13},{10,... | collective-permute-start | bytes 294920 | tf_op jit(solution)/shard_map/ppermute | solution.py:664
  65.1 1.6 %collective-permute-start.11 = (f32[24,1024]{1,0:T(8,128)S(1)}, f32[24,1024]{1,0:T(8,128)S(1)}, u32[]{:S(2)}, u32[]{:S(2)}) collective-permute-start(f32[24,1024]{1,0:T(8,128)S(1)} %get-tuple-element.50), channel_id=1, source_target_pairs={{0,6},{1,7},{2,0},{3,1},{4,2},{5,3},{6,4},{7,5},{8,14},{9,15},{10,... | collective-permute-start | bytes 294920 | tf_op jit(solution)/shard_map/ppermute | solution.py:664
  66.7 0.1 pad_add_fusion.table
  66.8 14.1 %block_outputs.1 = bf16[2,256,8192]{2,1,0:T(8,128)(2,1)} custom-call(s32[16]{0:T(128)} %len_ref.3, bf16[2,256,8192]{2,1,0:T(8,128)(2,1)} %x_hbm.3, bf16[2,256,128]{2,1,0:T(8,128)(2,1)} %dt_hbm.3, bf16[2,32,256]{2,1,0:T(8,128)(2,1)} %bitcast.9, f32[1,128]{1,0:T(1,128)} %bitcast.4, f32[1,128]{1,0:T(1,128)} %bitcast.6, bf16[768,128]{1,0:T(8,128)(2,1)} %copy-done.1, ...), custom_call_target="tpu_custom_call" | custom-call | bytes 36000000 | tf_op jit(solution)/shard_map/block_outputs/pallas_call | solution.py:440
  80.9 0.0 collective-permute-done.9.refs_1_
  80.9 0.0 collective-permute-done.10.refs_2_
  80.9 0.0 collective-permute-done.11.refs_3_
  81.0 3.1 %all-to-all-done.1.recv = bf16[16,256,256]{2,1,0:T(8,128)(2,1)} async-done(((bf16[16,256,256]{2,1,0:T(8,128)(2,1)}), bf16[16,256,256]{2,1,0:T(8,128)(2,1)}, u32[]{:S(2)}, u32[]{:S(2)}) %all-to-all-start.1) | async-done | bytes 2097184 | tf_op jit(solution)/shard_map/all_to_all | solution.py:692
  84.1 3.8 %attend.1 = (bf16[1,4096,256]{2,1,0:T(8,128)(2,1)}, bf16[1,4,1024]{2,1,0:T(4,128)(2,1)}, f32[1,16,1024]{2,1,0:T(8,128)}, bf16[1,4,1024]{2,1,0:T(4,128)(2,1)}) custom-call(s32[288]{0:T(512)S(1)} %pad_add_fusion.table, bf16[16,256,256]{2,1,0:T(8,128)(2,1)} %all-to-all-done.1.recv, bf16[1,4,1024]{2,1,0:T(4,128)(2,1)S(1)} %copy-done.7, ...), custom_call_target="tpu_custom_call" | custom-call | bytes 15000000 | tf_op jit(solution)/shard_map/attend/pallas_call | solution.py:544
  (28 shorter events, 0.1 us)
Async XLA Ops:
  8.4 5.6 %copy-start.17 = (bf16[528,128]{1,0:T(8,128)(2,1)S(1)}, bf16[528,128]{1,0:T(8,128)(2,1)}, u32[]{:S(2)}) copy-start(bf16[528,128]{1,0:T(8,128)(2,1)} %get-tuple-element.32) | copy-start | bytes 405508
  8.4 7.2 %copy-start.16 = (bf16[528,128]{1,0:T(8,128)(2,1)S(1)}, bf16[528,128]{1,0:T(8,128)(2,1)}, u32[]{:S(2)}) copy-start(bf16[528,128]{1,0:T(8,128)(2,1)} %get-tuple-element.33) | copy-start | bytes 405508
  8.4 10.1 %copy-start.15 = (bf16[528,128]{1,0:T(8,128)(2,1)S(1)}, bf16[528,128]{1,0:T(8,128)(2,1)}, u32[]{:S(2)}) copy-start(bf16[528,128]{1,0:T(8,128)(2,1)} %get-tuple-element.34) | copy-start | bytes 405508
  8.4 16.9 %copy-start.5 = (bf16[528,128]{1,0:T(8,128)(2,1)S(1)}, bf16[528,128]{1,0:T(8,128)(2,1)}, u32[]{:S(2)}) copy-start(bf16[528,128]{1,0:T(8,128)(2,1)} %get-tuple-element.31.refs_0_) | copy-start | bytes 405508
  8.4 29.1 %copy-start.6 = (s32[16]{0:T(128)S(1)}, s32[16]{0:T(128)}, u32[]{:S(2)}) copy-start(s32[16]{0:T(128)} %group_ref.5) | copy-start | bytes 196
  8.4 36.0 %all-to-all-start = ((bf16[8,560,256]{2,1,0:T(8,128)(2,1)}), bf16[8,560,256]{2,1,0:T(8,128)(2,1)S(1)}, u32[]{:S(2)}, u32[]{:S(2)}) async-start(bf16[8,560,256]{2,1,0:T(8,128)(2,1)} %get-tuple-element.30), calls=%async_computation | async-start | bytes 4587520 | tf_op jit(solution)/shard_map/all_to_all | solution.py:683
  14.0 7.3 %collective-permute-start = (bf16[528,128]{1,0:T(8,128)(2,1)S(1)}, bf16[528,128]{1,0:T(8,128)(2,1)S(1)}, u32[]{:S(2)}, u32[]{:S(2)}) collective-permute-start(bf16[528,128]{1,0:T(8,128)(2,1)S(1)} %copy-done.17), channel_id=1, source_target_pairs={{0,8},{8,16},{16,24},{24,0},{32,40},{40,48},{48,56},{56,32},{64,72... | collective-permute-start | bytes 405512 | tf_op jit(solution)/shard_map/ppermute | solution.py:669
  15.6 9.7 %collective-permute-start.1 = (bf16[528,128]{1,0:T(8,128)(2,1)S(1)}, bf16[528,128]{1,0:T(8,128)(2,1)S(1)}, u32[]{:S(2)}, u32[]{:S(2)}) collective-permute-start(bf16[528,128]{1,0:T(8,128)(2,1)S(1)} %copy-done.16), channel_id=1, source_target_pairs={{0,16},{8,24},{16,0},{24,8},{32,48},{40,56},{48,32},{56,40},{64,80... | collective-permute-start | bytes 405512 | tf_op jit(solution)/shard_map/ppermute | solution.py:669
  18.5 6.8 %collective-permute-start.2 = (bf16[528,128]{1,0:T(8,128)(2,1)S(1)}, bf16[528,128]{1,0:T(8,128)(2,1)S(1)}, u32[]{:S(2)}, u32[]{:S(2)}) collective-permute-start(bf16[528,128]{1,0:T(8,128)(2,1)S(1)} %copy-done.15), channel_id=1, source_target_pairs={{0,24},{8,0},{16,8},{24,16},{32,56},{40,32},{48,40},{56,48},{64,88... | collective-permute-start | bytes 405512 | tf_op jit(solution)/shard_map/ppermute | solution.py:669
  25.7 5.2 %collective-permute-start.3 = (bf16[528,128]{1,0:T(8,128)(2,1)S(1)}, bf16[528,128]{1,0:T(8,128)(2,1)S(1)}, u32[]{:S(2)}, u32[]{:S(2)}) collective-permute-start(bf16[528,128]{1,0:T(8,128)(2,1)S(1)} %row_totals.1.own), channel_id=1, source_target_pairs={{0,32},{8,40},{16,48},{24,56},{32,0},{40,8},{48,16},{56,24},{64,96... | collective-permute-start | bytes 405512 | tf_op jit(solution)/shard_map/ppermute | solution.py:686
  31.2 6.3 %collective-permute-start.4 = (bf16[528,128]{1,0:T(8,128)(2,1)S(1)}, bf16[528,128]{1,0:T(8,128)(2,1)S(1)}, u32[]{:S(2)}, u32[]{:S(2)}) collective-permute-start(bf16[528,128]{1,0:T(8,128)(2,1)S(1)} %pair_totals.1), channel_id=1, source_target_pairs={{0,96},{8,104},{16,112},{24,120},{32,64},{40,72},{48,80},{56,88},{... | collective-permute-start | bytes 405512 | tf_op jit(solution)/shard_map/ppermute | solution.py:688
  39.4 17.1 %copy-start.1 = (bf16[768,128]{1,0:T(8,128)(2,1)}, bf16[768,128]{1,0:T(8,128)(2,1)S(1)}, u32[]{:S(2)}) copy-start(bf16[768,128]{1,0:T(8,128)(2,1)S(1)} %get-tuple-element.40.refs_0_) | copy-start | bytes 589828
  39.4 8.9 %collective-permute-start.5 = (bf16[768,128]{1,0:T(8,128)(2,1)}, bf16[768,128]{1,0:T(8,128)(2,1)S(1)}, u32[]{:S(2)}, u32[]{:S(2)}) collective-permute-start(bf16[768,128]{1,0:T(8,128)(2,1)} %get-tuple-element.37), channel_id=1, source_target_pairs={{0,8},{8,16},{16,24},{24,0},{32,40},{40,48},{48,56},{56,32},{64,72... | collective-permute-start | bytes 589832 | tf_op jit(solution)/shard_map/ppermute | solution.py:669
  40.5 9.9 %collective-permute-start.6 = (bf16[768,128]{1,0:T(8,128)(2,1)S(1)}, bf16[768,128]{1,0:T(8,128)(2,1)S(1)}, u32[]{:S(2)}, u32[]{:S(2)}) collective-permute-start(bf16[768,128]{1,0:T(8,128)(2,1)S(1)} %get-tuple-element.38), channel_id=1, source_target_pairs={{0,16},{8,24},{16,0},{24,8},{32,48},{40,56},{48,32},{56,40},{64,80... | collective-permute-start | bytes 589832 | tf_op jit(solution)/shard_map/ppermute | solution.py:669
  43.1 7.2 %collective-permute-start.7 = (bf16[768,128]{1,0:T(8,128)(2,1)S(1)}, bf16[768,128]{1,0:T(8,128)(2,1)S(1)}, u32[]{:S(2)}, u32[]{:S(2)}) collective-permute-start(bf16[768,128]{1,0:T(8,128)(2,1)S(1)} %get-tuple-element.39), channel_id=1, source_target_pairs={{0,24},{8,0},{16,8},{24,16},{32,56},{40,32},{48,40},{56,48},{64,88... | collective-permute-start | bytes 589832 | tf_op jit(solution)/shard_map/ppermute | solution.py:669
  45.2 1.3 %copy-start = (bf16[16,256,256]{2,1,0:T(8,128)(2,1)}, bf16[16,256,256]{2,1,0:T(8,128)(2,1)S(1)}, u32[]{:S(2)}) copy-start(bf16[16,256,256]{2,1,0:T(8,128)(2,1)S(1)} %order_pages.1) | copy-start | bytes 6291460
  46.5 10.0 %copy-start.8 = (f32[128]{0:T(128)S(1)}, f32[128]{0:T(128)}, u32[]{:S(2)}) copy-start(f32[128]{0:T(128)} %param.19) | copy-start | bytes 1540
  46.5 10.0 %copy-start.10 = (f32[128]{0:T(128)S(1)}, f32[128]{0:T(128)}, u32[]{:S(2)}) copy-start(f32[128]{0:T(128)} %param.20) | copy-start | bytes 1540
  46.5 10.0 %copy-start.11 = (bf16[1,4,32]{2,1,0:T(4,128)(2,1)S(1)}, bf16[1,4,32]{2,1,0:T(4,128)(2,1)}, u32[]{:S(2)}) copy-start(bf16[1,4,32]{2,1,0:T(4,128)(2,1)} %maps_ref.1) | copy-start | bytes 772
  48.3 10.6 %copy-start.2 = (bf16[768,128]{1,0:T(8,128)(2,1)}, bf16[768,128]{1,0:T(8,128)(2,1)S(1)}, u32[]{:S(2)}) copy-start(bf16[768,128]{1,0:T(8,128)(2,1)S(1)} %collective-permute-done.5.refs_1_) | copy-start | bytes 589828
  50.4 8.5 %copy-start.3 = (bf16[768,128]{1,0:T(8,128)(2,1)}, bf16[768,128]{1,0:T(8,128)(2,1)S(1)}, u32[]{:S(2)}) copy-start(bf16[768,128]{1,0:T(8,128)(2,1)S(1)} %collective-permute-done.6.refs_2_) | copy-start | bytes 589828
  50.4 8.5 %copy-start.4 = (bf16[768,128]{1,0:T(8,128)(2,1)}, bf16[768,128]{1,0:T(8,128)(2,1)S(1)}, u32[]{:S(2)}) copy-start(bf16[768,128]{1,0:T(8,128)(2,1)S(1)} %collective-permute-done.7.refs_3_) | copy-start | bytes 589828
  50.4 33.7 %all-to-all-start.1 = ((bf16[16,256,256]{2,1,0:T(8,128)(2,1)}), bf16[16,256,256]{2,1,0:T(8,128)(2,1)}, u32[]{:S(2)}, u32[]{:S(2)}) async-start(bf16[16,256,256]{2,1,0:T(8,128)(2,1)} %copy-done), calls=%async_computation.1 | async-start | bytes 4194304 | tf_op jit(solution)/shard_map/all_to_all | solution.py:692
  56.4 2.5 %copy-start.12 = (s32[16,16]{1,0:T(8,128)S(1)}, s32[16,16]{1,0:T(8,128)}, u32[]{:S(2)}) copy-start(s32[16,16]{1,0:T(8,128)} %param.24) | copy-start | bytes 3076
  56.4 2.6 %copy-start.14 = (bf16[1024]{0:T(1024)(128)(2,1)S(1)}, bf16[1024]{0:T(1024)(128)(2,1)}, u32[]{:S(2)}) copy-start(bf16[1024]{0:T(1024)(128)(2,1)} %param.29) | copy-start | bytes 6148
  56.4 10.3 %copy-start.13 = (s32[16]{0:T(128)S(1)}, s32[16]{0:T(128)}, u32[]{:S(2)}) copy-start(s32[16]{0:T(128)} %len_ref.3) | copy-start | bytes 196
  58.8 2.0 %collective-permute-start.8 = (f32[4,24,1024]{2,1,0:T(8,128)}, f32[4,24,1024]{2,1,0:T(8,128)S(1)}, u32[]{:S(2)}, u32[]{:S(2)}) collective-permute-start(f32[4,24,1024]{2,1,0:T(8,128)} %get-tuple-element.46), channel_id=1, source_target_pairs={{0,1},{1,0},{2,3},{3,2},{4,5},{5,4},{6,7},{7,6},{8,9},{9,8},{10,11... | collective-permute-start | bytes 1179656 | tf_op jit(solution)/shard_map/ppermute | solution.py:694
  61.5 19.5 %collective-permute-start.9 = (f32[24,1024]{1,0:T(8,128)S(1)}, f32[24,1024]{1,0:T(8,128)S(1)}, u32[]{:S(2)}, u32[]{:S(2)}) collective-permute-start(f32[24,1024]{1,0:T(8,128)S(1)} %get-tuple-element.48), channel_id=1, source_target_pairs={{0,2},{1,3},{2,4},{3,5},{4,6},{5,7},{6,0},{7,1},{8,10},{9,11},{10,... | collective-permute-start | bytes 294920 | tf_op jit(solution)/shard_map/ppermute | solution.py:664
  62.4 18.5 %collective-permute-start.10 = (f32[24,1024]{1,0:T(8,128)S(1)}, f32[24,1024]{1,0:T(8,128)S(1)}, u32[]{:S(2)}, u32[]{:S(2)}) collective-permute-start(f32[24,1024]{1,0:T(8,128)S(1)} %get-tuple-element.49), channel_id=1, source_target_pairs={{0,4},{1,5},{2,6},{3,7},{4,0},{5,1},{6,2},{7,3},{8,12},{9,13},{10,... | collective-permute-start | bytes 294920 | tf_op jit(solution)/shard_map/ppermute | solution.py:664
  65.1 15.8 %collective-permute-start.11 = (f32[24,1024]{1,0:T(8,128)S(1)}, f32[24,1024]{1,0:T(8,128)S(1)}, u32[]{:S(2)}, u32[]{:S(2)}) collective-permute-start(f32[24,1024]{1,0:T(8,128)S(1)} %get-tuple-element.50), channel_id=1, source_target_pairs={{0,6},{1,7},{2,0},{3,1},{4,2},{5,3},{6,4},{7,5},{8,14},{9,15},{10,... | collective-permute-start | bytes 294920 | tf_op jit(solution)/shard_map/ppermute | solution.py:664
  66.8 17.3 %copy-start.7 = (bf16[1,4,1024]{2,1,0:T(4,128)(2,1)S(1)}, bf16[1,4,1024]{2,1,0:T(4,128)(2,1)}, u32[]{:S(2)}) copy-start(bf16[1,4,1024]{2,1,0:T(4,128)(2,1)} %q_ref.1) | copy-start | bytes 24580
  66.8 17.3 %copy-start.9 = (bf16[1,4,256]{2,1,0:T(4,128)(2,1)S(1)}, bf16[1,4,256]{2,1,0:T(4,128)(2,1)}, u32[]{:S(2)}) copy-start(bf16[1,4,256]{2,1,0:T(4,128)(2,1)} %fresh_ref.1) | copy-start | bytes 6148

commit v5 on v3

--- a/solution.py
+++ b/solution.py
@@ -127,14 +127,14 @@
     return pltpu.make_async_copy(*(ends[::-1] if out else ends), sem.at[p * STEPS + j])
 
 
-def local_kernel(len_ref, x_hbm, dt_hbm, bc_hbm, rate_hbm, kv, dx_hbm, dz_hbm, ddt_hbm, *refs):
-    outs, split, (stage, ft, bt, x_buf, dt_ref, bc_ref, rate_ref, sem), rest = (
+def local_kernel(len_hbm, x_hbm, dt_hbm, bc_hbm, rate_hbm, kv, dx_hbm, dz_hbm, ddt_hbm, *refs):
+    outs, split, (len_ref, stage, ft, bt, x_buf, dt_ref, bc_ref, rate_ref, sem), rest = (
         refs[:ROW],
         refs[ROW],
-        refs[ROW + 1 : ROW + 9],
-        refs[ROW + 9 :],
+        refs[ROW + 1 : ROW + 10],
+        refs[ROW + 10 :],
     )
-    small = fetch([(dt_hbm, dt_ref), (bc_hbm, bc_ref), (rate_hbm, rate_ref)], sem, 2 * STEPS)
+    small = fetch([(dt_hbm, dt_ref), (bc_hbm, bc_ref), (rate_hbm, rate_ref), (len_hbm, len_ref)], sem, 2 * STEPS)
     x_copies = block_copies(x_hbm, x_buf, sem)
     for c in x_copies[:STEPS]:
         c.start()
@@ -188,9 +188,10 @@
         local_kernel,
         out_shape=[jax.ShapeDtypeStruct((STATE_ROWS + NS, LANE), BF16)] * ROW
         + [jax.ShapeDtypeStruct((TP, PAGE_ROWS, 2 * HD), BF16)],
-        in_specs=[SM] + [ANY] * 8,
+        in_specs=[ANY] * 9,
         out_specs=[ANY] * (ROW + 1),
         scratch_shapes=[
+            pltpu.SMEM((SEQ,), jnp.int32),
             pltpu.VMEM((ROW, STATE_ROWS + NS, LANE), BF16),
             pltpu.VMEM((2, HEADS, BLK), F32),
             pltpu.VMEM((2, NS, BLK), F32),

time: 88.3 us -> 87.7 us (level)
  no operation moved by 1% of the time
where the time goes in v5:
time: 87.7 us; the launch traced here: 87.4 us
  starting transfers between devices  32.2 us (37%)
  Pallas kernels  31.1 us (35%)
  waiting for transfers between devices  19.8 us (23%)
  local copies, waits for them, and re-layouts  2.71 us (3%)
  between operations  0.89 us (1%)
    pallas_call x1, Pallas kernels, block_outputs(): pl.pallas_call(output_kernel, out_shape=jax.ShapeDtypeStruct((2, BLK, WID...  14 us
    ppermute x6, starting transfers between devices, along_y(): lax.ppermute(arrays[o], 'seq', moves[o])  11 us
    ppermute x6, waiting for transfers between devices, along_y(): lax.ppermute(arrays[o], 'seq', moves[o])  9.33 us
    pallas_call x1, Pallas kernels, local_states(): pl.pallas_call(local_kernel, out_shape=[jax.ShapeDtypeStruct((STATE_ROWS...  7.07 us
    all_to_all x1, starting transfers between devices, shards(): lax.all_to_all(ordered, 'seq', split_axis=0, concat_axis=0, tiled=True)  6.04 us
    all_to_all x1, starting transfers between devices, shards(): pages = lax.all_to_all(sent, 'tp', split_axis=0, concat_axis=0, tiled=True)  5.54 us
    ppermute x3, starting transfers between devices, along_z(): lax.ppermute(arrays[o], 'tp', moves[o])  5.19 us
    pallas_call x1, Pallas kernels, attend(): pl.pallas_call(attend_kernel, out_shape=[jax.ShapeDtypeStruct((1, SEQ * B...  3.92 us
  transfers between devices with their start and end apart: 14, of which 8 were waited for; matrix products, arithmetic and copies ran while one was open for 2% of the time, Pallas kernels for 23%

profile of v5, /device:TPU:0, one launch (start us, length us, event | category | flops | bytes accessed | tf_op | source)
XLA Modules:
  0.0 87.4 jit_solution(414027023501343140)
XLA Ops:
  0.6 7.1 %local_states.1 = (bf16[528,128]{1,0:T(8,128)(2,1)}, bf16[528,128]{1,0:T(8,128)(2,1)}, bf16[528,128]{1,0:T(8,128)(2,1)}, bf16[528,128]{1,0:T(8,128)(2,1)}, bf16[8,560,256]{2,1,0:T(8,128)(2,1)}) custom-call(s32[16]{0:T(128)} %len_ref.1, bf16[2,256,8192]{2,1,0:T(8,128)(2,1)} %x_hbm.3, bf16[2,256,128]{2,1,0:T(8,128)(2,1)} %dt_hbm.3, ...), custom_call_target="tpu_custom_call" | custom-call | bytes 18000000 | tf_op jit(solution)/shard_map/local_states/pallas_call | solution.py:187
  7.7 0.0 copy-start.5
  7.8 0.0 copy-start.7
  7.8 5.5 %all-to-all-start = ((bf16[8,560,256]{2,1,0:T(8,128)(2,1)}), bf16[8,560,256]{2,1,0:T(8,128)(2,1)S(1)}, u32[]{:S(2)}, u32[]{:S(2)}) async-start(bf16[8,560,256]{2,1,0:T(8,128)(2,1)} %get-tuple-element.30), calls=%async_computation | async-start | bytes 4587520 | tf_op jit(solution)/shard_map/all_to_all | solution.py:684
  13.3 1.6 %collective-permute-start = (bf16[528,128]{1,0:T(8,128)(2,1)S(1)}, bf16[528,128]{1,0:T(8,128)(2,1)S(1)}, u32[]{:S(2)}, u32[]{:S(2)}) collective-permute-start(bf16[528,128]{1,0:T(8,128)(2,1)S(1)} %copy-done.19), channel_id=1, source_target_pairs={{0,8},{8,16},{16,24},{24,0},{32,40},{40,48},{48,56},{56,32},{64,72... | collective-permute-start | bytes 405512 | tf_op jit(solution)/shard_map/ppermute | solution.py:670
  15.0 2.9 %collective-permute-start.1 = (bf16[528,128]{1,0:T(8,128)(2,1)S(1)}, bf16[528,128]{1,0:T(8,128)(2,1)S(1)}, u32[]{:S(2)}, u32[]{:S(2)}) collective-permute-start(bf16[528,128]{1,0:T(8,128)(2,1)S(1)} %copy-done.18), channel_id=1, source_target_pairs={{0,16},{8,24},{16,0},{24,8},{32,48},{40,56},{48,32},{56,40},{64,80... | collective-permute-start | bytes 405512 | tf_op jit(solution)/shard_map/ppermute | solution.py:670
  17.9 1.3 %collective-permute-start.2 = (bf16[528,128]{1,0:T(8,128)(2,1)S(1)}, bf16[528,128]{1,0:T(8,128)(2,1)S(1)}, u32[]{:S(2)}, u32[]{:S(2)}) collective-permute-start(bf16[528,128]{1,0:T(8,128)(2,1)S(1)} %copy-done.17), channel_id=1, source_target_pairs={{0,24},{8,0},{16,8},{24,16},{32,56},{40,32},{48,40},{56,48},{64,88... | collective-permute-start | bytes 405512 | tf_op jit(solution)/shard_map/ppermute | solution.py:670
  19.2 1.4 %collective-permute-done.refs_1_ = bf16[528,128]{1,0:T(8,128)(2,1)S(1)} collective-permute-done((bf16[528,128]{1,0:T(8,128)(2,1)S(1)}, bf16[528,128]{1,0:T(8,128)(2,1)S(1)}, u32[]{:S(2)}, u32[]{:S(2)}) %collective-permute-start) | collective-permute-done | bytes 135200 | tf_op jit(solution)/shard_map/ppermute | solution.py:670
  20.6 4.1 %collective-permute-done.1.refs_2_ = bf16[528,128]{1,0:T(8,128)(2,1)S(1)} collective-permute-done((bf16[528,128]{1,0:T(8,128)(2,1)S(1)}, bf16[528,128]{1,0:T(8,128)(2,1)S(1)}, u32[]{:S(2)}, u32[]{:S(2)}) %collective-permute-start.1) | collective-permute-done | bytes 135200 | tf_op jit(solution)/shard_map/ppermute | solution.py:670
  24.7 0.0 collective-permute-done.2.refs_3_
  24.7 0.3 row_totals.1.own
  25.0 1.6 %collective-permute-start.3 = (bf16[528,128]{1,0:T(8,128)(2,1)S(1)}, bf16[528,128]{1,0:T(8,128)(2,1)S(1)}, u32[]{:S(2)}, u32[]{:S(2)}) collective-permute-start(bf16[528,128]{1,0:T(8,128)(2,1)S(1)} %row_totals.1.own), channel_id=1, source_target_pairs={{0,32},{8,40},{16,48},{24,56},{32,0},{40,8},{48,16},{56,24},{64,96... | collective-permute-start | bytes 405512 | tf_op jit(solution)/shard_map/ppermute | solution.py:687
  26.6 3.7 %collective-permute-done.3.near = bf16[528,128]{1,0:T(8,128)(2,1)S(1)} collective-permute-done((bf16[528,128]{1,0:T(8,128)(2,1)S(1)}, bf16[528,128]{1,0:T(8,128)(2,1)S(1)}, u32[]{:S(2)}, u32[]{:S(2)}) %collective-permute-start.3) | collective-permute-done | bytes 135200 | tf_op jit(solution)/shard_map/ppermute | solution.py:687
  30.3 0.3 pair_totals.1
  30.5 2.8 %collective-permute-start.4 = (bf16[528,128]{1,0:T(8,128)(2,1)S(1)}, bf16[528,128]{1,0:T(8,128)(2,1)S(1)}, u32[]{:S(2)}, u32[]{:S(2)}) collective-permute-start(bf16[528,128]{1,0:T(8,128)(2,1)S(1)} %pair_totals.1), channel_id=1, source_target_pairs={{0,96},{8,104},{16,112},{24,120},{32,64},{40,72},{48,80},{56,88},{... | collective-permute-start | bytes 405512 | tf_op jit(solution)/shard_map/ppermute | solution.py:689
  33.4 3.5 %collective-permute-done.4.far = bf16[528,128]{1,0:T(8,128)(2,1)S(1)} collective-permute-done((bf16[528,128]{1,0:T(8,128)(2,1)S(1)}, bf16[528,128]{1,0:T(8,128)(2,1)S(1)}, u32[]{:S(2)}, u32[]{:S(2)}) %collective-permute-start.4) | collective-permute-done | bytes 135200 | tf_op jit(solution)/shard_map/ppermute | solution.py:689
  36.8 1.9 %enter_states.1 = (bf16[768,128]{1,0:T(8,128)(2,1)S(1)}, bf16[768,128]{1,0:T(8,128)(2,1)}, bf16[768,128]{1,0:T(8,128)(2,1)S(1)}, bf16[768,128]{1,0:T(8,128)(2,1)S(1)}) custom-call(s32[16]{0:T(128)S(1)} %copy-done.7, bf16[528,128]{1,0:T(8,128)(2,1)S(1)} %row_totals.1.own, bf16[528,128]{1,0:T(8,128)(2,1)S(1)} %collective-permute-done.3.near, ...), custom_call_target="tpu_custom_call" | custom-call | bytes 6000000 | tf_op jit(solution)/shard_map/enter_states/pallas_call | solution.py:340
  38.7 1.1 %collective-permute-start.5 = (bf16[768,128]{1,0:T(8,128)(2,1)}, bf16[768,128]{1,0:T(8,128)(2,1)S(1)}, u32[]{:S(2)}, u32[]{:S(2)}) collective-permute-start(bf16[768,128]{1,0:T(8,128)(2,1)} %get-tuple-element.37), channel_id=1, source_target_pairs={{0,8},{8,16},{16,24},{24,0},{32,40},{40,48},{48,56},{56,32},{64,72... | collective-permute-start | bytes 589832 | tf_op jit(solution)/shard_map/ppermute | solution.py:670
  39.8 2.7 %collective-permute-start.6 = (bf16[768,128]{1,0:T(8,128)(2,1)S(1)}, bf16[768,128]{1,0:T(8,128)(2,1)S(1)}, u32[]{:S(2)}, u32[]{:S(2)}) collective-permute-start(bf16[768,128]{1,0:T(8,128)(2,1)S(1)} %get-tuple-element.38), channel_id=1, source_target_pairs={{0,16},{8,24},{16,0},{24,8},{32,48},{40,56},{48,32},{56,40},{64,80... | collective-permute-start | bytes 589832 | tf_op jit(solution)/shard_map/ppermute | solution.py:670
  42.5 1.3 %collective-permute-start.7 = (bf16[768,128]{1,0:T(8,128)(2,1)S(1)}, bf16[768,128]{1,0:T(8,128)(2,1)S(1)}, u32[]{:S(2)}, u32[]{:S(2)}) collective-permute-start(bf16[768,128]{1,0:T(8,128)(2,1)S(1)} %get-tuple-element.39), channel_id=1, source_target_pairs={{0,24},{8,0},{16,8},{24,16},{32,56},{40,32},{48,40},{56,48},{64,88... | collective-permute-start | bytes 589832 | tf_op jit(solution)/shard_map/ppermute | solution.py:670
  43.8 0.0 all-to-all-done.pages.inputs
  43.8 0.7 order_pages.1
  44.5 0.0 copy-start
  44.5 1.3 %copy-done = bf16[16,256,256]{2,1,0:T(8,128)(2,1)} copy-done((bf16[16,256,256]{2,1,0:T(8,128)(2,1)}, bf16[16,256,256]{2,1,0:T(8,128)(2,1)S(1)}, u32[]{:S(2)}) %copy-start) | copy-done | bytes 2097176
  45.8 1.8 %collective-permute-done.5.refs_1_ = bf16[768,128]{1,0:T(8,128)(2,1)S(1)} collective-permute-done((bf16[768,128]{1,0:T(8,128)(2,1)}, bf16[768,128]{1,0:T(8,128)(2,1)S(1)}, u32[]{:S(2)}, u32[]{:S(2)}) %collective-permute-start.5) | collective-permute-done | bytes 196640 | tf_op jit(solution)/shard_map/ppermute | solution.py:670
  47.6 2.1 %collective-permute-done.6.refs_2_ = bf16[768,128]{1,0:T(8,128)(2,1)S(1)} collective-permute-done((bf16[768,128]{1,0:T(8,128)(2,1)S(1)}, bf16[768,128]{1,0:T(8,128)(2,1)S(1)}, u32[]{:S(2)}, u32[]{:S(2)}) %collective-permute-start.6) | collective-permute-done | bytes 196640 | tf_op jit(solution)/shard_map/ppermute | solution.py:670
  49.7 0.0 collective-permute-done.7.refs_3_
  49.7 6.0 %all-to-all-start.1 = ((bf16[16,256,256]{2,1,0:T(8,128)(2,1)}), bf16[16,256,256]{2,1,0:T(8,128)(2,1)}, u32[]{:S(2)}, u32[]{:S(2)}) async-start(bf16[16,256,256]{2,1,0:T(8,128)(2,1)} %copy-done), calls=%async_computation.1 | async-start | bytes 4194304 | tf_op jit(solution)/shard_map/all_to_all | solution.py:693
  55.8 0.0 copy-start.14
  55.8 0.0 copy-start.16
  55.8 0.0 copy-start.15
  55.8 2.3 %decode.1 = (f32[4,24,1024]{2,1,0:T(8,128)S(1)}, f32[4,24,1024]{2,1,0:T(8,128)}) custom-call(bf16[8,560,256]{2,1,0:T(8,128)(2,1)S(1)} %all-to-all-done.pages.inputs, bf16[1,4,32]{2,1,0:T(4,128)(2,1)S(1)} %copy-done.10, f32[1,128]{1,0:T(1,128)S(1)} %bitcast.5, f32[1,128]{1,0:T(1,128)S(1)} %bitcast.7, bf16[768,128]{1,0:T(8,128)(2,1)S(1)} %get-tuple-element.40.refs_0_, ...), custom_call_target="tpu_custom_call" | custom-call | bytes 12000000 | tf_op jit(solution)/shard_map/decode/pallas_call | solution.py:627
  58.2 0.1 collective-permute-start.8
  58.3 0.1 reshape.24
  58.4 0.6 reshape.25.gain_ref
  59.0 1.2 %collective-permute-done.8.other = f32[4,24,1024]{2,1,0:T(8,128)S(1)} collective-permute-done((f32[4,24,1024]{2,1,0:T(8,128)}, f32[4,24,1024]{2,1,0:T(8,128)S(1)}, u32[]{:S(2)}, u32[]{:S(2)}) %collective-permute-start.8) | collective-permute-done | bytes 393248 | tf_op jit(solution)/shard_map/ppermute | solution.py:695
  60.2 0.6 choose_side.1
  60.8 0.6 copy-done.6
  61.5 0.9 %collective-permute-start.9 = (f32[24,1024]{1,0:T(8,128)S(1)}, f32[24,1024]{1,0:T(8,128)S(1)}, u32[]{:S(2)}, u32[]{:S(2)}) collective-permute-start(f32[24,1024]{1,0:T(8,128)S(1)} %get-tuple-element.48), channel_id=1, source_target_pairs={{0,2},{1,3},{2,4},{3,5},{4,6},{5,7},{6,0},{7,1},{8,10},{9,11},{10,... | collective-permute-start | bytes 294920 | tf_op jit(solution)/shard_map/ppermute | solution.py:665
  62.4 2.7 %collective-permute-start.10 = (f32[24,1024]{1,0:T(8,128)S(1)}, f32[24,1024]{1,0:T(8,128)S(1)}, u32[]{:S(2)}, u32[]{:S(2)}) collective-permute-start(f32[24,1024]{1,0:T(8,128)S(1)} %get-tuple-element.49), channel_id=1, source_target_pairs={{0,4},{1,5},{2,6},{3,7},{4,0},{5,1},{6,2},{7,3},{8,12},{9,13},{10,... | collective-permute-start | bytes 294920 | tf_op jit(solution)/shard_map/ppermute | solution.py:665
  65.1 1.6 %collective-permute-start.11 = (f32[24,1024]{1,0:T(8,128)S(1)}, f32[24,1024]{1,0:T(8,128)S(1)}, u32[]{:S(2)}, u32[]{:S(2)}) collective-permute-start(f32[24,1024]{1,0:T(8,128)S(1)} %get-tuple-element.50), channel_id=1, source_target_pairs={{0,6},{1,7},{2,0},{3,1},{4,2},{5,3},{6,4},{7,5},{8,14},{9,15},{10,... | collective-permute-start | bytes 294920 | tf_op jit(solution)/shard_map/ppermute | solution.py:665
  66.7 0.7 pad_add_fusion.table
  67.3 14.0 %block_outputs.1 = bf16[2,256,8192]{2,1,0:T(8,128)(2,1)} custom-call(s32[16]{0:T(128)} %len_ref.1, bf16[2,256,8192]{2,1,0:T(8,128)(2,1)} %x_hbm.3, bf16[2,256,128]{2,1,0:T(8,128)(2,1)} %dt_hbm.3, bf16[2,32,256]{2,1,0:T(8,128)(2,1)} %bitcast.9, f32[1,128]{1,0:T(1,128)} %bitcast.4, f32[1,128]{1,0:T(1,128)} %bitcast.6, bf16[768,128]{1,0:T(8,128)(2,1)} %copy-done.1, ...), custom_call_target="tpu_custom_call" | custom-call | bytes 36000000 | tf_op jit(solution)/shard_map/block_outputs/pallas_call | solution.py:441
  81.3 0.0 collective-permute-done.9.refs_1_
  81.3 0.0 collective-permute-done.10.refs_2_
  81.3 0.0 collective-permute-done.11.refs_3_
  81.4 2.1 %all-to-all-done.1.recv = bf16[16,256,256]{2,1,0:T(8,128)(2,1)} async-done(((bf16[16,256,256]{2,1,0:T(8,128)(2,1)}), bf16[16,256,256]{2,1,0:T(8,128)(2,1)}, u32[]{:S(2)}, u32[]{:S(2)}) %all-to-all-start.1) | async-done | bytes 2097184 | tf_op jit(solution)/shard_map/all_to_all | solution.py:693
  83.5 3.9 %attend.1 = (bf16[1,4096,256]{2,1,0:T(8,128)(2,1)}, bf16[1,4,1024]{2,1,0:T(4,128)(2,1)}, f32[1,16,1024]{2,1,0:T(8,128)}, bf16[1,4,1024]{2,1,0:T(4,128)(2,1)}) custom-call(s32[288]{0:T(512)} %pad_add_fusion.table, bf16[16,256,256]{2,1,0:T(8,128)(2,1)} %all-to-all-done.1.recv, bf16[1,4,1024]{2,1,0:T(4,128)(2,1)} %q_ref.1, bf16[1,4,256]{2,1,0:T(4,128)(2,1)} %fresh_ref.1, ...), custom_call_target="tpu_custom_call" | custom-call | bytes 15000000 | tf_op jit(solution)/shard_map/attend/pallas_call | solution.py:545
  (32 shorter events, 0.1 us)
Async XLA Ops:
  7.7 5.6 %copy-start.19 = (bf16[528,128]{1,0:T(8,128)(2,1)S(1)}, bf16[528,128]{1,0:T(8,128)(2,1)}, u32[]{:S(2)}) copy-start(bf16[528,128]{1,0:T(8,128)(2,1)} %get-tuple-element.32) | copy-start | bytes 405508
  7.7 7.2 %copy-start.18 = (bf16[528,128]{1,0:T(8,128)(2,1)S(1)}, bf16[528,128]{1,0:T(8,128)(2,1)}, u32[]{:S(2)}) copy-start(bf16[528,128]{1,0:T(8,128)(2,1)} %get-tuple-element.33) | copy-start | bytes 405508
  7.7 10.1 %copy-start.17 = (bf16[528,128]{1,0:T(8,128)(2,1)S(1)}, bf16[528,128]{1,0:T(8,128)(2,1)}, u32[]{:S(2)}) copy-start(bf16[528,128]{1,0:T(8,128)(2,1)} %get-tuple-element.34) | copy-start | bytes 405508
  7.7 16.9 %copy-start.5 = (bf16[528,128]{1,0:T(8,128)(2,1)S(1)}, bf16[528,128]{1,0:T(8,128)(2,1)}, u32[]{:S(2)}) copy-start(bf16[528,128]{1,0:T(8,128)(2,1)} %get-tuple-element.31.refs_0_) | copy-start | bytes 405508
  7.8 29.1 %copy-start.7 = (s32[16]{0:T(128)S(1)}, s32[16]{0:T(128)}, u32[]{:S(2)}) copy-start(s32[16]{0:T(128)} %group_ref.5) | copy-start | bytes 196
  7.8 36.1 %all-to-all-start = ((bf16[8,560,256]{2,1,0:T(8,128)(2,1)}), bf16[8,560,256]{2,1,0:T(8,128)(2,1)S(1)}, u32[]{:S(2)}, u32[]{:S(2)}) async-start(bf16[8,560,256]{2,1,0:T(8,128)(2,1)} %get-tuple-element.30), calls=%async_computation | async-start | bytes 4587520 | tf_op jit(solution)/shard_map/all_to_all | solution.py:684
  13.3 7.3 %collective-permute-start = (bf16[528,128]{1,0:T(8,128)(2,1)S(1)}, bf16[528,128]{1,0:T(8,128)(2,1)S(1)}, u32[]{:S(2)}, u32[]{:S(2)}) collective-permute-start(bf16[528,128]{1,0:T(8,128)(2,1)S(1)} %copy-done.19), channel_id=1, source_target_pairs={{0,8},{8,16},{16,24},{24,0},{32,40},{40,48},{48,56},{56,32},{64,72... | collective-permute-start | bytes 405512 | tf_op jit(solution)/shard_map/ppermute | solution.py:670
  15.0 9.7 %collective-permute-start.1 = (bf16[528,128]{1,0:T(8,128)(2,1)S(1)}, bf16[528,128]{1,0:T(8,128)(2,1)S(1)}, u32[]{:S(2)}, u32[]{:S(2)}) collective-permute-start(bf16[528,128]{1,0:T(8,128)(2,1)S(1)} %copy-done.18), channel_id=1, source_target_pairs={{0,16},{8,24},{16,0},{24,8},{32,48},{40,56},{48,32},{56,40},{64,80... | collective-permute-start | bytes 405512 | tf_op jit(solution)/shard_map/ppermute | solution.py:670
  17.9 6.8 %collective-permute-start.2 = (bf16[528,128]{1,0:T(8,128)(2,1)S(1)}, bf16[528,128]{1,0:T(8,128)(2,1)S(1)}, u32[]{:S(2)}, u32[]{:S(2)}) collective-permute-start(bf16[528,128]{1,0:T(8,128)(2,1)S(1)} %copy-done.17), channel_id=1, source_target_pairs={{0,24},{8,0},{16,8},{24,16},{32,56},{40,32},{48,40},{56,48},{64,88... | collective-permute-start | bytes 405512 | tf_op jit(solution)/shard_map/ppermute | solution.py:670
  25.0 5.2 %collective-permute-start.3 = (bf16[528,128]{1,0:T(8,128)(2,1)S(1)}, bf16[528,128]{1,0:T(8,128)(2,1)S(1)}, u32[]{:S(2)}, u32[]{:S(2)}) collective-permute-start(bf16[528,128]{1,0:T(8,128)(2,1)S(1)} %row_totals.1.own), channel_id=1, source_target_pairs={{0,32},{8,40},{16,48},{24,56},{32,0},{40,8},{48,16},{56,24},{64,96... | collective-permute-start | bytes 405512 | tf_op jit(solution)/shard_map/ppermute | solution.py:687
  30.5 6.3 %collective-permute-start.4 = (bf16[528,128]{1,0:T(8,128)(2,1)S(1)}, bf16[528,128]{1,0:T(8,128)(2,1)S(1)}, u32[]{:S(2)}, u32[]{:S(2)}) collective-permute-start(bf16[528,128]{1,0:T(8,128)(2,1)S(1)} %pair_totals.1), channel_id=1, source_target_pairs={{0,96},{8,104},{16,112},{24,120},{32,64},{40,72},{48,80},{56,88},{... | collective-permute-start | bytes 405512 | tf_op jit(solution)/shard_map/ppermute | solution.py:689
  38.7 17.1 %copy-start.1 = (bf16[768,128]{1,0:T(8,128)(2,1)}, bf16[768,128]{1,0:T(8,128)(2,1)S(1)}, u32[]{:S(2)}) copy-start(bf16[768,128]{1,0:T(8,128)(2,1)S(1)} %get-tuple-element.40.refs_0_) | copy-start | bytes 589828
  38.7 8.9 %collective-permute-start.5 = (bf16[768,128]{1,0:T(8,128)(2,1)}, bf16[768,128]{1,0:T(8,128)(2,1)S(1)}, u32[]{:S(2)}, u32[]{:S(2)}) collective-permute-start(bf16[768,128]{1,0:T(8,128)(2,1)} %get-tuple-element.37), channel_id=1, source_target_pairs={{0,8},{8,16},{16,24},{24,0},{32,40},{40,48},{48,56},{56,32},{64,72... | collective-permute-start | bytes 589832 | tf_op jit(solution)/shard_map/ppermute | solution.py:670
  39.8 9.9 %collective-permute-start.6 = (bf16[768,128]{1,0:T(8,128)(2,1)S(1)}, bf16[768,128]{1,0:T(8,128)(2,1)S(1)}, u32[]{:S(2)}, u32[]{:S(2)}) collective-permute-start(bf16[768,128]{1,0:T(8,128)(2,1)S(1)} %get-tuple-element.38), channel_id=1, source_target_pairs={{0,16},{8,24},{16,0},{24,8},{32,48},{40,56},{48,32},{56,40},{64,80... | collective-permute-start | bytes 589832 | tf_op jit(solution)/shard_map/ppermute | solution.py:670
  42.5 7.2 %collective-permute-start.7 = (bf16[768,128]{1,0:T(8,128)(2,1)S(1)}, bf16[768,128]{1,0:T(8,128)(2,1)S(1)}, u32[]{:S(2)}, u32[]{:S(2)}) collective-permute-start(bf16[768,128]{1,0:T(8,128)(2,1)S(1)} %get-tuple-element.39), channel_id=1, source_target_pairs={{0,24},{8,0},{16,8},{24,16},{32,56},{40,32},{48,40},{56,48},{64,88... | collective-permute-start | bytes 589832 | tf_op jit(solution)/shard_map/ppermute | solution.py:670
  44.5 1.3 %copy-start = (bf16[16,256,256]{2,1,0:T(8,128)(2,1)}, bf16[16,256,256]{2,1,0:T(8,128)(2,1)S(1)}, u32[]{:S(2)}) copy-start(bf16[16,256,256]{2,1,0:T(8,128)(2,1)S(1)} %order_pages.1) | copy-start | bytes 6291460
  45.8 10.0 %copy-start.8 = (f32[128]{0:T(128)S(1)}, f32[128]{0:T(128)}, u32[]{:S(2)}) copy-start(f32[128]{0:T(128)} %param.19) | copy-start | bytes 1540
  45.8 10.0 %copy-start.9 = (f32[128]{0:T(128)S(1)}, f32[128]{0:T(128)}, u32[]{:S(2)}) copy-start(f32[128]{0:T(128)} %param.20) | copy-start | bytes 1540
  45.8 10.0 %copy-start.10 = (bf16[1,4,32]{2,1,0:T(4,128)(2,1)S(1)}, bf16[1,4,32]{2,1,0:T(4,128)(2,1)}, u32[]{:S(2)}) copy-start(bf16[1,4,32]{2,1,0:T(4,128)(2,1)} %maps_ref.1) | copy-start | bytes 772
  47.6 10.6 %copy-start.2 = (bf16[768,128]{1,0:T(8,128)(2,1)}, bf16[768,128]{1,0:T(8,128)(2,1)S(1)}, u32[]{:S(2)}) copy-start(bf16[768,128]{1,0:T(8,128)(2,1)S(1)} %collective-permute-done.5.refs_1_) | copy-start | bytes 589828
  49.7 8.5 %copy-start.3 = (bf16[768,128]{1,0:T(8,128)(2,1)}, bf16[768,128]{1,0:T(8,128)(2,1)S(1)}, u32[]{:S(2)}) copy-start(bf16[768,128]{1,0:T(8,128)(2,1)S(1)} %collective-permute-done.6.refs_2_) | copy-start | bytes 589828
  49.7 8.5 %copy-start.4 = (bf16[768,128]{1,0:T(8,128)(2,1)}, bf16[768,128]{1,0:T(8,128)(2,1)S(1)}, u32[]{:S(2)}) copy-start(bf16[768,128]{1,0:T(8,128)(2,1)S(1)} %collective-permute-done.7.refs_3_) | copy-start | bytes 589828
  49.7 33.7 %all-to-all-start.1 = ((bf16[16,256,256]{2,1,0:T(8,128)(2,1)}), bf16[16,256,256]{2,1,0:T(8,128)(2,1)}, u32[]{:S(2)}, u32[]{:S(2)}) async-start(bf16[16,256,256]{2,1,0:T(8,128)(2,1)} %copy-done), calls=%async_computation.1 | async-start | bytes 4194304 | tf_op jit(solution)/shard_map/all_to_all | solution.py:693
  55.8 2.5 %copy-start.14 = (s32[16,16]{1,0:T(8,128)S(1)}, s32[16,16]{1,0:T(8,128)}, u32[]{:S(2)}) copy-start(s32[16,16]{1,0:T(8,128)} %param.24) | copy-start | bytes 3076
  55.8 2.6 %copy-start.16 = (bf16[1024]{0:T(1024)(128)(2,1)S(1)}, bf16[1024]{0:T(1024)(128)(2,1)}, u32[]{:S(2)}) copy-start(bf16[1024]{0:T(1024)(128)(2,1)} %param.29) | copy-start | bytes 6148
  55.8 10.9 %copy-start.15 = (s32[16]{0:T(128)S(1)}, s32[16]{0:T(128)}, u32[]{:S(2)}) copy-start(s32[16]{0:T(128)} %len_ref.1) | copy-start | bytes 196
  58.2 2.0 %collective-permute-start.8 = (f32[4,24,1024]{2,1,0:T(8,128)}, f32[4,24,1024]{2,1,0:T(8,128)S(1)}, u32[]{:S(2)}, u32[]{:S(2)}) collective-permute-start(f32[4,24,1024]{2,1,0:T(8,128)} %get-tuple-element.46), channel_id=1, source_target_pairs={{0,1},{1,0},{2,3},{3,2},{4,5},{5,4},{6,7},{7,6},{8,9},{9,8},{10,11... | collective-permute-start | bytes 1179656 | tf_op jit(solution)/shard_map/ppermute | solution.py:695
  60.8 0.6 copy-start.6
  61.5 19.8 %collective-permute-start.9 = (f32[24,1024]{1,0:T(8,128)S(1)}, f32[24,1024]{1,0:T(8,128)S(1)}, u32[]{:S(2)}, u32[]{:S(2)}) collective-permute-start(f32[24,1024]{1,0:T(8,128)S(1)} %get-tuple-element.48), channel_id=1, source_target_pairs={{0,2},{1,3},{2,4},{3,5},{4,6},{5,7},{6,0},{7,1},{8,10},{9,11},{10,... | collective-permute-start | bytes 294920 | tf_op jit(solution)/shard_map/ppermute | solution.py:665
  62.4 19.0 %collective-permute-start.10 = (f32[24,1024]{1,0:T(8,128)S(1)}, f32[24,1024]{1,0:T(8,128)S(1)}, u32[]{:S(2)}, u32[]{:S(2)}) collective-permute-start(f32[24,1024]{1,0:T(8,128)S(1)} %get-tuple-element.49), channel_id=1, source_target_pairs={{0,4},{1,5},{2,6},{3,7},{4,0},{5,1},{6,2},{7,3},{8,12},{9,13},{10,... | collective-permute-start | bytes 294920 | tf_op jit(solution)/shard_map/ppermute | solution.py:665
  65.1 16.3 %collective-permute-start.11 = (f32[24,1024]{1,0:T(8,128)S(1)}, f32[24,1024]{1,0:T(8,128)S(1)}, u32[]{:S(2)}, u32[]{:S(2)}) collective-permute-start(f32[24,1024]{1,0:T(8,128)S(1)} %get-tuple-element.50), channel_id=1, source_target_pairs={{0,6},{1,7},{2,0},{3,1},{4,2},{5,3},{6,4},{7,5},{8,14},{9,15},{10,... | collective-permute-start | bytes 294920 | tf_op jit(solution)/shard_map/ppermute | solution.py:665
  81.3 2.1 %copy-start.11 = (f32[24,1024]{1,0:T(8,128)}, f32[24,1024]{1,0:T(8,128)S(1)}, u32[]{:S(2)}) copy-start(f32[24,1024]{1,0:T(8,128)S(1)} %collective-permute-done.9.refs_1_) | copy-start | bytes 294916
  81.3 2.1 %copy-start.12 = (f32[24,1024]{1,0:T(8,128)}, f32[24,1024]{1,0:T(8,128)S(1)}, u32[]{:S(2)}) copy-start(f32[24,1024]{1,0:T(8,128)S(1)} %collective-permute-done.10.refs_2_) | copy-start | bytes 294916
  81.4 2.1 %copy-start.13 = (f32[24,1024]{1,0:T(8,128)}, f32[24,1024]{1,0:T(8,128)S(1)}, u32[]{:S(2)}) copy-start(f32[24,1024]{1,0:T(8,128)S(1)} %collective-permute-done.11.refs_3_) | copy-start | bytes 294916
